TPU v7x, 128 devices: a whole 4x4x4 slice. The times are simulated.
128 devices in a mesh: segment: 4 (over x), dp: 16 (over z, y), mp: 2 (over core).
Axes of the slice: x: 4, y: 4, z: 4, core: 2. Of those that a mesh axis runs over, the one named last changes fastest.
Arguments:
- teacher_hidden: bfloat16 [4096, 8192], P('dp', 'mp'), may hold values from -6 to 6
- teacher_id: int32 [4096], P('dp'), may hold values from 0 to 2
- destination: int32 [4096], P('dp'), may hold values from 0 to 15, as said below
- row_counts: int32 [16, 16], P('dp'), may hold values from 0 to 32, as said below
- section_gain: bfloat16 [4, 8192], P('segment', 'mp'), may hold values from 0.25 to 1.75
- adapter_down: bfloat16 [4, 8192, 192], P('segment', 'mp'), may hold values from -0.0625 to 0.0625
- adapter_up: bfloat16 [4, 192, 8192], P('segment', None, 'mp'), may hold values from -0.75 to 0.75
- student_in: bfloat16 [8192, 5120], P('dp', 'mp'), may hold values from -6 to 6
- student_gain: float32 [5120], P('mp'), may hold values from 0.25 to 1.75
- student_weight: bfloat16 [5120, 5120], P('mp', 'segment'), may hold values from -0.078125 to 0.078125
- projector: bfloat16 [8192, 5120], P('mp', 'segment'), may hold values from -0.0625 to 0.0625
Outputs:
- weight_grad: float32 [2, 2560, 5120], P('mp', 'dp', 'segment')
- row_loss: float32 [8192], P('dp')
Inputs may be any that keep to these rules, and one draw needn't show every extreme that they name: Of the 256 rows of one shard at most 32 have one destination; in every draw one destination gets exactly 32 rows from every shard. row_counts[d, i] is the number of rows of shard i whose destination is d.
All inputs are finite; a program needn't handle non-finite values.
Results may differ from a plain program's by a relative error of at most 0.033.
Values may be sent and summed in bfloat16 or wider, within the bound.
A program may use at most 128 MiB of HBM per device.

v0:
```python
import jax
import jax.numpy as jnp
from jax import lax
from jax.sharding import PartitionSpec as P

D = 8192
S = 5120
RANK = 64
MICRO = 4
TOK_DEV = 256


def shifted(shard, axis, by):
    length = lax.axis_size(axis)
    pairs = [(i, i + by) for i in range(length) if 0 <= i + by < length]
    return lax.ppermute(shard, axis, pairs)


def spread(value, axis, source):
    kept = jnp.where(lax.axis_index(axis) == source, value, 0).astype(value.dtype)
    return lax.psum(kept, axis)


def section(rows, ids, gain, down, up):
    wide = rows.astype(jnp.float32)
    square_part = jnp.sum(wide * wide, axis=1)
    scaled = (wide * gain.astype(jnp.float32)[None, :]).astype(jnp.bfloat16)
    latent_part = jnp.dot(scaled, down, preferred_element_type=jnp.float32)
    square_sum, latent = (
        lax.psum(square_part.astype(jnp.bfloat16), "mp").astype(jnp.float32),
        lax.psum(latent_part.astype(jnp.bfloat16), "mp").astype(jnp.float32),
    )
    latent = latent * lax.rsqrt(square_sum / D + 1e-06)[:, None]
    column_teacher = jnp.arange(down.shape[1], dtype=jnp.int32) // RANK
    chosen = jnp.where(column_teacher[None, :] == ids[:, None], latent, 0.0).astype(jnp.bfloat16)
    return (wide + jnp.dot(chosen, up, preferred_element_type=jnp.float32)).astype(jnp.bfloat16)


def local(
    teacher_hidden,
    teacher_id,
    destination,
    row_counts,
    section_gain,
    adapter_down,
    adapter_up,
    student_in,
    student_gain,
    student_weight,
    projector,
):
    segment_count = lax.axis_size("segment")
    segment_here = lax.axis_index("segment")
    tok_rows = teacher_hidden.shape[0]
    half_width = teacher_hidden.shape[1]
    micro_rows = tok_rows // MICRO
    carried = jnp.zeros((micro_rows, half_width), jnp.bfloat16)
    final = jnp.zeros((tok_rows, half_width), jnp.bfloat16)
    total_steps = MICRO + segment_count - 1
    for step in range(total_steps):
        first = min(step, MICRO - 1)
        fresh = teacher_hidden[first * micro_rows : (first + 1) * micro_rows]
        current = jnp.where(segment_here == 0, fresh, carried)
        micro_index = jnp.clip(step - segment_here, 0, MICRO - 1)
        ids = lax.dynamic_slice_in_dim(teacher_id, micro_index * micro_rows, micro_rows)
        finished = section(current, ids, section_gain[0], adapter_down[0], adapter_up[0])
        last_micro = step - (segment_count - 1)
        if 0 <= last_micro < MICRO:
            lower = last_micro * micro_rows
            kept = final[lower : lower + micro_rows]
            final = final.at[lower : lower + micro_rows].set(
                jnp.where(segment_here == segment_count - 1, finished, kept)
            )
        if step + 1 < total_steps:
            carried = shifted(finished, "segment", 1)
    final = spread(final, "segment", segment_count - 1)
    shard_count = lax.axis_size("dp")
    slot_total = student_in.shape[0]
    capacity = slot_total // shard_count
    onehot = (destination[:, None] == jnp.arange(shard_count, dtype=jnp.int32)[None, :]).astype(
        jnp.int32
    )
    earlier = jnp.cumsum(onehot, axis=0) - onehot
    slot = jnp.sum(earlier * onehot, axis=1)
    position = destination * capacity + slot
    out_cols = projector.shape[1]
    outgoing = jnp.zeros((slot_total, half_width), jnp.bfloat16).at[position].set(final)
    outgoing = outgoing.reshape(shard_count, capacity, half_width)
    target_part = jnp.einsum(
        "sck,kn->scn",
        lax.all_to_all(outgoing, "dp", split_axis=0, concat_axis=0, tiled=True),
        projector,
        preferred_element_type=jnp.float32,
    )
    target_part = target_part.reshape(slot_total, out_cols)
    wide_in = student_in.astype(jnp.float32)
    square_part = jnp.sum(wide_in * wide_in, axis=1)
    sgated = (wide_in * student_gain[None, :]).astype(jnp.bfloat16)
    output_part = jnp.dot(sgated, student_weight, preferred_element_type=jnp.float32)
    square_sum, student_out, target = (
        lax.psum(square_part.astype(jnp.bfloat16), "mp").astype(jnp.float32),
        lax.psum(output_part.astype(jnp.bfloat16), "mp").astype(jnp.float32),
        lax.psum(target_part.astype(jnp.bfloat16), "mp").astype(jnp.float32),
    )
    recip = lax.rsqrt(square_sum / S + 1e-06)
    valid = (jnp.arange(capacity, dtype=jnp.int32)[None, :] < row_counts[0][:, None]).reshape(
        slot_total
    )
    diff = jnp.where(valid[:, None], student_out * recip[:, None] - target, 0.0)
    row_loss = lax.psum(jnp.sum(diff * diff, axis=1), "segment") / S
    normed = (wide_in * student_gain[None, :] * recip[:, None]).astype(jnp.bfloat16)
    grad_rows = diff.astype(jnp.bfloat16)
    grad_share = normed.shape[1] // shard_count
    weight_grad = lax.psum_scatter(
        (
            jnp.einsum("rk,rn->kn", normed, grad_rows, preferred_element_type=jnp.float32) / TOK_DEV
        ).astype(jnp.bfloat16),
        "dp",
        scatter_dimension=0,
        tiled=True,
    ).astype(jnp.float32)
    return (weight_grad.reshape(1, grad_share, out_cols), row_loss)


def solution(mesh):
    placed = (
        P("dp", "mp"),
        P("dp"),
        P("dp"),
        P("dp", None),
        P("segment", "mp"),
        P("segment", "mp", None),
        P("segment", None, "mp"),
        P("dp", "mp"),
        P("mp"),
        P("mp", "segment"),
        P("mp", "segment"),
    )
    return jax.shard_map(
        local,
        mesh=mesh,
        in_specs=placed,
        out_specs=(P("mp", "dp", "segment"), P("dp")),
        check_vma=False,
    )
```

profile of v0, /device:TPU:1, one launch (start us, length us, event | category | flops | bytes accessed | tf_op | source)
XLA Modules:
  0.0 442.4 jit_solution(6562154493824090284)
XLA Ops:
  9.4 2.2 fusion.52
  11.6 4.7 %all-reduce.7 = (bf16[64,192]{1,0:T(8,128)(2,1)S(1)}, bf16[64]{0:T(256)(128)(2,1)S(1)}) all-reduce(bf16[64,192]{1,0:T(8,128)(2,1)S(1)} %fusion.52, bf16[64]{0:T(256)(128)(2,1)S(1)} %fusion.74), channel_id=1, replica_groups=mesh['segment'=4,'dp'=16,'mp'=2] {'mp'}, use_global_device_ids=true, to_apply=%region_6.7 | all-reduce | flops 12352 | bytes 49408 | tf_op jit(solution)/shard_map/psum | solution.py:31
  16.5 1.6 fusion.7
  18.1 3.2 collective-permute-start
  21.3 11.1 %collective-permute-done = bf16[64,4096]{1,0:T(8,128)(2,1)S(1)} collective-permute-done((bf16[64,4096]{1,0:T(8,128)(2,1)S(1)}, bf16[64,4096]{1,0:T(8,128)(2,1)S(1)}, u32[]{:S(2)}, u32[]{:S(2)}) %collective-permute-start) | collective-permute-done | bytes 524320 | tf_op jit(solution)/shard_map/ppermute | solution.py:16
  32.4 1.3 fusion.76
  35.2 4.3 all-reduce.6
  39.5 1.5 fusion.8
  41.0 4.1 collective-permute-start.1
  45.1 11.1 %collective-permute-done.1 = bf16[64,4096]{1,0:T(8,128)(2,1)S(1)} collective-permute-done((bf16[64,4096]{1,0:T(8,128)(2,1)S(1)}, bf16[64,4096]{1,0:T(8,128)(2,1)S(1)}, u32[]{:S(2)}, u32[]{:S(2)}) %collective-permute-start.1) | collective-permute-done | bytes 524320 | tf_op jit(solution)/shard_map/ppermute | solution.py:16
  56.3 1.3 fusion.78
  59.0 4.3 all-reduce.5
  63.3 2.3 fusion.9
  65.6 4.9 %collective-permute-start.2 = (bf16[64,4096]{1,0:T(8,128)(2,1)}, bf16[64,4096]{1,0:T(8,128)(2,1)}, u32[]{:S(2)}, u32[]{:S(2)}) collective-permute-start(bf16[64,4096]{1,0:T(8,128)(2,1)} %fusion.9), channel_id=1, source_target_pairs={{0,32},{32,64},{64,96},{1,33},{33,65},{65,97},{2,34},{34,66},{66,9... | collective-permute-start | bytes 1572872 | tf_op jit(solution)/shard_map/ppermute | solution.py:16
  70.5 10.7 %collective-permute-done.2 = bf16[64,4096]{1,0:T(8,128)(2,1)} collective-permute-done((bf16[64,4096]{1,0:T(8,128)(2,1)}, bf16[64,4096]{1,0:T(8,128)(2,1)}, u32[]{:S(2)}, u32[]{:S(2)}) %collective-permute-start.2) | collective-permute-done | bytes 524320 | tf_op jit(solution)/shard_map/ppermute | solution.py:16
  81.2 1.3 fusion.80
  83.9 4.3 all-reduce.4
  88.2 1.5 broadcast_select_fusion.5
  89.7 4.3 collective-permute-start.3
  94.0 1.6 scatter.20
  95.6 9.6 %collective-permute-done.3 = bf16[64,4096]{1,0:T(8,128)(2,1)S(1)} collective-permute-done((bf16[64,4096]{1,0:T(8,128)(2,1)S(1)}, bf16[64,4096]{1,0:T(8,128)(2,1)S(1)}, u32[]{:S(2)}, u32[]{:S(2)}) %collective-permute-start.3) | collective-permute-done | bytes 524320 | tf_op jit(solution)/shard_map/ppermute | solution.py:16
  105.2 1.3 fusion.82
  107.9 4.3 all-reduce.3
  112.2 2.3 select_dynamic-update-slice_fusion
  114.5 4.1 collective-permute-start.4
  118.7 11.1 %collective-permute-done.4 = bf16[64,4096]{1,0:T(8,128)(2,1)S(1)} collective-permute-done((bf16[64,4096]{1,0:T(8,128)(2,1)S(1)}, bf16[64,4096]{1,0:T(8,128)(2,1)S(1)}, u32[]{:S(2)}, u32[]{:S(2)}) %collective-permute-start.4) | collective-permute-done | bytes 524320 | tf_op jit(solution)/shard_map/ppermute | solution.py:16
  129.8 1.3 fusion.84
  132.6 4.3 all-reduce.2
  136.9 2.7 fusion.94
  139.5 4.1 collective-permute-start.5
  144.3 10.5 %collective-permute-done.5 = bf16[64,4096]{1,0:T(8,128)(2,1)S(1)} collective-permute-done((bf16[64,4096]{1,0:T(8,128)(2,1)S(1)}, bf16[64,4096]{1,0:T(8,128)(2,1)S(1)}, u32[]{:S(2)}, u32[]{:S(2)}) %collective-permute-start.5) | collective-permute-done | bytes 524320 | tf_op jit(solution)/shard_map/ppermute | solution.py:16
  154.8 1.3 fusion.86
  156.9 4.4 %all-reduce.1 = (bf16[512]{0:T(512)(128)(2,1)S(1)}, bf16[64,192]{1,0:T(8,128)(2,1)S(1)}, bf16[64]{0:T(256)(128)(2,1)S(1)}) all-reduce(bf16[512]{0:T(512)(128)(2,1)S(1)} %fusion.6, bf16[64,192]{1,0:T(8,128)(2,1)S(1)} %fusion.70, bf16[64]{0:T(256)(128)(2,1)S(1)} %get-tuple-element.67), channel_id=1, replica_groups=mesh['segment'=4,'dp'=16,'mp'=2] {'mp'}, use_global_device_ids=true, to_apply=%region_1.2 | all-reduce | flops 12864 | bytes 51456 | tf_op jit(solution)/shard_map/psum | solution.py:101
  161.4 2.5 fusion.15
  163.9 1.4 broadcast_select_fusion
  166.9 61.4 %all-reduce.12.cloned.1.call-done = bf16[256,4096]{1,0:T(8,128)(2,1)} async-done(((bf16[256,4096]{1,0:T(8,128)(2,1)}), bf16[256,4096]{1,0:T(8,128)(2,1)}) %all-reduce.12.cloned.1.call-update) | async-done | bytes 2097168 | tf_op jit(solution)/shard_map/psum | solution.py:21
  228.3 7.1 %scatter_custom_fusion = bf16[512,4096]{1,0:T(8,128)(2,1)} fusion(s32[256]{0:T(256)S(1)} %compare_select_fusion, bf16[256,4096]{1,0:T(8,128)(2,1)} %all-reduce.12.cloned.1.call-done, bf16[]{:T(256)} %constant.174.clone.1), kind=kCustom, calls=%fused_computation.35 | custom fusion | bytes 4194816 | tf_op jit(solution)/shard_map/scatter | solution.py:87
  235.4 6.9 %all-to-all-start = ((bf16[16,32,4096]{2,1,0:T(8,128)(2,1)}), bf16[16,32,4096]{2,1,0:T(8,128)(2,1)}, u32[]{:S(2)}, u32[]{:S(2)}) async-start(bf16[16,32,4096]{2,1,0:T(8,128)(2,1)} %bitcast.84), calls=%async_computation | async-start | bytes 8388608 | tf_op jit(solution)/shard_map/all_to_all | solution.py:91
  242.4 8.3 %convolution_convert_fusion = bf16[512,1280]{1,0:T(8,128)(2,1)} fusion(bf16[2560,1280]{1,0:T(8,128)(2,1)} %param.28, bf16[512,2560]{1,0:T(8,128)(2,1)} %param.26, f32[2560]{0:T(1024)S(1)} %copy-done.13), kind=kOutput, calls=%fused_computation.28 | convolution fusion | flops 3360030720 | bytes 10496000 | tf_op jit(solution)/shard_map/dot_general | solution.py:99
  250.6 54.0 %all-to-all-done = bf16[16,32,4096]{2,1,0:T(8,128)(2,1)} async-done(((bf16[16,32,4096]{2,1,0:T(8,128)(2,1)}), bf16[16,32,4096]{2,1,0:T(8,128)(2,1)}, u32[]{:S(2)}, u32[]{:S(2)}) %all-to-all-start) | async-done | bytes 4194336 | tf_op jit(solution)/shard_map/all_to_all | solution.py:91
  304.7 11.3 %fusion.16 = bf16[16,32,1280]{2,1,0:T(8,128)(2,1)} fusion(bf16[16,32,4096]{2,1,0:T(8,128)(2,1)} %all-to-all-done, bf16[4096,1280]{1,0:T(8,128)(2,1)} %param.29), kind=kOutput, calls=%fused_computation.27 | convolution fusion | flops 5369364480 | bytes 15990784 | tf_op jit(solution)/shard_map/sck,kn->scn/dot_general | solution.py:89
  316.8 26.1 %all-reduce.14.cloned.1.call-done = (bf16[512,1280]{1,0:T(8,128)(2,1)}, bf16[512,1280]{1,0:T(8,128)(2,1)}) async-done(((bf16[512,1280]{1,0:T(8,128)(2,1)}, bf16[512,1280]{1,0:T(8,128)(2,1)}), (bf16[512,1280]{1,0:T(8,128)(2,1)}, bf16[512,1280]{1,0:T(8,128)(2,1)})) %all-reduce.14.cloned.1.call-update) | async-done | bytes 2621456 | tf_op jit(solution)/shard_map/psum | solution.py:103
  342.9 9.1 %fusion = bf16[2560,1280]{1,0:T(8,128)(2,1)} fusion(bf16[512,2560]{1,0:T(8,128)(2,1)} %param.26, f32[512]{0:T(512)S(1)} %add_rsqrt_fusion, f32[2560]{0:T(1024)S(1)} %copy-done.13, bf16[512,1280]{1,0:T(8,128)(2,1)} %get-tuple-element.65, bf16[512,1280]{1,0:T(8,128)(2,1)} %get-tuple-element.66, pred[512]{0:T(512)(128)(4,1)S(1)} %lt.53), kind=kOutput, calls=%fused_computation.2 | convolution fusion | flops 3371171840 | bytes 11809280 | tf_op jit(solution)/shard_map/rk,rn->kn/dot_general | solution.py:116
  352.1 1.3 copy-done.9
  353.4 2.1 multiply_reduce_fusion
  355.4 8.5 %psum.151 = f32[512]{0:T(512)S(1)} all-reduce(f32[512]{0:T(512)S(1)} %multiply_reduce_fusion), channel_id=1, replica_groups=mesh['segment'=4,'dp'=16,'mp'=2] {'segment'}, use_global_device_ids=true, to_apply=%region_32.33 | all-reduce | flops 512 | bytes 4096 | tf_op jit(solution)/shard_map/psum | solution.py:110
  364.5 69.4 %reduce-scatter.2.cloned.1.call-done = bf16[160,1280]{1,0:T(8,128)(2,1)} async-done(((bf16[2560,1280]{1,0:T(8,128)(2,1)}), bf16[160,1280]{1,0:T(8,128)(2,1)}) %reduce-scatter.2.cloned.1.call-update) | async-done | bytes 409616 | tf_op jit(solution)/shard_map/reduce_scatter | solution.py:114
  433.9 1.9 bitcast_convert_fusion
  (62 shorter events, 13.8 us)
Async XLA Ops:
  7.2 9.3 %copy-start = (bf16[1,192,4096]{2,1,0:T(8,128)(2,1)S(1)}, bf16[1,192,4096]{2,1,0:T(8,128)(2,1)}, u32[]{:S(2)}) copy-start(bf16[1,192,4096]{2,1,0:T(8,128)(2,1)} %param.25) | copy-start | bytes 4718596
  7.2 9.2 %copy-start.10 = (s32[256]{0:T(256)S(1)}, s32[256]{0:T(256)}, u32[]{:S(2)}) copy-start(s32[256]{0:T(256)} %param.20) | copy-start | bytes 3076
  7.2 221.1 %all-reduce.12.cloned.1.call-start = ((), (), s32[]{:S(2)}) async-start(), calls=%async_computation.2 | async-start | bytes 4194304 | tf_op jit(solution)/shard_map/psum | solution.py:21
  16.4 18.1 %copy-start.1 = (bf16[1,4096,192]{1,2,0:T(8,128)(2,1)S(1)}, bf16[1,4096,192]{1,2,0:T(8,128)(2,1)}, u32[]{:S(2)}) copy-start(bf16[1,4096,192]{1,2,0:T(8,128)(2,1)} %param.24) | copy-start | bytes 4718596
  18.1 14.4 %collective-permute-start = (bf16[64,4096]{1,0:T(8,128)(2,1)S(1)}, bf16[64,4096]{1,0:T(8,128)(2,1)S(1)}, u32[]{:S(2)}, u32[]{:S(2)}) collective-permute-start(bf16[64,4096]{1,0:T(8,128)(2,1)S(1)} %fusion.7), channel_id=1, source_target_pairs={{0,32},{32,64},{64,96},{1,33},{33,65},{65,97},{2,34},{34,66},{66,9... | collective-permute-start | bytes 1572872 | tf_op jit(solution)/shard_map/ppermute | solution.py:16
  33.8 0.8 copy-start.6
  41.0 15.3 %collective-permute-start.1 = (bf16[64,4096]{1,0:T(8,128)(2,1)S(1)}, bf16[64,4096]{1,0:T(8,128)(2,1)S(1)}, u32[]{:S(2)}, u32[]{:S(2)}) collective-permute-start(bf16[64,4096]{1,0:T(8,128)(2,1)S(1)} %fusion.8), channel_id=1, source_target_pairs={{0,32},{32,64},{64,96},{1,33},{33,65},{65,97},{2,34},{34,66},{66,9... | collective-permute-start | bytes 1572872 | tf_op jit(solution)/shard_map/ppermute | solution.py:16
  57.6 0.8 copy-start.7
  65.6 15.6 %collective-permute-start.2 = (bf16[64,4096]{1,0:T(8,128)(2,1)}, bf16[64,4096]{1,0:T(8,128)(2,1)}, u32[]{:S(2)}, u32[]{:S(2)}) collective-permute-start(bf16[64,4096]{1,0:T(8,128)(2,1)} %fusion.9), channel_id=1, source_target_pairs={{0,32},{32,64},{64,96},{1,33},{33,65},{65,97},{2,34},{34,66},{66,9... | collective-permute-start | bytes 1572872 | tf_op jit(solution)/shard_map/ppermute | solution.py:16
  82.5 0.8 copy-start.5
  89.7 15.4 %collective-permute-start.3 = (bf16[64,4096]{1,0:T(8,128)(2,1)S(1)}, bf16[64,4096]{1,0:T(8,128)(2,1)S(1)}, u32[]{:S(2)}, u32[]{:S(2)}) collective-permute-start(bf16[64,4096]{1,0:T(8,128)(2,1)S(1)} %get-tuple-element.87), channel_id=1, source_target_pairs={{0,32},{32,64},{64,96},{1,33},{33,65},{65,97},{2,34},{34,66},{66,9... | collective-permute-start | bytes 1572872 | tf_op jit(solution)/shard_map/ppermute | solution.py:16
  106.5 0.8 copy-start.4
  114.5 15.3 %collective-permute-start.4 = (bf16[64,4096]{1,0:T(8,128)(2,1)S(1)}, bf16[64,4096]{1,0:T(8,128)(2,1)S(1)}, u32[]{:S(2)}, u32[]{:S(2)}) collective-permute-start(bf16[64,4096]{1,0:T(8,128)(2,1)S(1)} %get-tuple-element.89), channel_id=1, source_target_pairs={{0,32},{32,64},{64,96},{1,33},{33,65},{65,97},{2,34},{34,66},{66,9... | collective-permute-start | bytes 1572872 | tf_op jit(solution)/shard_map/ppermute | solution.py:16
  131.1 0.8 copy-start.2
  136.8 6.8 %copy-start.8 = (bf16[512,2560]{1,0:T(8,128)(2,1)S(1)}, bf16[512,2560]{1,0:T(8,128)(2,1)}, u32[]{:S(2)}) copy-start(bf16[512,2560]{1,0:T(8,128)(2,1)} %param.26) | copy-start | bytes 7864324
  139.5 15.3 %collective-permute-start.5 = (bf16[64,4096]{1,0:T(8,128)(2,1)S(1)}, bf16[64,4096]{1,0:T(8,128)(2,1)S(1)}, u32[]{:S(2)}, u32[]{:S(2)}) collective-permute-start(bf16[64,4096]{1,0:T(8,128)(2,1)S(1)} %get-tuple-element.91), channel_id=1, source_target_pairs={{0,32},{32,64},{64,96},{1,33},{33,65},{65,97},{2,34},{34,66},{66,9... | collective-permute-start | bytes 1572872 | tf_op jit(solution)/shard_map/ppermute | solution.py:16
  156.1 0.8 copy-start.3
  165.3 0.7 copy-start.11
  235.4 6.9 %copy-start.13 = (f32[2560]{0:T(1024)S(1)}, f32[2560]{0:T(1024)}, u32[]{:S(2)}) copy-start(f32[2560]{0:T(1024)} %param.27) | copy-start | bytes 30724
  235.4 69.3 %all-to-all-start = ((bf16[16,32,4096]{2,1,0:T(8,128)(2,1)}), bf16[16,32,4096]{2,1,0:T(8,128)(2,1)}, u32[]{:S(2)}, u32[]{:S(2)}) async-start(bf16[16,32,4096]{2,1,0:T(8,128)(2,1)} %bitcast.84), calls=%async_computation | async-start | bytes 8388608 | tf_op jit(solution)/shard_map/all_to_all | solution.py:91
  242.3 100.6 %all-reduce.14.cloned.1.call-start = ((), (), s32[]{:S(2)}) async-start(), calls=%async_computation.4 | async-start | bytes 5242880 | tf_op jit(solution)/shard_map/psum | solution.py:103
  315.9 0.7 copy-start.12
  316.0 118.0 %reduce-scatter.2.cloned.1.call-start = ((), (), s32[]{:S(2)}) async-start(), calls=%async_computation.3 | async-start | bytes 6963200 | tf_op jit(solution)/shard_map/reduce_scatter | solution.py:114
  352.1 1.3 copy-start.9
Sparse Core Ops, SparseCore 0:
  165.4 62.8 all-reduce.11
  316.1 26.7 all-reduce.13
  352.2 81.6 reduce-scatter.1
where the time goes:
time: 444 us; the launch traced here: 442 us
  waiting for transfers between devices  275 us (62%)
  matrix products  49.1 us (11%)
  blocking collectives  38.9 us (9%)
  starting transfers between devices  32 us (7%)
  other arithmetic  17.5 us (4%)
  local copies, waits for them, and re-layouts  15.5 us (3%)
  between operations  14.1 us (3%)
    reduce_scatter x1, waiting for transfers between devices, local(): lax.psum_scatter((jnp.einsum('rk,rn->kn', normed, grad_rows, preferred_el...  69.4 us
    ppermute x6, waiting for transfers between devices, shifted(): return lax.ppermute(shard, axis, pairs)  64.1 us
    psum x1, waiting for transfers between devices, spread(): return lax.psum(kept, axis)  61.4 us
    all_to_all x1, waiting for transfers between devices, local(): lax.all_to_all(outgoing, 'dp', split_axis=0, concat_axis=0, tiled=True)  54 us
    psum x1, waiting for transfers between devices, local(): lax.psum(target_part.astype(jnp.bfloat16), 'mp').astype(jnp.float32)  26.1 us
    psum x6, blocking collectives, section(): lax.psum(latent_part.astype(jnp.bfloat16), 'mp').astype(jnp.float32)  26 us
    ppermute x6, starting transfers between devices, shifted(): return lax.ppermute(shard, axis, pairs)  24.8 us
    dot_general x7, matrix products, section(): jnp.dot(chosen, up, preferred_element_type=jnp.float32)  14.5 us
  transfers between devices with their start and end apart: 10, of which 10 were waited for; matrix products, arithmetic and copies ran while one was open for 3% of the time, Pallas kernels for 0%

commit v1 on v0

v1 whole, which is shorter than its diff:
```python
import jax
import jax.numpy as jnp
from jax import lax
from jax.sharding import PartitionSpec as P

D = 8192
S = 5120
RANK = 64
TOK_DEV = 256
TEACH = 3
bf16 = jnp.bfloat16
f32 = jnp.float32


def dot(a, b):
    return jnp.dot(a, b, preferred_element_type=f32)


def local(
    teacher_hidden,
    teacher_id,
    destination,
    row_counts,
    section_gain,
    adapter_down,
    adapter_up,
    student_in,
    student_gain,
    student_weight,
    projector,
):
    h = teacher_hidden
    tok = h.shape[0]
    half = h.shape[1]
    n_seg = lax.axis_size("segment")
    n_dp = lax.axis_size("dp")
    i = lax.axis_index("dp")
    up = adapter_up[0]
    down = adapter_down[0]
    q = RANK // n_dp
    slots = student_in.shape[0]
    cap = slots // n_dp
    cols = projector.shape[1]
    mine = lax.dynamic_index_in_dim(up.reshape(TEACH, n_dp, q, half), i, 1, keepdims=False)
    u_all = lax.all_gather(mine.reshape(TEACH * q, half), "segment").reshape(n_seg * TEACH * q, half)
    scaled_down = (section_gain[0].astype(f32)[:, None] * down.astype(f32)).astype(bf16)
    up_t = up.T
    hp_part = dot(h, projector).astype(bf16)
    mg = jnp.stack([dot(u_all, scaled_down), dot(u_all, up_t)], axis=1)
    mg = mg.reshape(n_seg, TEACH, q, 2, TEACH, RANK)
    mg = jnp.stack([mg[:, k, :, :, k] for k in range(TEACH)], axis=1)
    mg = mg.reshape(n_seg * TEACH * q, 2 * RANK)
    ids = teacher_id
    pick = (ids[:, None] == jnp.arange(TEACH, dtype=jnp.int32)[None, :]).astype(f32)
    ab = jnp.stack([dot(h, scaled_down), dot(h, up_t)], axis=1).reshape(tok, 2, TEACH, RANK)
    ab = jnp.sum(ab * pick[:, None, :, None], axis=2).reshape(tok, 2 * RANK)
    wide = h.astype(f32)
    sq_part = jnp.sum(wide * wide, axis=1)
    x = student_in.astype(f32)
    sx_part = jnp.sum(x * x, axis=1)
    mg, ab, sq, sx = lax.psum((mg, ab, sq_part, sx_part), "mp")
    upp = lax.psum_scatter(dot(u_all, projector).astype(bf16), "mp", scatter_dimension=1, tiled=True)
    upp = lax.all_gather(upp, "dp")
    mg = lax.all_gather(mg.astype(bf16), ("dp", "segment"))
    mg = mg.reshape(n_dp, n_seg, n_seg, TEACH * q, 2 * RANK)
    hp = lax.psum_scatter(hp_part, "mp", scatter_dimension=1, tiled=True)
    onehot = (destination[:, None] == jnp.arange(n_dp, dtype=jnp.int32)[None, :]).astype(jnp.int32)
    earlier = jnp.cumsum(onehot, axis=0) - onehot
    position = destination * cap + jnp.sum(earlier * onehot, axis=1)
    sel = (position[None, :] == jnp.arange(slots, dtype=jnp.int32)[:, None]).astype(bf16)
    sq_hi = sq.astype(bf16)
    sq_lo = (sq - sq_hi.astype(f32)).astype(bf16)
    meta = jnp.concatenate(
        [ab.astype(bf16), jnp.stack([ids.astype(bf16), sq_hi, sq_lo], axis=1), jnp.zeros((tok, 125), bf16)], axis=1
    )
    send = dot(sel, meta).astype(bf16).reshape(n_dp, cap, -1)
    meta = lax.all_to_all(send, "dp", split_axis=0, concat_axis=0, tiled=True).reshape(slots, -1)
    send = dot(sel, hp).astype(bf16).reshape(n_dp, cap, -1)
    hp = lax.all_to_all(send, "dp", split_axis=0, concat_axis=0, tiled=True).reshape(slots, -1)
    ab = lax.all_gather(meta[:, : 2 * RANK], "segment").astype(f32)
    sid = meta[:, 2 * RANK].astype(f32)
    norm = meta[:, 2 * RANK + 1].astype(f32) + meta[:, 2 * RANK + 2].astype(f32)
    cidx = jnp.arange(n_dp * TEACH * q, dtype=jnp.int32)
    src = (cidx // (TEACH * q)) * q + cidx % q
    spread = (jnp.arange(RANK, dtype=jnp.int32)[:, None] == src[None, :]).astype(bf16)
    keep = ((cidx // q) % TEACH).astype(f32)[None, :] == sid[:, None]
    chosen = []
    for s in range(n_seg):
        a_s, b_s = ab[s, :, :RANK], ab[s, :, RANK:]
        lat = a_s
        cross = 2.0 * b_s
        for t in range(s):
            table = mg[:, s, t].reshape(n_dp * TEACH * q, 2 * RANK)
            both = dot(chosen[t], table)
            lat = lat + both[:, :RANK]
            cross = cross + 2.0 * both[:, RANK:]
        lat = (lat * lax.rsqrt(jnp.maximum(norm, 0.0) / D + 1e-06)[:, None]).astype(bf16)
        wide_c = jnp.where(keep, dot(lat, spread), 0.0).astype(bf16)
        table = mg[:, s, s, :, RANK:].reshape(n_dp * TEACH * q, RANK)
        cross = cross + dot(wide_c, table)
        norm = norm + jnp.sum(cross * lat.astype(f32), axis=1)
        chosen.append(wide_c)
    c_all = jnp.stack(chosen, axis=1).reshape(slots, n_seg, n_dp, TEACH * q)
    c_all = c_all.transpose(0, 2, 1, 3).reshape(slots, -1)
    target = hp.astype(f32) + dot(c_all, upp.reshape(-1, cols // 2))
    recip = lax.rsqrt(sx / S + 1e-06)
    sgated = (x * student_gain[None, :]).astype(bf16)
    so = lax.psum_scatter(dot(sgated, student_weight).astype(bf16), "mp", scatter_dimension=1, tiled=True).astype(f32)
    valid = (jnp.arange(cap, dtype=jnp.int32)[None, :] < row_counts[0][:, None]).reshape(slots)
    diff = jnp.where(valid[:, None], so * recip[:, None] - target, 0.0)
    row_loss = lax.psum(jnp.sum(diff * diff, axis=1), ("segment", "mp")) / S
    normed = (x * student_gain[None, :] * recip[:, None]).astype(bf16)
    grad_rows = lax.all_gather(diff.astype(bf16), "mp", axis=1, tiled=True)
    share = normed.shape[1] // n_dp
    weight_grad = lax.psum_scatter(
        (jnp.einsum("rk,rn->kn", normed, grad_rows, preferred_element_type=f32) / TOK_DEV).astype(bf16),
        "dp",
        scatter_dimension=0,
        tiled=True,
    ).astype(f32)
    return (weight_grad.reshape(1, share, cols), row_loss)


def solution(mesh):
    placed = (
        P("dp", "mp"),
        P("dp"),
        P("dp"),
        P("dp", None),
        P("segment", "mp"),
        P("segment", "mp", None),
        P("segment", None, "mp"),
        P("dp", "mp"),
        P("mp"),
        P("mp", "segment"),
        P("mp", "segment"),
    )
    return jax.shard_map(
        local,
        mesh=mesh,
        in_specs=placed,
        out_specs=(P("mp", "dp", "segment"), P("dp")),
        check_vma=False,
    )
```

time: 444 us -> 431 us (0.971)
  blocking collectives: 38.9 us -> 216 us
  waiting for transfers between devices: 275 us -> 116 us
  starting transfers between devices: 32 us -> 11.7 us
  other arithmetic: 17.5 us -> 7.3 us
  matrix products: 49.1 us -> 44.4 us
  local copies, waits for them, and re-layouts: 15.5 us -> 20.1 us
    all_gather x0 -> x4, blocking collectives: none -> 197 us  [the longest x1 153 us: local(): mg = lax.all_gather(mg.astype(bf16), ('dp', 'segment'))]
    psum x2 -> x0, waiting for transfers between devices: 87.6 us -> none  [the longest x1 61.4 us: spread(): return lax.psum(kept, axis)]
    ppermute x6 -> x0, waiting for transfers between devices: 64.1 us -> none  [shifted(): return lax.ppermute(shard, axis, pairs)]
    all_to_all x1 -> x2, waiting for transfers between devices: 54 us -> 0.01 us  [local(): lax.all_to_all(send, 'dp', split_axis=0, concat_axis=0, tiled=True)]
    all_gather x0 -> x1, waiting for transfers between devices: none -> 46.5 us  [local(): grad_rows = lax.all_gather(diff.astype(bf16), 'mp', axis=1, tiled=True)]
    ppermute x6 -> x0, starting transfers between devices: 24.8 us -> none  [shifted(): return lax.ppermute(shard, axis, pairs)]
    psum x8 -> x2, blocking collectives: 38.9 us -> 18.5 us  [the longest x1 12 us: local(): row_loss = lax.psum(jnp.sum(diff * diff, axis=1), ('segment', 'mp')) / S]
    reduce_sum x10 -> x4, other arithmetic: 12 us -> 1.2 us  [the longest x1 0.59 us: local(): sx_part = jnp.sum(x * x, axis=1)]
  transfers between devices with their start and end apart: 10 -> 7, of which waited for: 10 -> 2; matrix products, arithmetic and copies ran while one was open for 3% -> 11% of each run, Pallas kernels for 0% -> 0%
where the time goes in v1:
time: 431 us; the launch traced here: 430 us
  blocking collectives  216 us (50%)
  waiting for transfers between devices  116 us (27%)
  matrix products  44.4 us (10%)
  local copies, waits for them, and re-layouts  20.1 us (5%)
  between operations  14.4 us (3%)
  starting transfers between devices  11.7 us (3%)
  other arithmetic  7.3 us (2%)
    all_gather x1, blocking collectives, local(): mg = lax.all_gather(mg.astype(bf16), ('dp', 'segment'))  153 us
    reduce_scatter x1, waiting for transfers between devices, local(): lax.psum_scatter((jnp.einsum('rk,rn->kn', normed, grad_rows, preferred_el...  69.5 us
    all_gather x1, waiting for transfers between devices, local(): grad_rows = lax.all_gather(diff.astype(bf16), 'mp', axis=1, tiled=True)  46.5 us
    dot_general x22, matrix products, dot(): return jnp.dot(a, b, preferred_element_type=f32)  37.4 us
    all_gather x1, blocking collectives, local(): upp = lax.all_gather(upp, 'dp')  21.3 us
    all_gather x1, blocking collectives, local(): lax.all_gather(mine.reshape(TEACH * q, half), 'segment')  12.6 us
    unnamed x41, local copies, waits for them, and re-layouts  12.1 us
    psum x1, blocking collectives, local(): row_loss = lax.psum(jnp.sum(diff * diff, axis=1), ('segment', 'mp')) / S  12 us
  transfers between devices with their start and end apart: 7, of which 2 were waited for; matrix products, arithmetic and copies ran while one was open for 11% of the time, Pallas kernels for 0%

profile of v1, /device:TPU:1, one launch (start us, length us, event | category | flops | bytes accessed | tf_op | source)
XLA Modules:
  0.0 429.7 jit_solution(15450894747180848162)
XLA Ops:
  7.2 7.6 %convolution_convert_fusion.1 = bf16[256,1280]{1,0:T(8,128)(2,1)S(1)} fusion(bf16[256,4096]{1,0:T(8,128)(2,1)} %param.11, bf16[4096,1280]{1,0:T(8,128)(2,1)} %param.21), kind=kOutput, calls=%fused_computation.18 | convolution fusion | flops 2684682240 | bytes 13238272 | tf_op jit(solution)/shard_map/dot_general | solution.py:16
  14.9 1.1 copy.86
  16.0 0.5 multiply_reduce_fusion
  16.6 0.8 copy-done.3
  17.4 0.8 fusion.15
  18.2 1.5 fusion.7
  19.7 0.8 copy-done
  20.5 0.6 fusion.4
  21.1 0.6 reduce-window.6
  21.7 3.6 reshape_squeeze.30
  25.4 2.9 fusion.24
  28.3 0.9 dynamic-slice_bitcast_fusion
  29.3 12.6 %all_gather.26 = bf16[4,12,4096]{2,1,0:T(8,128)(2,1)S(1)} all-gather(bf16[1,12,4096]{2,1,0:T(8,128)(2,1)S(1)} %all_gather_reshape.3), channel_id=1, replica_groups=mesh['segment'=4,'dp'=16,'mp'=2] {'segment'}, dimensions={0}, use_global_device_ids=true | all-gather | bytes 491520 | tf_op jit(solution)/shard_map/all_gather | solution.py:45
  41.9 0.3 copy.71
  42.2 2.2 convolution_bitcast_fusion.1
  44.4 0.8 convolution_bitcast_fusion
  45.5 6.5 %all-reduce.2 = (bf16[256,128]{0,1:T(8,128)(2,1)S(1)}, f32[256]{0:T(256)S(1)}, bf16[48,128]{1,0:T(8,128)(2,1)S(1)}, f32[512]{0:T(512)}) all-reduce(f32[256,128]{0,1:T(8,128)S(1)} %bitcast.174, f32[256]{0:T(256)S(1)} %multiply_reduce_fusion, f32[48,128]{1,0:T(8,128)S(1)} %reshape.209, ...), channel_id=1, replica_groups=mesh['segment'=4,'dp'=16,'mp'=2] {'mp'}, use_global_device_ids=true, to_apply=%region_8.9 | all-reduce | flops 39680 | bytes 239616 | tf_op jit(solution)/shard_map/psum | solution.py:61
  52.2 0.3 concatenate.6
  52.7 1.0 convolution_convert_fusion.4
  53.6 7.8 %all-to-all-start.1 = ((bf16[16,32,256]{2,1,0:T(8,128)(2,1)}), bf16[16,32,256]{2,1,0:T(8,128)(2,1)}, u32[]{:S(2)}, u32[]{:S(2)}) async-start(bf16[16,32,256]{2,1,0:T(8,128)(2,1)} %bitcast.13), calls=%async_computation.1 | async-start | bytes 524288 | tf_op jit(solution)/shard_map/all_to_all | solution.py:77
  61.5 5.8 %convolution_convert_fusion.2 = bf16[48,1280]{1,0:T(8,128)(2,1)S(1)} fusion(bf16[48,4096]{1,0:T(8,128)(2,1)S(1)} %reshape.212, bf16[4096,1280]{1,0:T(8,128)(2,1)} %param.21), kind=kOutput, calls=%fused_computation.19 | convolution fusion | flops 503377920 | bytes 11001856 | tf_op jit(solution)/shard_map/dot_general | solution.py:16
  67.4 0.9 copy.88
  68.6 7.5 %convolution_convert_fusion = bf16[512,1280]{1,0:T(8,128)(2,1)} fusion(bf16[2560,1280]{1,0:T(8,128)(2,1)} %param.20, bf16[512,2560]{1,0:T(8,128)(2,1)S(1)} %copy-done, f32[2560]{0:T(1024)S(1)} %copy-done.11), kind=kOutput, calls=%fused_computation.14 | convolution fusion | flops 3360030720 | bytes 10496000 | tf_op jit(solution)/shard_map/dot_general | solution.py:16
  76.1 2.4 copy.84
  78.5 153.1 %all-gather.1 = bf16[3072,128]{1,0:T(8,128)(2,1)S(1)} all-gather(bf16[48,128]{1,0:T(8,128)(2,1)S(1)} %get-tuple-element.4), channel_id=3, replica_groups=mesh['segment'=4,'dp'=16,'mp'=2] {'dp','segment'}, dimensions={0}, use_global_device_ids=true | all-gather | bytes 798720 | tf_op jit(solution)/shard_map/all_gather | solution.py:64
  232.4 1.0 convert_reduce_fusion
  233.4 0.9 slice.141
  234.3 1.1 fusion.75
  235.7 10.2 %all-gather = bf16[2048,128]{1,0:T(8,128)(2,1)S(1)} all-gather(bf16[512,128]{1,0:T(8,128)(2,1)S(1)} %slice.141), channel_id=2, replica_groups=mesh['segment'=4,'dp'=16,'mp'=2] {'segment'}, dimensions={0}, use_global_device_ids=true | all-gather | bytes 655360 | tf_op jit(solution)/shard_map/all_gather | solution.py:80
  246.9 0.3 fusion.20
  247.9 0.3 fusion.21
  248.2 0.2 fusion.33
  248.7 0.3 fusion.22
  249.0 0.2 fusion.34
  249.7 2.2 convolution_convert_fusion.3
  251.9 3.6 all-to-all-start
  255.7 1.0 copy.89
  256.8 0.4 fusion.23
  257.7 21.3 %all-gather.2 = bf16[768,640]{1,0:T(8,128)(2,1)} all-gather(bf16[48,640]{1,0:T(8,128)(2,1)S(1)} %copy.89), channel_id=4, replica_groups=mesh['segment'=4,'dp'=16,'mp'=2] {'dp'}, dimensions={0}, use_global_device_ids=true | all-gather | bytes 1044480 | tf_op jit(solution)/shard_map/all_gather | solution.py:63
  279.0 2.2 copy.85
  281.1 0.8 copy-done.5
  282.0 3.5 multiply_reduce_fusion.1
  285.6 46.5 %all-gather.5.cloned.1.call-done = bf16[512,1280]{1,0:T(8,128)(2,1)} async-done(((bf16[512,640]{1,0:T(8,128)(2,1)}), bf16[512,1280]{1,0:T(8,128)(2,1)}) %all-gather.5.cloned.1.call-update) | async-done | bytes 1310736 | tf_op jit(solution)/shard_map/all_gather | solution.py:113
  332.1 7.1 %fusion = bf16[2560,1280]{1,0:T(8,128)(2,1)} fusion(bf16[512,1280]{1,0:T(8,128)(2,1)} %all-gather.5.cloned.1.call-done, bf16[512,2560]{1,0:T(8,128)(2,1)S(1)} %copy-done.1, f32[512]{0:T(512)S(1)} %add_rsqrt_fusion.4, f32[2560]{0:T(1024)S(1)} %copy-done.12), kind=kOutput, calls=%fused_computation.1 | convolution fusion | flops 3367239680 | bytes 10498048 | tf_op jit(solution)/shard_map/rk,rn->kn/dot_general | solution.py:116
  339.2 12.0 %psum.39 = f32[512]{0:T(512)S(1)} all-reduce(f32[512]{0:T(512)S(1)} %get-tuple-element.10), channel_id=1, replica_groups=mesh['segment'=4,'dp'=16,'mp'=2] {'segment','mp'}, use_global_device_ids=true, to_apply=%region_18.19 | all-reduce | flops 512 | bytes 4096 | tf_op jit(solution)/shard_map/psum | solution.py:111
  351.1 0.6 broadcast_multiply_fusion
  351.7 69.5 %reduce-scatter.11.cloned.1.call-done = bf16[160,1280]{1,0:T(8,128)(2,1)} async-done(((bf16[2560,1280]{1,0:T(8,128)(2,1)}), bf16[160,1280]{1,0:T(8,128)(2,1)}) %reduce-scatter.11.cloned.1.call-update) | async-done | bytes 409616 | tf_op jit(solution)/shard_map/reduce_scatter | solution.py:115
  421.2 1.9 bitcast_convert_fusion
  (104 shorter events, 5.2 us)
Async XLA Ops:
  7.2 242.5 %reduce-scatter.15.cloned.1.call-start = ((), (), s32[]{:S(2)}) async-start(), calls=%async_computation.9 | async-start | bytes 983040
  7.2 8.8 %copy-start.2 = (bf16[256,4096]{1,0:T(8,128)(2,1)S(1)}, bf16[256,4096]{1,0:T(8,128)(2,1)}, u32[]{:S(2)}) copy-start(bf16[256,4096]{1,0:T(8,128)(2,1)} %param.11) | copy-start | bytes 6291460
  14.8 1.6 copy-start.9
  14.9 1.7 copy-start.6
  16.0 1.4 copy-start.3
  18.2 2.3 copy-start
  19.7 1.4 copy-start.7
  29.3 15.1 %copy-start.4 = (bf16[1,192,4096]{2,1,0:T(8,128)(2,1)S(1)}, bf16[1,192,4096]{2,1,0:T(8,128)(2,1)}, u32[]{:S(2)}) copy-start(bf16[1,192,4096]{2,1,0:T(8,128)(2,1)} %param.17) | copy-start | bytes 4718596
  53.6 178.8 %all-to-all-start.1 = ((bf16[16,32,256]{2,1,0:T(8,128)(2,1)}), bf16[16,32,256]{2,1,0:T(8,128)(2,1)}, u32[]{:S(2)}, u32[]{:S(2)}) async-start(bf16[16,32,256]{2,1,0:T(8,128)(2,1)} %bitcast.13), calls=%async_computation.1 | async-start | bytes 524288 | tf_op jit(solution)/shard_map/all_to_all | solution.py:77
  61.4 194.4 %reduce-scatter.17.cloned.1.call-start = ((), (), s32[]{:S(2)}) async-start(), calls=%async_computation.10 | async-start | bytes 491520
  61.5 7.0 %copy-start.11 = (f32[2560]{0:T(1024)S(1)}, f32[2560]{0:T(1024)}, u32[]{:S(2)}) copy-start(f32[2560]{0:T(1024)} %param.19) | copy-start | bytes 30724
  68.3 210.7 %reduce-scatter.13.cloned.1.call-start = ((), (), s32[]{:S(2)}) async-start(), calls=%async_computation.8 | async-start | bytes 1966080
  78.5 153.4 %copy-start.10 = (s32[1,16]{1,0:T(1,128)S(1)}, s32[1,16]{1,0:T(1,128)}, u32[]{:S(2)}) copy-start(s32[1,16]{1,0:T(1,128)} %param.14) | copy-start | bytes 196
  231.6 0.7 copy-start.8
  251.9 29.3 %all-to-all-start = ((bf16[16,32,640]{2,1,0:T(8,128)(2,1)}), bf16[16,32,640]{2,1,0:T(8,128)(2,1)S(1)}, u32[]{:S(2)}, u32[]{:S(2)}) async-start(bf16[16,32,640]{2,1,0:T(8,128)(2,1)} %bitcast.3), calls=%async_computation | async-start | bytes 1310720 | tf_op jit(solution)/shard_map/all_to_all | solution.py:79
  255.5 76.6 %all-gather.5.cloned.1.call-start = ((), (), s32[]{:S(2)}) async-start(), calls=%async_computation.6 | async-start | bytes 1966080 | tf_op jit(solution)/shard_map/all_gather | solution.py:113
  281.1 0.8 copy-start.5
  282.0 50.1 %copy-start.1 = (bf16[512,2560]{1,0:T(8,128)(2,1)S(1)}, bf16[512,2560]{1,0:T(8,128)(2,1)}, u32[]{:S(2)}) copy-start(bf16[512,2560]{1,0:T(8,128)(2,1)} %param.18) | copy-start | bytes 7864324
  282.0 50.1 %copy-start.12 = (f32[2560]{0:T(1024)S(1)}, f32[2560]{0:T(1024)}, u32[]{:S(2)}) copy-start(f32[2560]{0:T(1024)} %param.19) | copy-start | bytes 30724
  285.5 135.7 %reduce-scatter.11.cloned.1.call-start = ((), (), s32[]{:S(2)}) async-start(), calls=%async_computation.7 | async-start | bytes 6963200 | tf_op jit(solution)/shard_map/reduce_scatter | solution.py:115
Sparse Core Ops, SparseCore 0:
  16.1 14.4 reduce-scatter.14
  68.4 12.2 reduce-scatter.16
  83.1 12.7 reduce-scatter.12
  285.6 46.3 all-gather.4
  339.3 81.8 reduce-scatter.10

commit v2 on v1

--- a/solution.py
+++ b/solution.py
@@ -1,6 +1,10 @@
+import functools
+
 import jax
 import jax.numpy as jnp
 from jax import lax
+from jax.experimental import pallas as pl
+from jax.experimental.pallas import tpu as pltpu
 from jax.sharding import PartitionSpec as P
 
 D = 8192
@@ -14,6 +18,216 @@
 
 def dot(a, b):
     return jnp.dot(a, b, preferred_element_type=f32)
+
+
+def remote(src, dst, send, recv, **where):
+    return pltpu.make_async_remote_copy(
+        src_ref=src,
+        dst_ref=dst,
+        send_sem=send,
+        recv_sem=recv,
+        device_id=where,
+        device_id_type=pl.DeviceIdType.MESH,
+    )
+
+
+def back_kernel(n_seg, side, sgt, gdh, loss, out, loss_out, gd, part, own, got, part2, got2, losses, ss, rs, ls, lr):
+    share = out.shape[0]
+    half = gdh.shape[1]
+    part_rows = share // 2
+    me_s = lax.axis_index("segment")
+    me_m = lax.axis_index("mp")
+    me_d = lax.axis_index("dp")
+    z = me_d // side
+    y = me_d % side
+    other = 1 - me_m
+    y_next = [z * side + (y + step) % side for step in (1, side - 1)]
+    z_next = [((z + step) % side) * side + y for step in (1, side - 1)]
+    rings = (y_next, z_next)
+    places = (y, z)
+
+    barrier = pltpu.get_barrier_semaphore()
+    for where in y_next + z_next:
+        pl.semaphore_signal(barrier, inc=1, device_id={"dp": where}, device_id_type=pl.DeviceIdType.MESH)
+    peers = []
+    for ds in range(n_seg):
+        for dm in range(2):
+            if ds or dm:
+                peers.append({"segment": (me_s + ds) % n_seg, "mp": (me_m + dm) % 2})
+    for where in peers:
+        pl.semaphore_signal(barrier, inc=1, device_id=where, device_id_type=pl.DeviceIdType.MESH)
+    pl.semaphore_wait(barrier, 4 + len(peers))
+
+    swap = remote(gdh, gd.at[me_m], ss.at[24], rs.at[24], mp=other)
+    swap.start()
+    mine = me_s * 2 + me_m
+    tells = []
+    for n, where in enumerate(peers):
+        tell = remote(loss, losses.at[mine], ls.at[n], lr.at[n], **where)
+        tell.start()
+        tells.append(tell)
+    losses[mine] = loss[...]
+    gd[me_m] = gdh[...]
+    swap.wait()
+
+    def rows(f, g, k):
+        block = (k * side + g) if f == 0 else (g * side + k)
+        return pl.ds(pl.multiple_of(block * share, share), share)
+
+    def product(f, g, k):
+        return jnp.dot(sgt[rows(f, g, k), :], gd[f], preferred_element_type=f32)
+
+    copies = []
+
+    def send(src, dst, number, where):
+        copy = remote(src, dst, ss.at[number], rs.at[number], dp=where)
+        copy.start()
+        copies.append(copy)
+        return copy
+
+    first = {}
+    for f in (0, 1):
+        far = (places[f] + 2) % side
+
+        @pl.loop(0, 2)
+        def _(k):
+            part[f, 1, k] = product(f, far, k).astype(bf16)
+
+        first[f, 0] = send(part.at[f, 1, 0:2], got.at[f, 0, 0], f * 6 + 0, rings[f][0])
+
+        @pl.loop(2, 4)
+        def _(k):
+            part[f, 1, k] = product(f, far, k).astype(bf16)
+
+        first[f, 1] = send(part.at[f, 1, 2:4], got.at[f, 1, 0], f * 6 + 3, rings[f][1])
+    second = {}
+    for f in (0, 1):
+        for way in (0, 1):
+            near = (places[f] + (1, side - 1)[way]) % side
+            low = 2 - 2 * way
+
+            @pl.loop(low, low + 2)
+            def _(k):
+                part[f, 2 * way, k] = product(f, near, k).astype(bf16)
+
+            second[f, way] = send(part.at[f, 2 * way, low : low + 2], got.at[f, way, 1], f * 6 + 3 * way + 1, rings[f][way])
+    third = {}
+    for f in (0, 1):
+        for way in (0, 1):
+            near = (places[f] + (1, side - 1)[way]) % side
+            low = 2 * way
+            first[f, way].wait_recv()
+
+            @pl.loop(low, low + 2)
+            def _(k):
+                part[f, 2 * way, k] = (product(f, near, k) + got[f, way, 0, k - low].astype(f32)).astype(bf16)
+
+            third[f, way] = send(part.at[f, 2 * way, low : low + 2], got.at[f, way, 2], f * 6 + 3 * way + 2, rings[f][way])
+    for f in (0, 1):
+
+        @pl.loop(0, 4)
+        def _(k):
+            own[f, k] = product(f, places[f], k)
+
+    first2 = {}
+    second2 = {}
+    third2 = {}
+    for f in (0, 1):
+        second[f, 0].wait_recv()
+        second[f, 1].wait_recv()
+
+        @pl.loop(0, 2)
+        def _(k):
+            own[f, k] += got[f, 1, 1, k].astype(f32)
+            own[f, k + 2] += got[f, 0, 1, k].astype(f32)
+
+    for f in (0, 1):
+        third[f, 0].wait_recv()
+        third[f, 1].wait_recv()
+
+        @pl.loop(0, 2)
+        def _(k):
+            own[f, k] += got[f, 0, 2, k].astype(f32)
+            own[f, k + 2] += got[f, 1, 2, k].astype(f32)
+
+        g = 1 - f
+        far = (places[g] + 2) % side
+        part2[f, 1] = own[f, far].astype(bf16)
+        base = 12 + f * 6
+        first2[f, 0] = send(part2.at[f, 1, 0:part_rows], got2.at[f, 0, 0], base, rings[g][0])
+        first2[f, 1] = send(part2.at[f, 1, part_rows:share], got2.at[f, 1, 0], base + 3, rings[g][1])
+        for way in (0, 1):
+            near = (places[g] + (1, side - 1)[way]) % side
+            low = (1 - way) * part_rows
+            part2[f, 2 * way, low : low + part_rows] = own[f, near, low : low + part_rows].astype(bf16)
+            second2[f, way] = send(part2.at[f, 2 * way, low : low + part_rows], got2.at[f, way, 1], base + 3 * way + 1, rings[g][way])
+    for f in (0, 1):
+        g = 1 - f
+        base = 12 + f * 6
+        for way in (0, 1):
+            near = (places[g] + (1, side - 1)[way]) % side
+            low = way * part_rows
+            first2[f, way].wait_recv()
+            part2[f, 2 * way, low : low + part_rows] = (
+                own[f, near, low : low + part_rows] + got2[f, way, 0].astype(f32)
+            ).astype(bf16)
+            third2[f, way] = send(part2.at[f, 2 * way, low : low + part_rows], got2.at[f, way, 2], base + 3 * way + 2, rings[g][way])
+    for tell in tells:
+        tell.wait()
+    total = losses[0]
+    for n in range(1, 2 * n_seg):
+        total = total + losses[n]
+    loss_out[...] = total * (1.0 / S)
+    for f in (0, 1):
+        g = 1 - f
+        for way in (0, 1):
+            second2[f, way].wait_recv()
+        for way in (0, 1):
+            third2[f, way].wait_recv()
+        span = slice(f * half, (f + 1) * half)
+        top = slice(0, part_rows)
+        end = slice(part_rows, share)
+        out[top, span] = own[f, places[g], top] + got2[f, 0, 2].astype(f32) + got2[f, 1, 1].astype(f32)
+        out[end, span] = own[f, places[g], end] + got2[f, 0, 1].astype(f32) + got2[f, 1, 2].astype(f32)
+    for copy in copies:
+        copy.wait_send()
+
+
+def back(sgt, grad_half, loss_part):
+    n_seg = lax.axis_size("segment")
+    n_dp = lax.axis_size("dp")
+    side = 4
+    share = sgt.shape[0] // n_dp
+    slots, half = grad_half.shape
+    half_rows = share // 2
+    vmem = pl.BlockSpec(memory_space=pltpu.VMEM)
+    flops = 2 * sgt.shape[0] * slots * 2 * half
+    return pl.pallas_call(
+        functools.partial(back_kernel, n_seg, side),
+        out_shape=(
+            jax.ShapeDtypeStruct((share, 2 * half), f32),
+            jax.ShapeDtypeStruct((1, slots), f32),
+        ),
+        in_specs=[vmem] * 3,
+        out_specs=(vmem, vmem),
+        scratch_shapes=[
+            pltpu.VMEM((2, slots, half), bf16),
+            pltpu.VMEM((2, 3, 4, share, half), bf16),
+            pltpu.VMEM((2, 4, share, half), f32),
+            pltpu.VMEM((2, 2, 3, 2, share, half), bf16),
+            pltpu.VMEM((2, 3, share, half), bf16),
+            pltpu.VMEM((2, 2, 3, half_rows, half), bf16),
+            pltpu.VMEM((2 * n_seg, 1, slots), f32),
+            pltpu.SemaphoreType.DMA((25,)),
+            pltpu.SemaphoreType.DMA((25,)),
+            pltpu.SemaphoreType.DMA((2 * n_seg - 1,)),
+            pltpu.SemaphoreType.DMA((2 * n_seg - 1,)),
+        ],
+        compiler_params=pltpu.CompilerParams(
+            collective_id=1, has_side_effects=True, vmem_limit_bytes=56 * 2**20
+        ),
+        cost_estimate=pl.CostEstimate(flops=flops, bytes_accessed=8 * 2**20, transcendentals=0),
+    )(sgt, grad_half, loss_part)
 
 
 def local(
@@ -61,7 +275,7 @@
     mg, ab, sq, sx = lax.psum((mg, ab, sq_part, sx_part), "mp")
     upp = lax.psum_scatter(dot(u_all, projector).astype(bf16), "mp", scatter_dimension=1, tiled=True)
     upp = lax.all_gather(upp, "dp")
-    mg = lax.all_gather(mg.astype(bf16), ("dp", "segment"))
+    mg = lax.all_gather(lax.all_gather(mg.astype(bf16), "segment"), "dp")
     mg = mg.reshape(n_dp, n_seg, n_seg, TEACH * q, 2 * RANK)
     hp = lax.psum_scatter(hp_part, "mp", scatter_dimension=1, tiled=True)
     onehot = (destination[:, None] == jnp.arange(n_dp, dtype=jnp.int32)[None, :]).astype(jnp.int32)
@@ -108,16 +322,11 @@
     so = lax.psum_scatter(dot(sgated, student_weight).astype(bf16), "mp", scatter_dimension=1, tiled=True).astype(f32)
     valid = (jnp.arange(cap, dtype=jnp.int32)[None, :] < row_counts[0][:, None]).reshape(slots)
     diff = jnp.where(valid[:, None], so * recip[:, None] - target, 0.0)
-    row_loss = lax.psum(jnp.sum(diff * diff, axis=1), ("segment", "mp")) / S
-    normed = (x * student_gain[None, :] * recip[:, None]).astype(bf16)
-    grad_rows = lax.all_gather(diff.astype(bf16), "mp", axis=1, tiled=True)
-    share = normed.shape[1] // n_dp
-    weight_grad = lax.psum_scatter(
-        (jnp.einsum("rk,rn->kn", normed, grad_rows, preferred_element_type=f32) / TOK_DEV).astype(bf16),
-        "dp",
-        scatter_dimension=0,
-        tiled=True,
-    ).astype(f32)
+    loss_part = jnp.sum(diff * diff, axis=1).reshape(1, slots)
+    grad_half = (diff * (recip / TOK_DEV)[:, None]).astype(bf16)
+    weight_grad, row_loss = back(sgated.T, grad_half, loss_part)
+    share = weight_grad.shape[0]
+    row_loss = row_loss.reshape(slots)
     return (weight_grad.reshape(1, share, cols), row_loss)
 
 

time: 431 us -> 238 us (0.55)
  blocking collectives: 216 us -> 80.1 us
  waiting for transfers between devices: 116 us -> 0.11 us
  Pallas kernels: 0 us -> 61.7 us
  matrix products: 44.4 us -> 35.9 us
  local copies, waits for them, and re-layouts: 20.1 us -> 25.3 us
    all_gather x1 -> x2, blocking collectives: 153 us -> 28.7 us  [local(): mg = lax.all_gather(lax.all_gather(mg.astype(bf16), 'segment'), 'dp')]
    reduce_scatter x1 -> x0, waiting for transfers between devices: 69.5 us -> none  [local(): lax.psum_scatter((jnp.einsum('rk,rn->kn', normed, grad_rows, preferred_el...]
    pallas_call x0 -> x1, Pallas kernels: none -> 61.7 us  [back(): pl.pallas_call(functools.partial(back_kernel, n_seg, side), out_shape=(ja...]
    all_gather x1 -> x0, waiting for transfers between devices: 46.5 us -> none  [local(): grad_rows = lax.all_gather(diff.astype(bf16), 'mp', axis=1, tiled=True)]
    psum x1 -> x0, blocking collectives: 12 us -> none  [local(): row_loss = lax.psum(jnp.sum(diff * diff, axis=1), ('segment', 'mp')) / S]
    dot_general x1 -> x0, matrix products: 7.06 us -> none  [local(): jnp.einsum('rk,rn->kn', normed, grad_rows, preferred_element_type=f32)]
    unnamed x41 -> x38, local copies, waits for them, and re-layouts: 12.1 us -> 16.1 us
  transfers between devices with their start and end apart: 7 -> 5, of which waited for: 2 -> 0; matrix products, arithmetic and copies ran while one was open for 11% -> 22% of each run, Pallas kernels for 0% -> 0%
where the time goes in v2:
time: 238 us; the launch traced here: 237 us
  blocking collectives  80.1 us (34%)
  Pallas kernels  61.7 us (26%)
  matrix products  35.9 us (15%)
  local copies, waits for them, and re-layouts  25.3 us (11%)
  between operations  14.4 us (6%)
  starting transfers between devices  12.5 us (5%)
  other arithmetic  6.49 us (3%)
    pallas_call x1, Pallas kernels, back(): pl.pallas_call(functools.partial(back_kernel, n_seg, side), out_shape=(ja...  61.7 us
    dot_general x22, matrix products, dot(): return jnp.dot(a, b, preferred_element_type=f32)  35.9 us
    all_gather x2, blocking collectives, local(): mg = lax.all_gather(lax.all_gather(mg.astype(bf16), 'segment'), 'dp')  28.7 us
    all_gather x1, blocking collectives, local(): upp = lax.all_gather(upp, 'dp')  22.6 us
    unnamed x38, local copies, waits for them, and re-layouts  16.1 us
    all_gather x1, blocking collectives, local(): lax.all_gather(mine.reshape(TEACH * q, half), 'segment')  12.4 us
    all_to_all x2, starting transfers between devices, local(): lax.all_to_all(send, 'dp', split_axis=0, concat_axis=0, tiled=True)  12.2 us
    all_gather x1, blocking collectives, local(): ab = lax.all_gather(meta[:, :2 * RANK], 'segment').astype(f32)  9.94 us
  transfers between devices with their start and end apart: 5, of which 0 were waited for; matrix products, arithmetic and copies ran while one was open for 22% of the time, Pallas kernels for 0%

profile of v2, /device:TPU:1, one launch (start us, length us, event | category | flops | bytes accessed | tf_op | source)
XLA Modules:
  0.0 236.5 jit_solution(13458849246857763595)
XLA Ops:
  7.2 7.6 %convolution_convert_fusion.1 = bf16[256,1280]{1,0:T(8,128)(2,1)S(1)} fusion(bf16[256,4096]{1,0:T(8,128)(2,1)} %param.11, bf16[4096,1280]{1,0:T(8,128)(2,1)} %param.21), kind=kOutput, calls=%fused_computation.11 | convolution fusion | flops 2684682240 | bytes 13238272 | tf_op jit(solution)/shard_map/dot_general | solution.py:20
  14.9 1.1 copy.131
  16.0 0.5 multiply_reduce_fusion
  16.6 0.8 copy-done.1
  17.4 0.8 fusion.7
  18.2 1.5 fusion.4
  19.7 0.6 reduce-window.6
  20.3 3.6 %reshape_squeeze.30 = bf16[3,16,4,4096]{3,2,1,0:T(4,128)(2,1)} reshape(bf16[1,192,4096]{2,1,0:T(8,128)(2,1)} %param.17) | data formatting | bytes 3145728 | tf_op jit(solution)/shard_map/reshape;squeeze | solution.py:258
  24.0 2.3 fusion.16
  26.3 1.1 dynamic-slice_bitcast_fusion
  27.4 12.4 %all_gather.29 = bf16[4,12,4096]{2,1,0:T(8,128)(2,1)S(1)} all-gather(bf16[1,12,4096]{2,1,0:T(8,128)(2,1)S(1)} %all_gather_reshape.3), channel_id=1, replica_groups=mesh['segment'=4,'dp'=16,'mp'=2] {'segment'}, dimensions={0}, use_global_device_ids=true | all-gather | bytes 491520 | tf_op jit(solution)/shard_map/all_gather | solution.py:259
  39.7 0.3 copy.106
  40.1 2.2 convolution_bitcast_fusion.1
  42.3 0.8 convolution_bitcast_fusion
  43.3 3.0 %copy.99 = bf16[512,2560]{0,1:T(8,128)(2,1)S(1)} copy(bf16[512,2560]{1,0:T(8,128)(2,1)} %param.18) | data formatting | bytes 5242880 | tf_op args[7]
  46.3 2.3 fusion.1
  48.6 6.5 %all-reduce.2 = (bf16[256,128]{0,1:T(8,128)(2,1)S(1)}, f32[256]{0:T(256)S(1)}, bf16[48,128]{1,0:T(8,128)(2,1)S(1)}, f32[512]{0:T(512)}) all-reduce(f32[256,128]{0,1:T(8,128)S(1)} %bitcast.198, f32[256]{0:T(256)S(1)} %multiply_reduce_fusion, f32[48,128]{1,0:T(8,128)S(1)} %reshape.213, ...), channel_id=1, replica_groups=mesh['segment'=4,'dp'=16,'mp'=2] {'mp'}, use_global_device_ids=true, to_apply=%region_8.9 | all-reduce | flops 39680 | bytes 239616 | tf_op jit(solution)/shard_map/psum | solution.py:275
  55.4 0.3 concatenate.6
  55.8 1.0 convolution_convert_fusion.4
  56.8 7.8 %all-to-all-start.1 = ((bf16[16,32,256]{2,1,0:T(8,128)(2,1)}), bf16[16,32,256]{2,1,0:T(8,128)(2,1)}, u32[]{:S(2)}, u32[]{:S(2)}) async-start(bf16[16,32,256]{2,1,0:T(8,128)(2,1)} %bitcast.14), calls=%async_computation.1 | async-start | bytes 524288 | tf_op jit(solution)/shard_map/all_to_all | solution.py:291
  64.7 5.8 %convolution_convert_fusion.2 = bf16[48,1280]{1,0:T(8,128)(2,1)S(1)} fusion(bf16[48,4096]{1,0:T(8,128)(2,1)S(1)} %reshape.216, bf16[4096,1280]{1,0:T(8,128)(2,1)} %param.21), kind=kOutput, calls=%fused_computation.12 | convolution fusion | flops 503377920 | bytes 11001856 | tf_op jit(solution)/shard_map/dot_general | solution.py:20
  70.6 0.9 copy.133
  71.7 7.8 %convolution_convert_fusion = bf16[512,1280]{1,0:T(8,128)(2,1)} fusion(bf16[2560,1280]{1,0:T(8,128)(2,1)} %param.20, bf16[512,2560]{0,1:T(8,128)(2,1)S(1)} %copy.99, f32[2560]{0:T(1024)S(1)} %copy-done.5), kind=kOutput, calls=%fused_computation.10 | convolution fusion | flops 3360030720 | bytes 10496000 | tf_op jit(solution)/shard_map/dot_general | solution.py:20
  79.5 2.4 %copy.129 = bf16[512,1280]{0,1:T(8,128)(2,1)} copy(bf16[512,1280]{1,0:T(8,128)(2,1)} %convolution_convert_fusion) | data formatting | bytes 2621440
  82.0 9.4 %all-gather.1 = bf16[192,128]{1,0:T(8,128)(2,1)S(1)} all-gather(bf16[48,128]{1,0:T(8,128)(2,1)S(1)} %get-tuple-element.8), channel_id=3, replica_groups=mesh['segment'=4,'dp'=16,'mp'=2] {'segment'}, dimensions={0}, use_global_device_ids=true | all-gather | bytes 61440 | tf_op jit(solution)/shard_map/all_gather | solution.py:278
  91.4 19.3 %all-gather.2 = bf16[64,48,128]{2,1,0:T(8,128)(2,1)S(1)} all-gather(bf16[4,48,128]{2,1,0:T(8,128)(2,1)S(1)} %bitcast.202), channel_id=4, replica_groups=mesh['segment'=4,'dp'=16,'mp'=2] {'dp'}, dimensions={0}, use_global_device_ids=true | all-gather | bytes 835584 | tf_op jit(solution)/shard_map/all_gather | solution.py:278
  110.9 0.5 fusion.67
  111.4 0.6 fusion.66
  112.8 1.0 convert_reduce_fusion
  113.8 0.9 slice.141
  114.7 1.1 fusion.69
  116.1 9.9 %all-gather = bf16[2048,128]{1,0:T(8,128)(2,1)S(1)} all-gather(bf16[512,128]{1,0:T(8,128)(2,1)S(1)} %slice.141), channel_id=2, replica_groups=mesh['segment'=4,'dp'=16,'mp'=2] {'segment'}, dimensions={0}, use_global_device_ids=true | all-gather | bytes 655360 | tf_op jit(solution)/shard_map/all_gather | solution.py:294
  127.1 0.3 fusion.12
  127.3 0.2 fusion.24
  128.0 0.3 fusion.13
  128.3 0.2 fusion.25
  128.8 0.3 fusion.14
  129.1 0.2 fusion.26
  129.8 2.2 convolution_convert_fusion.3
  132.0 4.4 %all-to-all-start = ((bf16[16,32,640]{2,1,0:T(8,128)(2,1)}), bf16[16,32,640]{2,1,0:T(8,128)(2,1)S(1)}, u32[]{:S(2)}, u32[]{:S(2)}) async-start(bf16[16,32,640]{2,1,0:T(8,128)(2,1)} %bitcast.4), calls=%async_computation | async-start | bytes 1310720 | tf_op jit(solution)/shard_map/all_to_all | solution.py:293
  136.6 1.0 copy.134
  137.6 0.4 fusion.15
  138.6 22.6 %all-gather.3 = bf16[768,640]{1,0:T(8,128)(2,1)S(1)} all-gather(bf16[48,640]{1,0:T(8,128)(2,1)S(1)} %copy.134), channel_id=5, replica_groups=mesh['segment'=4,'dp'=16,'mp'=2] {'dp'}, dimensions={0}, use_global_device_ids=true | all-gather | bytes 1044480 | tf_op jit(solution)/shard_map/all_gather | solution.py:277
  161.1 1.4 copy.130
  162.5 2.4 %multiply_reduce_fusion.1 = (f32[512]{0:T(512)}, bf16[512,640]{1,0:T(8,128)(2,1)}) fusion(f32[512]{0:T(512)S(1)} %get-tuple-element.39, bf16[512,768]{0,1:T(8,128)(2,1)S(1)} %reshape.215, bf16[768,640]{1,0:T(8,128)(2,1)S(1)} %all-gather.3, bf16[512,640]{1,0:T(8,128)(2,1)S(1)} %bitcast.197, f32[512]{0:T(512)S(1)} %get-tuple-element.40, ...), kind=kOutput, calls=%fused_computation.21 | convolution fusion | flops 506592768 | bytes 3742208 | tf_op jit(solution)/shard_map/dot_general | solution.py:20
  164.9 61.7 %shard_map.122 = (f32[160,1280]{1,0:T(8,128)}, f32[1,512]{1,0:T(1,128)}) custom-call(bf16[2560,512]{1,0:T(8,128)(2,1)} %get-tuple-element.15.sgt, bf16[512,640]{1,0:T(8,128)(2,1)} %get-tuple-element.17.gdh, f32[1,512]{1,0:T(1,128)} %bitcast.218), custom_call_target="tpu_custom_call" | custom-call | flops 3355443200 | bytes 8388608 | tf_op jit(solution)/shard_map/pallas_call | solution.py:205
  226.7 2.1 copy.157
  228.7 1.3 copy.158
  (102 shorter events, 5.1 us)
Async XLA Ops:
  7.2 122.6 %reduce-scatter.12.cloned.1.call-start = ((), (), s32[]{:S(2)}) async-start(), calls=%async_computation.6 | async-start | bytes 983040
  7.2 8.8 %copy-start = (bf16[256,4096]{1,0:T(8,128)(2,1)S(1)}, bf16[256,4096]{1,0:T(8,128)(2,1)}, u32[]{:S(2)}) copy-start(bf16[256,4096]{1,0:T(8,128)(2,1)} %param.11) | copy-start | bytes 6291460
  14.8 1.6 copy-start.8
  14.9 1.7 copy-start.3
  16.0 1.4 copy-start.1
  18.2 1.5 copy-start.6
  26.3 16.0 %copy-start.2 = (bf16[1,192,4096]{2,1,0:T(8,128)(2,1)S(1)}, bf16[1,192,4096]{2,1,0:T(8,128)(2,1)}, u32[]{:S(2)}) copy-start(bf16[1,192,4096]{2,1,0:T(8,128)(2,1)} %param.17) | copy-start | bytes 4718596
  43.3 3.0 %copy-start.4 = (f32[2560]{0:T(1024)S(1)}, f32[2560]{0:T(1024)}, u32[]{:S(2)}) copy-start(f32[2560]{0:T(1024)} %param.19) | copy-start | bytes 30724
  56.8 56.0 %all-to-all-start.1 = ((bf16[16,32,256]{2,1,0:T(8,128)(2,1)}), bf16[16,32,256]{2,1,0:T(8,128)(2,1)}, u32[]{:S(2)}, u32[]{:S(2)}) async-start(bf16[16,32,256]{2,1,0:T(8,128)(2,1)} %bitcast.14), calls=%async_computation.1 | async-start | bytes 524288 | tf_op jit(solution)/shard_map/all_to_all | solution.py:291
  64.6 72.0 %reduce-scatter.14.cloned.1.call-start = ((), (), s32[]{:S(2)}) async-start(), calls=%async_computation.7 | async-start | bytes 491520
  64.7 7.0 %copy-start.5 = (f32[2560]{0:T(1024)S(1)}, f32[2560]{0:T(1024)}, u32[]{:S(2)}) copy-start(f32[2560]{0:T(1024)} %param.19) | copy-start | bytes 30724
  71.5 89.6 %reduce-scatter.10.cloned.1.call-start = ((), (), s32[]{:S(2)}) async-start(), calls=%async_computation.5 | async-start | bytes 1966080
  91.4 20.6 %copy-start.9 = (s32[1,16]{1,0:T(1,128)S(1)}, s32[1,16]{1,0:T(1,128)}, u32[]{:S(2)}) copy-start(s32[1,16]{1,0:T(1,128)} %param.14) | copy-start | bytes 196
  110.9 1.8 copy-start.7
  132.0 30.5 %all-to-all-start = ((bf16[16,32,640]{2,1,0:T(8,128)(2,1)}), bf16[16,32,640]{2,1,0:T(8,128)(2,1)S(1)}, u32[]{:S(2)}, u32[]{:S(2)}) async-start(bf16[16,32,640]{2,1,0:T(8,128)(2,1)} %bitcast.4), calls=%async_computation | async-start | bytes 1310720 | tf_op jit(solution)/shard_map/all_to_all | solution.py:293
Sparse Core Ops, SparseCore 0:
  16.1 14.4 reduce-scatter.11
  71.6 12.2 reduce-scatter.13
  86.2 12.7 reduce-scatter.9

commit v3 on v2

--- a/solution.py
+++ b/solution.py
@@ -2,6 +2,7 @@
 
 import jax
 import jax.numpy as jnp
+import numpy as np
 from jax import lax
 from jax.experimental import pallas as pl
 from jax.experimental.pallas import tpu as pltpu
@@ -12,6 +13,7 @@
 RANK = 64
 TOK_DEV = 256
 TEACH = 3
+LANES = 128
 bf16 = jnp.bfloat16
 f32 = jnp.float32
 
@@ -230,6 +232,393 @@
     )(sgt, grad_half, loss_part)
 
 
+def iota(shape, dim):
+    return lax.broadcasted_iota(jnp.int32, shape, dim)
+
+
+def ones_where(mask):
+    return jnp.where(mask, 1.0, 0.0).astype(bf16)
+
+
+def dot_nt(a, b):
+    return lax.dot_general(a, b, (((1,), (1,)), ((), ())), preferred_element_type=f32)
+
+
+def turned(row):
+    return jnp.broadcast_to(row, (LANES, row.shape[1])).T
+
+
+def fold(wide, keep):
+    kept = jnp.where(keep, wide, 0.0)
+    both = kept[:, :LANES] + kept[:, LANES:]
+    return both + pltpu.roll(both, RANK, 1)
+
+
+def front_kernel(
+    n_seg, n_dp, cap,
+    h_hbm, down_hbm, up_hbm, x_hbm, w_hbm, p_hbm, xmap_hbm,
+    ids, dest, counts, gain, sgain, kcol,
+    gd_out, loss_out, sgt_out,
+    h, down, up, x, w, p, xmap,
+    usend, ugot, ucat, wide_a, wide_b, abx, abgot, sel, pay, aslots, agot, aall,
+    mgx, mggot, mgs, mgall, upx, upgot, upall,
+    hpx, hpsend, hpgot, hslots, hgot,
+    sg, sox, sosend, sogot, sxx, sxgot, ctil,
+    lsem, s_m, r_m, s_x, r_x, s_d, r_d,
+):
+    me_s = lax.axis_index("segment")
+    me_m = lax.axis_index("mp")
+    me_d = lax.axis_index("dp")
+    other = 1 - me_m
+    tok, half = h.shape
+    slots = x.shape[0]
+    cols = p.shape[1]
+    out_half = cols // 2
+    rows_u = mgx.shape[0]
+    per = rows_u // n_seg
+    q = per // TEACH
+    part = half // n_seg
+
+    loads = []
+    for n, (src, dst) in enumerate(
+        ((up_hbm, up), (h_hbm, h), (down_hbm, down), (p_hbm, p), (xmap_hbm, xmap), (x_hbm, x), (w_hbm, w))
+    ):
+        copy = pltpu.make_async_copy(src, dst, lsem.at[n])
+        copy.start()
+        loads.append(copy)
+    up_in, h_in, down_in, p_in, xmap_in, x_in, w_in = loads
+
+    barrier = pltpu.get_barrier_semaphore()
+    mesh_id = pl.DeviceIdType.MESH
+    pl.semaphore_signal(barrier, inc=1, device_id={"mp": other}, device_id_type=mesh_id)
+    for n in range(1, n_seg):
+        pl.semaphore_signal(barrier, inc=1, device_id={"segment": (me_s + n) % n_seg}, device_id_type=mesh_id)
+
+    @pl.loop(1, n_dp)
+    def _(n):
+        pl.semaphore_signal(barrier, inc=1, device_id={"dp": (me_d + n) % n_dp}, device_id_type=mesh_id)
+
+    def to_peer(n, src, dst):
+        return remote(src, dst, s_m.at[n], r_m.at[n], mp=other)
+
+    def to_seg(kind, n, src, dst):
+        number = kind * (n_seg - 1) + n - 1
+        return remote(src, dst, s_x.at[number], r_x.at[number], segment=(me_s + n) % n_seg)
+
+    def to_dp(kind, n, src, dst):
+        number = kind * (n_dp - 1) + n - 1
+        return remote(src, dst, s_d.at[number], r_d.at[number], dp=(me_d + n) % n_dp)
+
+    packed = n_seg * per
+    row = iota((packed, up.shape[0]), 0)
+    col = iota((packed, up.shape[0]), 1)
+    quad = row >> 2
+    block = (quad >= 3).astype(jnp.int32) + (quad >= 6).astype(jnp.int32) + (quad >= 9).astype(jnp.int32)
+    teacher = quad - 3 * block
+    hit = ((col >> 6) == teacher) & (((col & 63) >> 2) == me_d) & ((col & 3) == (row & 3))
+    up_in.wait()
+    mine = jnp.zeros((packed, part), f32)
+    for g in range(n_seg):
+        mine = mine + dot(ones_where(hit & (block == g)), up[:, g * part : (g + 1) * part])
+    usend[...] = mine.astype(bf16)
+    ugot[me_s] = usend[...]
+    pl.semaphore_wait(barrier, 1 + (n_seg - 1) + (n_dp - 1))
+    u_sent = [to_seg(0, n, usend, ugot.at[me_s]) for n in range(1, n_seg)]
+    for copy in u_sent:
+        copy.start()
+
+    h_in.wait()
+    down_in.wait()
+    wide_a[...] = jnp.zeros(wide_a.shape, f32)
+    wide_b[...] = jnp.zeros(wide_b.shape, f32)
+    abx[...] = jnp.zeros(abx.shape, f32)
+    rank_all = down.shape[1]
+
+    @pl.loop(0, n_seg)
+    def _(g):
+        span = pl.ds(pl.multiple_of(g * part, part), part)
+        here = h[:, span]
+        wide = here.astype(f32)
+        scaled = (wide * gain[:, span].astype(f32)).astype(bf16)
+        wide_a[:, :rank_all] += dot(scaled, down[span, :])
+        wide_b[:, :rank_all] += dot_nt(here, up[:, span])
+        abx[:, LANES:] += jnp.broadcast_to(jnp.sum(wide * wide, axis=1, keepdims=True), (tok, LANES))
+
+    id_col = turned(ids[...].astype(f32))
+    lane2 = iota((tok, 2 * LANES), 1)
+    own = (lane2 >> 6).astype(f32) == jnp.concatenate([id_col, id_col], axis=1)
+    lane = iota((tok, LANES), 1)
+    abx[:, :LANES] = jnp.where(lane < RANK, fold(wide_a[...], own), fold(wide_b[...], own))
+    ab_sent = to_peer(0, abx, abgot)
+    ab_sent.start()
+
+    dest_f = dest[...].astype(f32)
+    onehot = jnp.where(iota((n_dp, tok), 0).astype(f32) == dest_f, 1.0, 0.0)
+    before = ones_where(iota((tok, tok), 0) < iota((tok, tok), 1))
+    earlier = dot(onehot.astype(bf16), before)
+    position = dest_f * cap + jnp.sum(earlier * onehot, axis=0, keepdims=True)
+    sel[...] = ones_where(iota((slots, tok), 0).astype(f32) == position)
+
+    ab_sent.wait_recv()
+    total = abx[...] + abgot[...]
+    sq = total[:, LANES:]
+    sq_hi = sq.astype(bf16).astype(f32)
+    extra = jnp.where(lane == 0, id_col, jnp.where(lane == 1, sq_hi, jnp.where(lane == 2, sq - sq_hi, 0.0)))
+    pay[:, :LANES] = total[:, :LANES].astype(bf16)
+    pay[:, LANES:] = extra.astype(bf16)
+    aslots[...] = dot(sel[...], pay[...]).astype(bf16).reshape(aslots.shape)
+    agot[me_d] = aslots[me_d]
+
+    def a_copy(n):
+        return to_dp(0, n, aslots.at[(me_d + n) % n_dp], agot.at[me_d])
+
+    @pl.loop(1, n_dp)
+    def _(n):
+        a_copy(n).start()
+
+    for copy in u_sent:
+        copy.wait_recv()
+    row = iota((packed, n_seg * packed), 0)
+    col = iota((packed, n_seg * packed), 1)
+    quad = row >> 2
+    block = (quad >= 3).astype(jnp.int32) + (quad >= 6).astype(jnp.int32) + (quad >= 9).astype(jnp.int32)
+    got_u = ugot[...].reshape(n_seg * packed, part)
+    for g in range(n_seg):
+        take = ones_where(col == row + (packed - per) * block + per * g)
+        ucat[:, g * part : (g + 1) * part] = dot(take, got_u).astype(bf16)
+    u = ucat[...]
+    u_scaled = (u.astype(f32) * gain[...].astype(f32)).astype(bf16)
+    wide_a[:rows_u, :rank_all] = dot(u_scaled, down[...])
+    wide_b[:rows_u, :rank_all] = dot_nt(u, up[...])
+    row = iota((rows_u, 2 * LANES), 0)
+    quad = row >> 2
+    block = (quad >= 3).astype(jnp.int32) + (quad >= 6).astype(jnp.int32) + (quad >= 9).astype(jnp.int32)
+    same = (quad - 3 * block) == (iota((rows_u, 2 * LANES), 1) >> 6)
+    lane_u = iota((rows_u, LANES), 1)
+    mgx[...] = jnp.where(lane_u < RANK, fold(wide_a[:rows_u, :], same), fold(wide_b[:rows_u, :], same))
+    mg_sent = to_peer(1, mgx, mggot)
+    mg_sent.start()
+    p_in.wait()
+    tile = 2 * LANES
+
+    @pl.loop(0, cols // tile)
+    def _(n):
+        span = pl.ds(pl.multiple_of(n * tile, tile), tile)
+        upx[:, span] = dot(ucat[...], p[:, span])
+
+    away = pl.ds(pl.multiple_of(other * out_half, LANES), out_half)
+    kept = pl.ds(pl.multiple_of(me_m * out_half, LANES), out_half)
+    up_sent = to_peer(2, upx.at[:, away], upgot)
+    up_sent.start()
+    mg_sent.wait_recv()
+    mgs[me_s] = (mgx[...] + mggot[...]).astype(bf16)
+    mg_x = [to_seg(1, n, mgs.at[me_s], mgs.at[me_s]) for n in range(1, n_seg)]
+    for copy in mg_x:
+        copy.start()
+    up_sent.wait_recv()
+    upall[me_d] = (upx[:, kept] + upgot[...]).astype(bf16)
+
+    def u_copy(n):
+        return to_dp(1, n, upall.at[me_d], upall.at[me_d])
+
+    @pl.loop(1, n_dp)
+    def _(n):
+        u_copy(n).start()
+
+    @pl.loop(0, cols // tile)
+    def _(n):
+        span = pl.ds(pl.multiple_of(n * tile, tile), tile)
+        hpx[:, span] = dot(h[...], p[:, span])
+
+    hpsend[...] = hpx[:, away].astype(bf16)
+    hp_sent = to_peer(3, hpsend, hpgot)
+    hp_sent.start()
+    for copy in mg_x:
+        copy.wait_recv()
+    pair = n_seg // 2
+    mgall[me_m, me_d] = mgs[pl.ds(me_m * pair, pair)]
+
+    def m_copy(n):
+        return to_dp(2, n, mgall.at[me_m, me_d], mgall.at[me_m, me_d])
+
+    @pl.loop(1, n_dp)
+    def _(n):
+        m_copy(n).start()
+
+    @pl.loop(1, n_dp)
+    def _(n):
+        a_copy(n).wait_recv()
+
+    aall[me_s] = agot[:, :, :LANES].reshape(slots, LANES)
+    a_x = [to_seg(2, n, aall.at[me_s], aall.at[me_s]) for n in range(1, n_seg)]
+    for copy in a_x:
+        copy.start()
+    hp_sent.wait_recv()
+    hp = (hpx[:, kept] + hpgot[...].astype(f32)).astype(bf16)
+    hslots[...] = dot(sel[...], hp).astype(bf16).reshape(hslots.shape)
+    hgot[me_d] = hslots[me_d]
+
+    def h_copy(n):
+        return to_dp(3, n, hslots.at[(me_d + n) % n_dp], hgot.at[me_d])
+
+    @pl.loop(1, n_dp)
+    def _(n):
+        h_copy(n).start()
+
+    x_in.wait()
+    chunk = 128
+
+    @pl.loop(0, slots // chunk)
+    def _(n):
+        span = pl.ds(pl.multiple_of(n * chunk, chunk), chunk)
+        wide = x[span, :].astype(f32)
+        sxx[span, :] = jnp.broadcast_to(jnp.sum(wide * wide, axis=1, keepdims=True), (chunk, LANES))
+        sg[span, :] = (wide * sgain[...]).astype(bf16)
+
+    sx_sent = to_peer(4, sxx, sxgot)
+    sx_sent.start()
+    w_in.wait()
+
+    @pl.loop(0, cols // tile)
+    def _(n):
+        span = pl.ds(pl.multiple_of(n * tile, tile), tile)
+        sox[:, span] = dot(sg[...], w[:, span])
+
+    sosend[...] = sox[:, away].astype(bf16)
+    so_sent = to_peer(5, sosend, sogot)
+    so_sent.start()
+
+    @pl.loop(0, x.shape[1] // chunk)
+    def _(n):
+        span = pl.ds(pl.multiple_of(n * chunk, chunk), chunk)
+        sgt_out[span, :] = sg[:, span].T
+
+    xmap_in.wait()
+
+    @pl.loop(1, n_dp)
+    def _(n):
+        m_copy(n).wait_recv()
+
+    mg_swap = to_peer(6, mgall.at[me_m], mgall.at[me_m])
+    mg_swap.start()
+    extra = agot[:, :, LANES:].reshape(slots, LANES).astype(f32)
+    id_slot = extra[:, 0:1]
+    norm = extra[:, 1:2] + extra[:, 2:3]
+    keep = kcol[...] == id_slot
+    lane = iota((slots, LANES), 1)
+    for copy in a_x:
+        copy.wait_recv()
+    mg_swap.wait_recv()
+    known = rows_u * n_dp
+    both = jnp.zeros((slots, LANES), f32)
+    for s in range(n_seg):
+        ab = aall[s].astype(f32)
+        lat = (ab + both) * lax.rsqrt(jnp.maximum(norm, 0.0) * (1.0 / D) + 1e-06)
+        lat = lat.astype(bf16)
+        lat_low = jnp.where(lane < RANK, lat.astype(f32), 0.0)
+        wide_c = jnp.where(keep, dot(lat_low.astype(bf16), xmap[s]), 0.0).astype(bf16)
+        if s == 0:
+            ctil[...] = wide_c
+        else:
+            ctil[...] += wide_c
+        if s + 1 < n_seg:
+            here = mgall[s // pair, :, s % pair].reshape(known, LANES)
+            after = mgall[(s + 1) // pair, :, (s + 1) % pair].reshape(known, LANES)
+            self_part = dot(ctil[...], here)
+            lat_high = pltpu.roll(lat_low, RANK, 1)
+            norm = norm + jnp.sum(lat_high * (2.0 * ab + both + self_part), axis=1, keepdims=True)
+            both = dot(ctil[...], after)
+
+    @pl.loop(1, n_dp)
+    def _(n):
+        u_copy(n).wait_recv()
+        h_copy(n).wait_recv()
+
+    sx_sent.wait_recv()
+    so_sent.wait_recv()
+    table = upall[...].reshape(known, out_half)
+    slot = iota((slots, n_dp), 0)
+    source = iota((slots, n_dp), 1)
+    room = slot - source * cap
+    valid = jnp.sum(
+        jnp.where((room >= 0) & (room < cap) & (room < counts[...]), 1.0, 0.0), axis=1, keepdims=True
+    )
+    recip = lax.rsqrt((sxx[:, 0:1] + sxgot[:, 0:1]) * (1.0 / S) + 1e-06)
+    target = dot(ctil[...], table) + hgot[...].reshape(slots, out_half).astype(f32)
+    out = (sox[:, kept] + sogot[...].astype(f32)) * recip
+    diff = jnp.where(valid > 0.0, out - target, 0.0)
+    loss = jnp.sum(diff * diff, axis=1, keepdims=True)
+    loss_out[...] = jnp.broadcast_to(loss, (slots, LANES)).T[0:1, :]
+    gd_out[...] = (diff * (recip * (1.0 / TOK_DEV))).astype(bf16)
+
+    for copy in u_sent + mg_x + a_x + [ab_sent, mg_sent, up_sent, hp_sent, sx_sent, so_sent, mg_swap]:
+        copy.wait_send()
+
+    @pl.loop(1, n_dp)
+    def _(n):
+        a_copy(n).wait_send()
+        u_copy(n).wait_send()
+        m_copy(n).wait_send()
+        h_copy(n).wait_send()
+
+
+def front(h, ids, dest, counts, gain, down, up, x, sgain, w, p):
+    n_seg = lax.axis_size("segment")
+    n_dp = lax.axis_size("dp")
+    tok, half = h.shape
+    slots, width = x.shape
+    cols = p.shape[1]
+    out_half = cols // 2
+    cap = slots // n_dp
+    q = RANK // n_dp
+    per = TEACH * q
+    rows_u = n_seg * per
+    known = rows_u * n_dp
+    c = np.arange(known)
+    c_i, c_t, c_k, c_q = c // rows_u, c % rows_u // per, c % per // q, c % q
+    spot = np.arange(LANES)[None, :, None]
+    xmap = (np.arange(n_seg)[:, None, None] == c_t) & (spot == c_i * q + c_q)
+    xmap = jnp.asarray(xmap.astype(np.float32), dtype=bf16)
+    kcol = jnp.asarray(c_k[None, :].astype(np.float32))
+    vmem = pl.BlockSpec(memory_space=pltpu.VMEM)
+    hbm = pl.BlockSpec(memory_space=pl.ANY)
+    flops = 2 * (tok * half * cols + slots * width * cols)
+    scratch = [
+        (h.shape, bf16), (down.shape, bf16), (up.shape, bf16), (x.shape, bf16), (w.shape, bf16), (p.shape, bf16),
+        (xmap.shape, bf16),
+        ((rows_u, half // n_seg), bf16), ((n_seg, rows_u, half // n_seg), bf16), ((rows_u, half), bf16),
+        ((tok, 2 * LANES), f32), ((tok, 2 * LANES), f32), ((tok, 2 * LANES), f32), ((tok, 2 * LANES), f32),
+        ((slots, tok), bf16), ((tok, 2 * LANES), bf16),
+        ((n_dp, cap, 2 * LANES), bf16), ((n_dp, cap, 2 * LANES), bf16), ((n_seg, slots, LANES), bf16),
+        ((rows_u, LANES), f32), ((rows_u, LANES), f32), ((n_seg, rows_u, LANES), bf16),
+        ((2, n_dp, n_seg // 2, rows_u, LANES), bf16),
+        ((rows_u, cols), f32), ((rows_u, out_half), f32), ((n_dp, rows_u, out_half), bf16),
+        ((tok, cols), f32), ((tok, out_half), bf16), ((tok, out_half), bf16),
+        ((n_dp, cap, out_half), bf16), ((n_dp, cap, out_half), bf16),
+        (x.shape, bf16), ((slots, cols), f32), ((slots, out_half), bf16), ((slots, out_half), bf16),
+        ((slots, LANES), f32), ((slots, LANES), f32), ((slots, known), bf16),
+    ]
+    sems = [7, 7, 7, 3 * (n_seg - 1), 3 * (n_seg - 1), 4 * (n_dp - 1), 4 * (n_dp - 1)]
+    return pl.pallas_call(
+        functools.partial(front_kernel, n_seg, n_dp, cap),
+        out_shape=(
+            jax.ShapeDtypeStruct((slots, out_half), bf16),
+            jax.ShapeDtypeStruct((1, slots), f32),
+            jax.ShapeDtypeStruct((width, slots), bf16),
+        ),
+        in_specs=[hbm] * 7 + [vmem] * 6,
+        out_specs=(vmem, vmem, vmem),
+        scratch_shapes=[pltpu.VMEM(*s) for s in scratch] + [pltpu.SemaphoreType.DMA((n,)) for n in sems],
+        compiler_params=pltpu.CompilerParams(
+            collective_id=0, has_side_effects=True, vmem_limit_bytes=60 * 2**20
+        ),
+        cost_estimate=pl.CostEstimate(flops=flops, bytes_accessed=25 * 2**20, transcendentals=0),
+    )(
+        h, down, up, x, w, p, xmap,
+        ids.reshape(1, tok), dest.reshape(1, tok), counts, gain, sgain.reshape(1, width), kcol,
+    )
+
+
 def local(
     teacher_hidden,
     teacher_id,
@@ -243,91 +632,22 @@
     student_weight,
     projector,
 ):
-    h = teacher_hidden
-    tok = h.shape[0]
-    half = h.shape[1]
-    n_seg = lax.axis_size("segment")
-    n_dp = lax.axis_size("dp")
-    i = lax.axis_index("dp")
-    up = adapter_up[0]
-    down = adapter_down[0]
-    q = RANK // n_dp
-    slots = student_in.shape[0]
-    cap = slots // n_dp
-    cols = projector.shape[1]
-    mine = lax.dynamic_index_in_dim(up.reshape(TEACH, n_dp, q, half), i, 1, keepdims=False)
-    u_all = lax.all_gather(mine.reshape(TEACH * q, half), "segment").reshape(n_seg * TEACH * q, half)
-    scaled_down = (section_gain[0].astype(f32)[:, None] * down.astype(f32)).astype(bf16)
-    up_t = up.T
-    hp_part = dot(h, projector).astype(bf16)
-    mg = jnp.stack([dot(u_all, scaled_down), dot(u_all, up_t)], axis=1)
-    mg = mg.reshape(n_seg, TEACH, q, 2, TEACH, RANK)
-    mg = jnp.stack([mg[:, k, :, :, k] for k in range(TEACH)], axis=1)
-    mg = mg.reshape(n_seg * TEACH * q, 2 * RANK)
-    ids = teacher_id
-    pick = (ids[:, None] == jnp.arange(TEACH, dtype=jnp.int32)[None, :]).astype(f32)
-    ab = jnp.stack([dot(h, scaled_down), dot(h, up_t)], axis=1).reshape(tok, 2, TEACH, RANK)
-    ab = jnp.sum(ab * pick[:, None, :, None], axis=2).reshape(tok, 2 * RANK)
-    wide = h.astype(f32)
-    sq_part = jnp.sum(wide * wide, axis=1)
-    x = student_in.astype(f32)
-    sx_part = jnp.sum(x * x, axis=1)
-    mg, ab, sq, sx = lax.psum((mg, ab, sq_part, sx_part), "mp")
-    upp = lax.psum_scatter(dot(u_all, projector).astype(bf16), "mp", scatter_dimension=1, tiled=True)
-    upp = lax.all_gather(upp, "dp")
-    mg = lax.all_gather(lax.all_gather(mg.astype(bf16), "segment"), "dp")
-    mg = mg.reshape(n_dp, n_seg, n_seg, TEACH * q, 2 * RANK)
-    hp = lax.psum_scatter(hp_part, "mp", scatter_dimension=1, tiled=True)
-    onehot = (destination[:, None] == jnp.arange(n_dp, dtype=jnp.int32)[None, :]).astype(jnp.int32)
-    earlier = jnp.cumsum(onehot, axis=0) - onehot
-    position = destination * cap + jnp.sum(earlier * onehot, axis=1)
-    sel = (position[None, :] == jnp.arange(slots, dtype=jnp.int32)[:, None]).astype(bf16)
-    sq_hi = sq.astype(bf16)
-    sq_lo = (sq - sq_hi.astype(f32)).astype(bf16)
-    meta = jnp.concatenate(
-        [ab.astype(bf16), jnp.stack([ids.astype(bf16), sq_hi, sq_lo], axis=1), jnp.zeros((tok, 125), bf16)], axis=1
+    grad_half, loss_part, sgt = front(
+        teacher_hidden,
+        teacher_id,
+        destination,
+        row_counts,
+        section_gain,
+        adapter_down[0],
+        adapter_up[0],
+        student_in,
+        student_gain,
+        student_weight,
+        projector,
     )
-    send = dot(sel, meta).astype(bf16).reshape(n_dp, cap, -1)
-    meta = lax.all_to_all(send, "dp", split_axis=0, concat_axis=0, tiled=True).reshape(slots, -1)
-    send = dot(sel, hp).astype(bf16).reshape(n_dp, cap, -1)
-    hp = lax.all_to_all(send, "dp", split_axis=0, concat_axis=0, tiled=True).reshape(slots, -1)
-    ab = lax.all_gather(meta[:, : 2 * RANK], "segment").astype(f32)
-    sid = meta[:, 2 * RANK].astype(f32)
-    norm = meta[:, 2 * RANK + 1].astype(f32) + meta[:, 2 * RANK + 2].astype(f32)
-    cidx = jnp.arange(n_dp * TEACH * q, dtype=jnp.int32)
-    src = (cidx // (TEACH * q)) * q + cidx % q
-    spread = (jnp.arange(RANK, dtype=jnp.int32)[:, None] == src[None, :]).astype(bf16)
-    keep = ((cidx // q) % TEACH).astype(f32)[None, :] == sid[:, None]
-    chosen = []
-    for s in range(n_seg):
-        a_s, b_s = ab[s, :, :RANK], ab[s, :, RANK:]
-        lat = a_s
-        cross = 2.0 * b_s
-        for t in range(s):
-            table = mg[:, s, t].reshape(n_dp * TEACH * q, 2 * RANK)
-            both = dot(chosen[t], table)
-            lat = lat + both[:, :RANK]
-            cross = cross + 2.0 * both[:, RANK:]
-        lat = (lat * lax.rsqrt(jnp.maximum(norm, 0.0) / D + 1e-06)[:, None]).astype(bf16)
-        wide_c = jnp.where(keep, dot(lat, spread), 0.0).astype(bf16)
-        table = mg[:, s, s, :, RANK:].reshape(n_dp * TEACH * q, RANK)
-        cross = cross + dot(wide_c, table)
-        norm = norm + jnp.sum(cross * lat.astype(f32), axis=1)
-        chosen.append(wide_c)
-    c_all = jnp.stack(chosen, axis=1).reshape(slots, n_seg, n_dp, TEACH * q)
-    c_all = c_all.transpose(0, 2, 1, 3).reshape(slots, -1)
-    target = hp.astype(f32) + dot(c_all, upp.reshape(-1, cols // 2))
-    recip = lax.rsqrt(sx / S + 1e-06)
-    sgated = (x * student_gain[None, :]).astype(bf16)
-    so = lax.psum_scatter(dot(sgated, student_weight).astype(bf16), "mp", scatter_dimension=1, tiled=True).astype(f32)
-    valid = (jnp.arange(cap, dtype=jnp.int32)[None, :] < row_counts[0][:, None]).reshape(slots)
-    diff = jnp.where(valid[:, None], so * recip[:, None] - target, 0.0)
-    loss_part = jnp.sum(diff * diff, axis=1).reshape(1, slots)
-    grad_half = (diff * (recip / TOK_DEV)[:, None]).astype(bf16)
-    weight_grad, row_loss = back(sgated.T, grad_half, loss_part)
-    share = weight_grad.shape[0]
-    row_loss = row_loss.reshape(slots)
-    return (weight_grad.reshape(1, share, cols), row_loss)
+    weight_grad, row_loss = back(sgt, grad_half, loss_part)
+    share, cols = weight_grad.shape
+    return (weight_grad.reshape(1, share, cols), row_loss.reshape(student_in.shape[0]))
 
 
 def solution(mesh):

time: 238 us -> 107 us (0.45)
  blocking collectives: 80.1 us -> 0 us
  matrix products: 35.9 us -> 0 us
  Pallas kernels: 61.7 us -> 97.3 us
  local copies, waits for them, and re-layouts: 25.3 us -> 8.48 us
  between operations: 14.4 us -> 0.65 us
  starting transfers between devices: 12.5 us -> 0 us
  other arithmetic: 6.49 us -> 0 us
    all_gather x5 -> x0, blocking collectives: 73.6 us -> none  [the longest x2 28.7 us: local(): mg = lax.all_gather(lax.all_gather(mg.astype(bf16), 'segment'), 'dp')]
    pallas_call x0 -> x1, Pallas kernels: none -> 50 us  [front(): pl.pallas_call(functools.partial(front_kernel, n_seg, n_dp, cap), out_sha...]
    dot_general x22 -> x0, matrix products: 35.9 us -> none  [dot(): return jnp.dot(a, b, preferred_element_type=f32)]
    pallas_call x1, Pallas kernels: 61.7 us -> 47.3 us  [back(): pl.pallas_call(functools.partial(back_kernel, n_seg, side), out_shape=(ja...]
    all_to_all x2 -> x0, starting transfers between devices: 12.2 us -> none  [local(): lax.all_to_all(send, 'dp', split_axis=0, concat_axis=0, tiled=True)]
    unnamed x38 -> x3, local copies, waits for them, and re-layouts: 16.1 us -> 7.17 us
    psum x1 -> x0, blocking collectives: 6.47 us -> none  [local(): mg, ab, sq, sx = lax.psum((mg, ab, sq_part, sx_part), 'mp')]
    another operation x20 -> x0, local copies, waits for them, and re-layouts: 4.09 us -> none  [the longest x1 3.65 us: local(): up.reshape(TEACH, n_dp, q, half)]
  transfers between devices with their start and end apart: 5 -> 0, of which waited for: 0 -> 0; matrix products, arithmetic and copies ran while one was open for 22% -> 0% of each run, Pallas kernels for 0% -> 0%
where the time goes in v3:
time: 107 us; the launch traced here: 106 us
  Pallas kernels  97.3 us (91%)
  local copies, waits for them, and re-layouts  8.48 us (8%)
    pallas_call x1, Pallas kernels, front(): pl.pallas_call(functools.partial(front_kernel, n_seg, n_dp, cap), out_sha...  50 us
    pallas_call x1, Pallas kernels, back(): pl.pallas_call(functools.partial(back_kernel, n_seg, side), out_shape=(ja...  47.3 us
    unnamed x3, local copies, waits for them, and re-layouts  7.17 us

profile of v3, /device:TPU:1, one launch (start us, length us, event | category | flops | bytes accessed | tf_op | source)
XLA Modules:
  0.0 106.4 jit_solution(1640952810922232476)
XLA Ops:
  0.6 1.3 %reshape.21.sgain = f32[1,2560]{1,0:T(1,128)} reshape(f32[2560]{0:T(1024)} %param.21) | data formatting | bytes 20480 | tf_op jit(solution)/shard_map/reshape | solution.py:618
  1.9 3.8 %copy.15 = bf16[1,4096,192]{2,1,0:T(8,128)(2,1)} copy(bf16[1,4096,192]{1,2,0:T(8,128)(2,1)} %param.18) | data formatting | bytes 3145728 | tf_op args[5]
  5.8 50.0 %shard_map.140 = (bf16[512,640]{1,0:T(8,128)(2,1)}, f32[1,512]{1,0:T(1,128)}, bf16[2560,512]{1,0:T(8,128)(2,1)}) custom-call(bf16[256,4096]{1,0:T(8,128)(2,1)} %h_hbm.1, bf16[4096,192]{1,0:T(8,128)(2,1)} %bitcast.6, bf16[192,4096]{1,0:T(8,128)(2,1)} %bitcast.7, bf16[512,2560]{1,0:T(8,128)(2,1)} %x_hbm.1, bf16[2560,1280]{1,0:T(8,128)(2,1)} %w_hbm.1, ...), custom_call_target="tpu_custom_call" | custom-call | flops 6039797760 | bytes 26214400 | tf_op jit(solution)/shard_map/pallas_call | solution.py:602
  55.7 47.3 %shard_map.141 = (f32[160,1280]{1,0:T(8,128)}, f32[1,512]{1,0:T(1,128)}) custom-call(bf16[2560,512]{1,0:T(8,128)(2,1)} %get-tuple-element.7.sgt, bf16[512,640]{1,0:T(8,128)(2,1)} %get-tuple-element.8.gdh, f32[1,512]{1,0:T(1,128)} %get-tuple-element.9.loss), custom_call_target="tpu_custom_call" | custom-call | flops 3355443200 | bytes 8388608 | tf_op jit(solution)/shard_map/pallas_call | solution.py:207
  103.1 2.1 %copy.18 = f32[1,160,1280]{2,1,0:T(8,128)} copy(f32[1,160,1280]{2,1,0:T(8,128)} %bitcast.8) | data formatting | bytes 1638400
  105.2 1.3 %copy.19 = f32[512]{0:T(512)} copy(f32[512]{0:T(512)} %bitcast.9) | data formatting | bytes 4096

commit v4 on v3

--- a/solution.py
+++ b/solution.py
@@ -255,13 +255,13 @@
 
 
 def front_kernel(
-    n_seg, n_dp, cap,
+    n_seg, side, cap,
     h_hbm, down_hbm, up_hbm, x_hbm, w_hbm, p_hbm, xmap_hbm,
     ids, dest, counts, gain, sgain, kcol,
     gd_out, loss_out, sgt_out,
     h, down, up, x, w, p, xmap,
     usend, ugot, ucat, wide_a, wide_b, abx, abgot, sel, pay, aslots, agot, aall,
-    mgx, mggot, mgs, mgall, upx, upgot, upall,
+    mgx, mggot, mgs, upx, upgot, blocks, tables,
     hpx, hpsend, hpgot, hslots, hgot,
     sg, sox, sosend, sogot, sxx, sxgot, ctil,
     lsem, s_m, r_m, s_x, r_x, s_d, r_d,
@@ -270,23 +270,40 @@
     me_m = lax.axis_index("mp")
     me_d = lax.axis_index("dp")
     other = 1 - me_m
+    n_dp = side * side
     tok, half = h.shape
     slots = x.shape[0]
     cols = p.shape[1]
     out_half = cols // 2
     rows_u = mgx.shape[0]
     per = rows_u // n_seg
-    q = per // TEACH
     part = half // n_seg
-
-    loads = []
-    for n, (src, dst) in enumerate(
-        ((up_hbm, up), (h_hbm, h), (down_hbm, down), (p_hbm, p), (xmap_hbm, xmap), (x_hbm, x), (w_hbm, w))
-    ):
+    tile = 2 * LANES
+    tiles = cols // tile
+    pair = n_seg // 2
+
+    def load(n, src, dst):
         copy = pltpu.make_async_copy(src, dst, lsem.at[n])
         copy.start()
-        loads.append(copy)
-    up_in, h_in, down_in, p_in, xmap_in, x_in, w_in = loads
+        return copy
+
+    def p_copy(n):
+        span = pl.ds(pl.multiple_of(n * tile, tile), tile)
+        return pltpu.make_async_copy(p_hbm.at[:, span], p.at[:, span], lsem.at[5 + n])
+
+    def w_copy(n):
+        span = pl.ds(pl.multiple_of(n * tile, tile), tile)
+        return pltpu.make_async_copy(w_hbm.at[:, span], w.at[:, span], lsem.at[5 + tiles + n])
+
+    up_in = load(0, up_hbm, up)
+    h_in = load(1, h_hbm, h)
+    for n in range(tiles):
+        p_copy(n).start()
+    down_in = load(2, down_hbm, down)
+    x_in = load(3, x_hbm, x)
+    for n in range(tiles):
+        w_copy(n).start()
+    xmap_in = load(4, xmap_hbm, xmap)
 
     barrier = pltpu.get_barrier_semaphore()
     mesh_id = pl.DeviceIdType.MESH
@@ -308,6 +325,22 @@
     def to_dp(kind, n, src, dst):
         number = kind * (n_dp - 1) + n - 1
         return remote(src, dst, s_d.at[number], r_d.at[number], dp=(me_d + n) % n_dp)
+
+    z = me_d // side
+    y = me_d % side
+
+    def place(first, second):
+        a = ((z * other + y * me_m) + second) % side
+        b = ((y * other + z * me_m) + first) % side
+        return (a * other + b * me_m) * side + b * other + a * me_m
+
+    def gather_first(n):
+        return remote(blocks.at[me_d], blocks.at[me_d], s_d.at[n + 29], r_d.at[n + 29], dp=place(n, 0))
+
+    def gather_second(k, n):
+        source = place(side - k, 0)
+        number = 33 + k * (side - 1) + n - 1
+        return remote(blocks.at[source], blocks.at[source], s_d.at[number], r_d.at[number], dp=place(0, n))
 
     packed = n_seg * per
     row = iota((packed, up.shape[0]), 0)
@@ -327,54 +360,29 @@
     for copy in u_sent:
         copy.start()
 
-    h_in.wait()
-    down_in.wait()
-    wide_a[...] = jnp.zeros(wide_a.shape, f32)
-    wide_b[...] = jnp.zeros(wide_b.shape, f32)
-    abx[...] = jnp.zeros(abx.shape, f32)
-    rank_all = down.shape[1]
-
-    @pl.loop(0, n_seg)
-    def _(g):
-        span = pl.ds(pl.multiple_of(g * part, part), part)
-        here = h[:, span]
-        wide = here.astype(f32)
-        scaled = (wide * gain[:, span].astype(f32)).astype(bf16)
-        wide_a[:, :rank_all] += dot(scaled, down[span, :])
-        wide_b[:, :rank_all] += dot_nt(here, up[:, span])
-        abx[:, LANES:] += jnp.broadcast_to(jnp.sum(wide * wide, axis=1, keepdims=True), (tok, LANES))
-
-    id_col = turned(ids[...].astype(f32))
-    lane2 = iota((tok, 2 * LANES), 1)
-    own = (lane2 >> 6).astype(f32) == jnp.concatenate([id_col, id_col], axis=1)
-    lane = iota((tok, LANES), 1)
-    abx[:, :LANES] = jnp.where(lane < RANK, fold(wide_a[...], own), fold(wide_b[...], own))
-    ab_sent = to_peer(0, abx, abgot)
-    ab_sent.start()
-
     dest_f = dest[...].astype(f32)
     onehot = jnp.where(iota((n_dp, tok), 0).astype(f32) == dest_f, 1.0, 0.0)
     before = ones_where(iota((tok, tok), 0) < iota((tok, tok), 1))
     earlier = dot(onehot.astype(bf16), before)
     position = dest_f * cap + jnp.sum(earlier * onehot, axis=0, keepdims=True)
     sel[...] = ones_where(iota((slots, tok), 0).astype(f32) == position)
-
-    ab_sent.wait_recv()
-    total = abx[...] + abgot[...]
-    sq = total[:, LANES:]
-    sq_hi = sq.astype(bf16).astype(f32)
-    extra = jnp.where(lane == 0, id_col, jnp.where(lane == 1, sq_hi, jnp.where(lane == 2, sq - sq_hi, 0.0)))
-    pay[:, :LANES] = total[:, :LANES].astype(bf16)
-    pay[:, LANES:] = extra.astype(bf16)
-    aslots[...] = dot(sel[...], pay[...]).astype(bf16).reshape(aslots.shape)
-    agot[me_d] = aslots[me_d]
-
-    def a_copy(n):
-        return to_dp(0, n, aslots.at[(me_d + n) % n_dp], agot.at[me_d])
-
-    @pl.loop(1, n_dp)
-    def _(n):
-        a_copy(n).start()
+    wide_a[...] = jnp.zeros(wide_a.shape, f32)
+    wide_b[...] = jnp.zeros(wide_b.shape, f32)
+    abx[...] = jnp.zeros(abx.shape, f32)
+
+    away = pl.ds(pl.multiple_of(other * out_half, LANES), out_half)
+    kept = pl.ds(pl.multiple_of(me_m * out_half, LANES), out_half)
+    h_in.wait()
+
+    @pl.loop(0, tiles)
+    def _(n):
+        span = pl.ds(pl.multiple_of(n * tile, tile), tile)
+        p_copy(n).wait()
+        hpx[:, span] = dot(h[...], p[:, span])
+
+    hpsend[...] = hpx[:, away].astype(bf16)
+    hp_sent = to_peer(3, hpsend, hpgot)
+    hp_sent.start()
 
     for copy in u_sent:
         copy.wait_recv()
@@ -386,9 +394,11 @@
     for g in range(n_seg):
         take = ones_where(col == row + (packed - per) * block + per * g)
         ucat[:, g * part : (g + 1) * part] = dot(take, got_u).astype(bf16)
+    down_in.wait()
+    rank_all = down.shape[0]
     u = ucat[...]
     u_scaled = (u.astype(f32) * gain[...].astype(f32)).astype(bf16)
-    wide_a[:rows_u, :rank_all] = dot(u_scaled, down[...])
+    wide_a[:rows_u, :rank_all] = dot_nt(u_scaled, down[...])
     wide_b[:rows_u, :rank_all] = dot_nt(u, up[...])
     row = iota((rows_u, 2 * LANES), 0)
     quad = row >> 2
@@ -398,16 +408,12 @@
     mgx[...] = jnp.where(lane_u < RANK, fold(wide_a[:rows_u, :], same), fold(wide_b[:rows_u, :], same))
     mg_sent = to_peer(1, mgx, mggot)
     mg_sent.start()
-    p_in.wait()
-    tile = 2 * LANES
-
-    @pl.loop(0, cols // tile)
+
+    @pl.loop(0, tiles)
     def _(n):
         span = pl.ds(pl.multiple_of(n * tile, tile), tile)
         upx[:, span] = dot(ucat[...], p[:, span])
 
-    away = pl.ds(pl.multiple_of(other * out_half, LANES), out_half)
-    kept = pl.ds(pl.multiple_of(me_m * out_half, LANES), out_half)
     up_sent = to_peer(2, upx.at[:, away], upgot)
     up_sent.start()
     mg_sent.wait_recv()
@@ -415,102 +421,155 @@
     mg_x = [to_seg(1, n, mgs.at[me_s], mgs.at[me_s]) for n in range(1, n_seg)]
     for copy in mg_x:
         copy.start()
-    up_sent.wait_recv()
-    upall[me_d] = (upx[:, kept] + upgot[...]).astype(bf16)
-
-    def u_copy(n):
-        return to_dp(1, n, upall.at[me_d], upall.at[me_d])
-
-    @pl.loop(1, n_dp)
-    def _(n):
-        u_copy(n).start()
-
-    @pl.loop(0, cols // tile)
-    def _(n):
-        span = pl.ds(pl.multiple_of(n * tile, tile), tile)
-        hpx[:, span] = dot(h[...], p[:, span])
-
-    hpsend[...] = hpx[:, away].astype(bf16)
-    hp_sent = to_peer(3, hpsend, hpgot)
-    hp_sent.start()
-    for copy in mg_x:
-        copy.wait_recv()
-    pair = n_seg // 2
-    mgall[me_m, me_d] = mgs[pl.ds(me_m * pair, pair)]
-
-    def m_copy(n):
-        return to_dp(2, n, mgall.at[me_m, me_d], mgall.at[me_m, me_d])
-
-    @pl.loop(1, n_dp)
-    def _(n):
-        m_copy(n).start()
-
-    @pl.loop(1, n_dp)
-    def _(n):
-        a_copy(n).wait_recv()
-
-    aall[me_s] = agot[:, :, :LANES].reshape(slots, LANES)
-    a_x = [to_seg(2, n, aall.at[me_s], aall.at[me_s]) for n in range(1, n_seg)]
-    for copy in a_x:
-        copy.start()
+
     hp_sent.wait_recv()
     hp = (hpx[:, kept] + hpgot[...].astype(f32)).astype(bf16)
     hslots[...] = dot(sel[...], hp).astype(bf16).reshape(hslots.shape)
     hgot[me_d] = hslots[me_d]
 
     def h_copy(n):
-        return to_dp(3, n, hslots.at[(me_d + n) % n_dp], hgot.at[me_d])
+        return to_dp(1, n, hslots.at[(me_d + n) % n_dp], hgot.at[me_d])
 
     @pl.loop(1, n_dp)
     def _(n):
         h_copy(n).start()
 
+    wide_a[:rows_u, :] = jnp.zeros((rows_u, 2 * LANES), f32)
+    wide_b[:rows_u, :] = jnp.zeros((rows_u, 2 * LANES), f32)
+
+    @pl.loop(0, n_seg)
+    def _(g):
+        span = pl.ds(pl.multiple_of(g * part, part), part)
+        here = h[:, span]
+        wide = here.astype(f32)
+        scaled = (wide * gain[:, span].astype(f32)).astype(bf16)
+        wide_a[:, :rank_all] += dot_nt(scaled, down[:, span])
+        wide_b[:, :rank_all] += dot_nt(here, up[:, span])
+        abx[:, LANES:] += jnp.broadcast_to(jnp.sum(wide * wide, axis=1, keepdims=True), (tok, LANES))
+
+    id_col = turned(ids[...].astype(f32))
+    lane2 = iota((tok, 2 * LANES), 1)
+    own = (lane2 >> 6).astype(f32) == jnp.concatenate([id_col, id_col], axis=1)
+    lane = iota((tok, LANES), 1)
+    abx[:, :LANES] = jnp.where(lane < RANK, fold(wide_a[...], own), fold(wide_b[...], own))
+    ab_sent = to_peer(0, abx, abgot)
+    ab_sent.start()
+
+    up_sent.wait_recv()
+    blocks[me_d, :, :out_half] = (upx[:, kept] + upgot[...]).astype(bf16)
+    for copy in mg_x:
+        copy.wait_recv()
+    for n in range(pair):
+        low = out_half + n * LANES
+        blocks[me_d, :, low : low + LANES] = mgs[me_m * pair + n]
+    firsts = [gather_first(n) for n in range(1, side)]
+    for copy in firsts:
+        copy.start()
+    seconds = [gather_second(0, n) for n in range(1, side)]
+    for copy in seconds:
+        copy.start()
+
+    ab_sent.wait_recv()
+    total = abx[...] + abgot[...]
+    sq = total[:, LANES:]
+    sq_hi = sq.astype(bf16).astype(f32)
+    extra = jnp.where(lane == 0, id_col, jnp.where(lane == 1, sq_hi, jnp.where(lane == 2, sq - sq_hi, 0.0)))
+    pay[:, :LANES] = total[:, :LANES].astype(bf16)
+    pay[:, LANES:] = extra.astype(bf16)
+    lanes_here = pl.ds(pl.multiple_of(me_m * LANES, LANES), LANES)
+    aslots[...] = dot(sel[...], pay[:, lanes_here]).astype(bf16).reshape(aslots.shape)
+    agot[me_m, me_d] = aslots[me_d]
+
+    def a_copy(n):
+        return to_dp(0, n, aslots.at[(me_d + n) % n_dp], agot.at[me_m, me_d])
+
+    @pl.loop(1, n_dp)
+    def _(n):
+        a_copy(n).start()
+
     x_in.wait()
-    chunk = 128
-
-    @pl.loop(0, slots // chunk)
-    def _(n):
-        span = pl.ds(pl.multiple_of(n * chunk, chunk), chunk)
-        wide = x[span, :].astype(f32)
-        sxx[span, :] = jnp.broadcast_to(jnp.sum(wide * wide, axis=1, keepdims=True), (chunk, LANES))
-        sg[span, :] = (wide * sgain[...]).astype(bf16)
+    sxx[...] = jnp.zeros(sxx.shape, f32)
+
+    @pl.loop(0, x.shape[1] // LANES)
+    def _(n):
+        span = pl.ds(pl.multiple_of(n * LANES, LANES), LANES)
+        wide = x[:, span].astype(f32)
+        sxx[...] += wide * wide
+        sg[:, span] = (wide * sgain[pl.ds(n, 1), :]).astype(bf16)
 
     sx_sent = to_peer(4, sxx, sxgot)
     sx_sent.start()
-    w_in.wait()
-
-    @pl.loop(0, cols // tile)
-    def _(n):
+    for k in range(1, side):
+        firsts[k - 1].wait_recv()
+        for n in range(1, side):
+            copy = gather_second(k, n)
+            copy.start()
+            seconds.append(copy)
+
+    def student(n):
         span = pl.ds(pl.multiple_of(n * tile, tile), tile)
+        w_copy(n).wait()
         sox[:, span] = dot(sg[...], w[:, span])
 
+    pl.loop(0, tiles // 2)(student)
+
+    @pl.loop(1, n_dp)
+    def _(n):
+        a_copy(n).wait_recv()
+
+    a_x = [to_seg(2, n, aall.at[me_s], aall.at[me_s]) for n in range(1, n_seg)]
+    extra_swap = to_peer(6, agot.at[1], agot.at[1])
+
+    @pl.when(me_m == 0)
+    def _():
+        aall[me_s] = agot[0].reshape(slots, LANES)
+        for copy in a_x:
+            copy.start()
+
+    @pl.when(me_m == 1)
+    def _():
+        extra_swap.start()
+
+    pl.loop(tiles // 2, tiles)(student)
     sosend[...] = sox[:, away].astype(bf16)
     so_sent = to_peer(5, sosend, sogot)
     so_sent.start()
-
-    @pl.loop(0, x.shape[1] // chunk)
-    def _(n):
-        span = pl.ds(pl.multiple_of(n * chunk, chunk), chunk)
+    a_swap = to_peer(7, aall, aall)
+
+    @pl.when(me_m == 0)
+    def _():
+        for copy in a_x:
+            copy.wait_recv()
+        a_swap.start()
+
+    @pl.loop(0, x.shape[1] // LANES)
+    def _(n):
+        span = pl.ds(pl.multiple_of(n * LANES, LANES), LANES)
         sgt_out[span, :] = sg[:, span].T
 
+    for copy in seconds:
+        copy.wait_recv()
+    tables[me_m] = blocks[:, :, out_half:]
+    table_swap = to_peer(8, tables.at[me_m], tables.at[me_m])
+    table_swap.start()
+
+    @pl.when(me_m == 0)
+    def _():
+        extra_swap.wait_recv()
+
+    @pl.when(me_m == 1)
+    def _():
+        a_swap.wait_recv()
+
     xmap_in.wait()
-
-    @pl.loop(1, n_dp)
-    def _(n):
-        m_copy(n).wait_recv()
-
-    mg_swap = to_peer(6, mgall.at[me_m], mgall.at[me_m])
-    mg_swap.start()
-    extra = agot[:, :, LANES:].reshape(slots, LANES).astype(f32)
+    extra = agot[1].reshape(slots, LANES).astype(f32)
     id_slot = extra[:, 0:1]
     norm = extra[:, 1:2] + extra[:, 2:3]
     keep = kcol[...] == id_slot
     lane = iota((slots, LANES), 1)
-    for copy in a_x:
-        copy.wait_recv()
-    mg_swap.wait_recv()
     known = rows_u * n_dp
     both = jnp.zeros((slots, LANES), f32)
+    table_swap.wait_recv()
     for s in range(n_seg):
         ab = aall[s].astype(f32)
         lat = (ab + both) * lax.rsqrt(jnp.maximum(norm, 0.0) * (1.0 / D) + 1e-06)
@@ -522,8 +581,9 @@
         else:
             ctil[...] += wide_c
         if s + 1 < n_seg:
-            here = mgall[s // pair, :, s % pair].reshape(known, LANES)
-            after = mgall[(s + 1) // pair, :, (s + 1) % pair].reshape(known, LANES)
+            low, high = (s % pair) * LANES, ((s + 1) % pair) * LANES
+            here = tables[s // pair, :, :, low : low + LANES].reshape(known, LANES)
+            after = tables[(s + 1) // pair, :, :, high : high + LANES].reshape(known, LANES)
             self_part = dot(ctil[...], here)
             lat_high = pltpu.roll(lat_low, RANK, 1)
             norm = norm + jnp.sum(lat_high * (2.0 * ab + both + self_part), axis=1, keepdims=True)
@@ -531,19 +591,19 @@
 
     @pl.loop(1, n_dp)
     def _(n):
-        u_copy(n).wait_recv()
         h_copy(n).wait_recv()
 
     sx_sent.wait_recv()
     so_sent.wait_recv()
-    table = upall[...].reshape(known, out_half)
+    table = blocks[:, :, :out_half].reshape(known, out_half)
     slot = iota((slots, n_dp), 0)
     source = iota((slots, n_dp), 1)
     room = slot - source * cap
     valid = jnp.sum(
         jnp.where((room >= 0) & (room < cap) & (room < counts[...]), 1.0, 0.0), axis=1, keepdims=True
     )
-    recip = lax.rsqrt((sxx[:, 0:1] + sxgot[:, 0:1]) * (1.0 / S) + 1e-06)
+    square = jnp.sum(sxx[...] + sxgot[...], axis=1, keepdims=True)
+    recip = lax.rsqrt(square * (1.0 / S) + 1e-06)
     target = dot(ctil[...], table) + hgot[...].reshape(slots, out_half).astype(f32)
     out = (sox[:, kept] + sogot[...].astype(f32)) * recip
     diff = jnp.where(valid > 0.0, out - target, 0.0)
@@ -551,18 +611,26 @@
     loss_out[...] = jnp.broadcast_to(loss, (slots, LANES)).T[0:1, :]
     gd_out[...] = (diff * (recip * (1.0 / TOK_DEV))).astype(bf16)
 
-    for copy in u_sent + mg_x + a_x + [ab_sent, mg_sent, up_sent, hp_sent, sx_sent, so_sent, mg_swap]:
+    for copy in u_sent + mg_x + firsts + seconds + [ab_sent, mg_sent, up_sent, hp_sent, sx_sent, so_sent, table_swap]:
         copy.wait_send()
 
+    @pl.when(me_m == 0)
+    def _():
+        for copy in a_x + [a_swap]:
+            copy.wait_send()
+
+    @pl.when(me_m == 1)
+    def _():
+        extra_swap.wait_send()
+
     @pl.loop(1, n_dp)
     def _(n):
         a_copy(n).wait_send()
-        u_copy(n).wait_send()
-        m_copy(n).wait_send()
         h_copy(n).wait_send()
 
 
 def front(h, ids, dest, counts, gain, down, up, x, sgain, w, p):
+    side = 4
     n_seg = lax.axis_size("segment")
     n_dp = lax.axis_size("dp")
     tok, half = h.shape
@@ -589,18 +657,18 @@
         ((rows_u, half // n_seg), bf16), ((n_seg, rows_u, half // n_seg), bf16), ((rows_u, half), bf16),
         ((tok, 2 * LANES), f32), ((tok, 2 * LANES), f32), ((tok, 2 * LANES), f32), ((tok, 2 * LANES), f32),
         ((slots, tok), bf16), ((tok, 2 * LANES), bf16),
-        ((n_dp, cap, 2 * LANES), bf16), ((n_dp, cap, 2 * LANES), bf16), ((n_seg, slots, LANES), bf16),
+        ((n_dp, cap, LANES), bf16), ((2, n_dp, cap, LANES), bf16), ((n_seg, slots, LANES), bf16),
         ((rows_u, LANES), f32), ((rows_u, LANES), f32), ((n_seg, rows_u, LANES), bf16),
-        ((2, n_dp, n_seg // 2, rows_u, LANES), bf16),
-        ((rows_u, cols), f32), ((rows_u, out_half), f32), ((n_dp, rows_u, out_half), bf16),
+        ((rows_u, cols), f32), ((rows_u, out_half), f32),
+        ((n_dp, rows_u, out_half + n_seg // 2 * LANES), bf16), ((2, n_dp, rows_u, n_seg // 2 * LANES), bf16),
         ((tok, cols), f32), ((tok, out_half), bf16), ((tok, out_half), bf16),
         ((n_dp, cap, out_half), bf16), ((n_dp, cap, out_half), bf16),
         (x.shape, bf16), ((slots, cols), f32), ((slots, out_half), bf16), ((slots, out_half), bf16),
         ((slots, LANES), f32), ((slots, LANES), f32), ((slots, known), bf16),
     ]
-    sems = [7, 7, 7, 3 * (n_seg - 1), 3 * (n_seg - 1), 4 * (n_dp - 1), 4 * (n_dp - 1)]
+    sems = [5 + cols // LANES, 9, 9, 3 * (n_seg - 1), 3 * (n_seg - 1), 3 * (n_dp - 1), 3 * (n_dp - 1)]
     return pl.pallas_call(
-        functools.partial(front_kernel, n_seg, n_dp, cap),
+        functools.partial(front_kernel, n_seg, side, cap),
         out_shape=(
             jax.ShapeDtypeStruct((slots, out_half), bf16),
             jax.ShapeDtypeStruct((1, slots), f32),
@@ -615,7 +683,7 @@
         cost_estimate=pl.CostEstimate(flops=flops, bytes_accessed=25 * 2**20, transcendentals=0),
     )(
         h, down, up, x, w, p, xmap,
-        ids.reshape(1, tok), dest.reshape(1, tok), counts, gain, sgain.reshape(1, width), kcol,
+        ids.reshape(1, tok), dest.reshape(1, tok), counts, gain, sgain.reshape(width // LANES, LANES), kcol,
     )
 
 
@@ -638,7 +706,7 @@
         destination,
         row_counts,
         section_gain,
-        adapter_down[0],
+        adapter_down[0].T,
         adapter_up[0],
         student_in,
         student_gain,

time: 107 us -> 105 us (0.981)
  local copies, waits for them, and re-layouts: 8.48 us -> 3.34 us
  Pallas kernels: 97.3 us -> 101 us
    unnamed x3 -> x2, local copies, waits for them, and re-layouts: 7.17 us -> 3.34 us
    pallas_call x1, Pallas kernels: 50 us -> 52.8 us  [front(): pl.pallas_call(functools.partial(front_kernel, n_seg, side, cap), out_sha...]
    reshape x1 -> x0, local copies, waits for them, and re-layouts: 1.31 us -> none  [front(): sgain.reshape(1, width)]
where the time goes in v4:
time: 105 us
  Pallas kernels  101 us (96%)
  local copies, waits for them, and re-layouts  3.34 us (3%)
    pallas_call x1, Pallas kernels, front(): pl.pallas_call(functools.partial(front_kernel, n_seg, side, cap), out_sha...  52.8 us
    pallas_call x1, Pallas kernels, back(): pl.pallas_call(functools.partial(back_kernel, n_seg, side), out_shape=(ja...  48.2 us
    unnamed x2, local copies, waits for them, and re-layouts  3.34 us

profile of v4, /device:TPU:1, one launch (start us, length us, event | category | flops | bytes accessed | tf_op | source)
XLA Modules:
  0.0 105.0 jit_solution(11193104926692919760)
XLA Ops:
  0.6 52.8 %shard_map.140 = (bf16[512,640]{1,0:T(8,128)(2,1)}, f32[1,512]{1,0:T(1,128)}, bf16[2560,512]{1,0:T(8,128)(2,1)}) custom-call(bf16[256,4096]{1,0:T(8,128)(2,1)} %h_hbm.1, bf16[192,4096]{1,0:T(8,128)(2,1)} %bitcast.9, bf16[192,4096]{1,0:T(8,128)(2,1)} %bitcast.10, bf16[512,2560]{1,0:T(8,128)(2,1)} %x_hbm.1, bf16[2560,1280]{1,0:T(8,128)(2,1)} %w_hbm.1, ...), custom_call_target="tpu_custom_call" | custom-call | flops 6039797760 | bytes 26214400 | tf_op jit(solution)/shard_map/pallas_call | solution.py:670
  53.5 48.2 %shard_map.141 = (f32[160,1280]{1,0:T(8,128)}, f32[1,512]{1,0:T(1,128)}) custom-call(bf16[2560,512]{1,0:T(8,128)(2,1)} %get-tuple-element.7.sgt, bf16[512,640]{1,0:T(8,128)(2,1)} %get-tuple-element.8.gdh, f32[1,512]{1,0:T(1,128)} %get-tuple-element.9.loss), custom_call_target="tpu_custom_call" | custom-call | flops 3355443200 | bytes 8388608 | tf_op jit(solution)/shard_map/pallas_call | solution.py:207
  101.6 2.1 %copy.17 = f32[1,160,1280]{2,1,0:T(8,128)} copy(f32[1,160,1280]{2,1,0:T(8,128)} %bitcast.11) | data formatting | bytes 1638400
  103.7 1.3 %copy.18 = f32[512]{0:T(512)} copy(f32[512]{0:T(512)} %bitcast.13) | data formatting | bytes 4096

commit v5 on v4

v5 whole, which is shorter than its diff:
```python
import functools

import jax
import jax.numpy as jnp
import numpy as np
from jax import lax
from jax.experimental import pallas as pl
from jax.experimental.pallas import tpu as pltpu
from jax.sharding import PartitionSpec as P

D = 8192
S = 5120
RANK = 64
TOK_DEV = 256
TEACH = 3
LANES = 128
bf16 = jnp.bfloat16
f32 = jnp.float32


def dot(a, b):
    return jnp.dot(a, b, preferred_element_type=f32)


def remote(src, dst, send, recv, **where):
    return pltpu.make_async_remote_copy(
        src_ref=src,
        dst_ref=dst,
        send_sem=send,
        recv_sem=recv,
        device_id=where,
        device_id_type=pl.DeviceIdType.MESH,
    )


def iota(shape, dim):
    return lax.broadcasted_iota(jnp.int32, shape, dim)


def ones_where(mask):
    return jnp.where(mask, 1.0, 0.0).astype(bf16)


def dot_nt(a, b):
    return lax.dot_general(a, b, (((1,), (1,)), ((), ())), preferred_element_type=f32)


def turned(row):
    return jnp.broadcast_to(row, (LANES, row.shape[1])).T


def fold(wide, keep):
    kept = jnp.where(keep, wide, 0.0)
    both = kept[:, :LANES] + kept[:, LANES:]
    return both + pltpu.roll(both, RANK, 1)


def step_kernel(
    n_seg, side, cap,
    h_hbm, down_hbm, up_hbm, x_hbm, w_hbm, p_hbm, xmap_hbm,
    ids, dest, counts, gain, sgain, kcol,
    out, loss_out,
    h, down, up, x, w, p, xmap,
    usend, ugot, ucat, wide_a, wide_b, abx, abgot, sel, pay, aslots, agot, aall,
    mgx, mggot, mgs, upx, upgot, blocks, tables,
    hpx, hpsend, hpgot, hslots, hgot,
    sg, sox, sosend, sogot, sxx, sxgot, ctil,
    sgt, gd, held, part2, got2, losspart, lossgot, losses,
    lsem, s_m, r_m, s_x, r_x, s_d, r_d, s_r, r_r,
):
    me_s = lax.axis_index("segment")
    me_m = lax.axis_index("mp")
    me_d = lax.axis_index("dp")
    other = 1 - me_m
    n_dp = side * side
    tok, half = h.shape
    slots = x.shape[0]
    cols = p.shape[1]
    out_half = cols // 2
    rows_u = mgx.shape[0]
    per = rows_u // n_seg
    part = half // n_seg
    tile = 2 * LANES
    tiles = cols // tile
    pair = n_seg // 2

    def load(n, src, dst):
        copy = pltpu.make_async_copy(src, dst, lsem.at[n])
        copy.start()
        return copy

    def p_copy(n):
        span = pl.ds(pl.multiple_of(n * tile, tile), tile)
        return pltpu.make_async_copy(p_hbm.at[:, span], p.at[:, span], lsem.at[5 + n])

    def w_copy(n):
        span = pl.ds(pl.multiple_of(n * tile, tile), tile)
        return pltpu.make_async_copy(w_hbm.at[:, span], w.at[:, span], lsem.at[5 + tiles + n])

    up_in = load(0, up_hbm, up)
    h_in = load(1, h_hbm, h)
    for n in range(tiles):
        p_copy(n).start()
    down_in = load(2, down_hbm, down)
    x_in = load(3, x_hbm, x)
    for n in range(tiles):
        w_copy(n).start()
    xmap_in = load(4, xmap_hbm, xmap)

    barrier = pltpu.get_barrier_semaphore()
    mesh_id = pl.DeviceIdType.MESH
    pl.semaphore_signal(barrier, inc=1, device_id={"mp": other}, device_id_type=mesh_id)
    for n in range(1, n_seg):
        pl.semaphore_signal(barrier, inc=1, device_id={"segment": (me_s + n) % n_seg}, device_id_type=mesh_id)

    @pl.loop(1, n_dp)
    def _(n):
        pl.semaphore_signal(barrier, inc=1, device_id={"dp": (me_d + n) % n_dp}, device_id_type=mesh_id)

    def to_peer(n, src, dst):
        return remote(src, dst, s_m.at[n], r_m.at[n], mp=other)

    def to_seg(kind, n, src, dst):
        number = kind * (n_seg - 1) + n - 1
        return remote(src, dst, s_x.at[number], r_x.at[number], segment=(me_s + n) % n_seg)

    def to_dp(kind, n, src, dst):
        number = kind * (n_dp - 1) + n - 1
        return remote(src, dst, s_d.at[number], r_d.at[number], dp=(me_d + n) % n_dp)

    z = me_d // side
    y = me_d % side

    def place(first, second):
        a = ((z * other + y * me_m) + second) % side
        b = ((y * other + z * me_m) + first) % side
        return (a * other + b * me_m) * side + b * other + a * me_m

    def gather_first(n):
        return remote(blocks.at[me_d], blocks.at[me_d], s_d.at[n + 29], r_d.at[n + 29], dp=place(n, 0))

    def gather_second(k, n):
        source = place(side - k, 0)
        number = 33 + k * (side - 1) + n - 1
        return remote(blocks.at[source], blocks.at[source], s_d.at[number], r_d.at[number], dp=place(0, n))

    packed = n_seg * per
    row = iota((packed, up.shape[0]), 0)
    col = iota((packed, up.shape[0]), 1)
    quad = row >> 2
    block = (quad >= 3).astype(jnp.int32) + (quad >= 6).astype(jnp.int32) + (quad >= 9).astype(jnp.int32)
    teacher = quad - 3 * block
    hit = ((col >> 6) == teacher) & (((col & 63) >> 2) == me_d) & ((col & 3) == (row & 3))
    up_in.wait()
    mine = jnp.zeros((packed, part), f32)
    for g in range(n_seg):
        mine = mine + dot(ones_where(hit & (block == g)), up[:, g * part : (g + 1) * part])
    usend[...] = mine.astype(bf16)
    ugot[me_s] = usend[...]
    dest_f = dest[...].astype(f32)
    onehot = jnp.where(iota((n_dp, tok), 0).astype(f32) == dest_f, 1.0, 0.0)
    before = ones_where(iota((tok, tok), 0) < iota((tok, tok), 1))
    earlier = dot(onehot.astype(bf16), before)
    position = dest_f * cap + jnp.sum(earlier * onehot, axis=0, keepdims=True)
    sel[...] = ones_where(iota((slots, tok), 0).astype(f32) == position)
    wide_a[...] = jnp.zeros(wide_a.shape, f32)
    wide_b[...] = jnp.zeros(wide_b.shape, f32)
    abx[...] = jnp.zeros(abx.shape, f32)

    pl.semaphore_wait(barrier, 1 + (n_seg - 1) + (n_dp - 1))
    u_sent = [to_seg(0, n, usend, ugot.at[me_s]) for n in range(1, n_seg)]
    for copy in u_sent:
        copy.start()

    away = pl.ds(pl.multiple_of(other * out_half, LANES), out_half)
    kept = pl.ds(pl.multiple_of(me_m * out_half, LANES), out_half)
    h_in.wait()

    @pl.loop(0, tiles)
    def _(n):
        span = pl.ds(pl.multiple_of(n * tile, tile), tile)
        p_copy(n).wait()
        hpx[:, span] = dot(h[...], p[:, span])

    hpsend[...] = hpx[:, away].astype(bf16)
    hp_sent = to_peer(3, hpsend, hpgot)
    hp_sent.start()

    down_in.wait()
    rank_all = down.shape[0]

    @pl.loop(0, n_seg)
    def _(g):
        span = pl.ds(pl.multiple_of(g * part, part), part)
        here = h[:, span]
        wide = here.astype(f32)
        scaled = (wide * gain[:, span].astype(f32)).astype(bf16)
        wide_a[:, :rank_all] += dot_nt(scaled, down[:, span])
        wide_b[:, :rank_all] += dot_nt(here, up[:, span])
        abx[:, LANES:] += jnp.broadcast_to(jnp.sum(wide * wide, axis=1, keepdims=True), (tok, LANES))

    id_col = turned(ids[...].astype(f32))
    lane2 = iota((tok, 2 * LANES), 1)
    own = (lane2 >> 6).astype(f32) == jnp.concatenate([id_col, id_col], axis=1)
    lane = iota((tok, LANES), 1)
    abx[:, :LANES] = jnp.where(lane < RANK, fold(wide_a[...], own), fold(wide_b[...], own))
    ab_sent = to_peer(0, abx, abgot)
    ab_sent.start()

    hp_sent.wait_recv()
    hp = (hpx[:, kept] + hpgot[...].astype(f32)).astype(bf16)
    hslots[...] = dot(sel[...], hp).astype(bf16).reshape(hslots.shape)
    hgot[me_d] = hslots[me_d]

    def h_copy(n):
        return to_dp(1, n, hslots.at[(me_d + n) % n_dp], hgot.at[me_d])

    @pl.loop(1, n_dp)
    def _(n):
        h_copy(n).start()

    for copy in u_sent:
        copy.wait_recv()
    row = iota((packed, n_seg * packed), 0)
    col = iota((packed, n_seg * packed), 1)
    quad = row >> 2
    block = (quad >= 3).astype(jnp.int32) + (quad >= 6).astype(jnp.int32) + (quad >= 9).astype(jnp.int32)
    got_u = ugot[...].reshape(n_seg * packed, part)
    for g in range(n_seg):
        take = ones_where(col == row + (packed - per) * block + per * g)
        ucat[:, g * part : (g + 1) * part] = dot(take, got_u).astype(bf16)
    u = ucat[...]
    u_scaled = (u.astype(f32) * gain[...].astype(f32)).astype(bf16)
    wide_a[:rows_u, :rank_all] = dot_nt(u_scaled, down[...])
    wide_b[:rows_u, :rank_all] = dot_nt(u, up[...])
    row = iota((rows_u, 2 * LANES), 0)
    quad = row >> 2
    block = (quad >= 3).astype(jnp.int32) + (quad >= 6).astype(jnp.int32) + (quad >= 9).astype(jnp.int32)
    same = (quad - 3 * block) == (iota((rows_u, 2 * LANES), 1) >> 6)
    lane_u = iota((rows_u, LANES), 1)
    mgx[...] = jnp.where(lane_u < RANK, fold(wide_a[:rows_u, :], same), fold(wide_b[:rows_u, :], same))
    mg_sent = to_peer(1, mgx, mggot)
    mg_sent.start()

    ab_sent.wait_recv()
    total = abx[...] + abgot[...]
    sq = total[:, LANES:]
    sq_hi = sq.astype(bf16).astype(f32)
    extra = jnp.where(lane == 0, id_col, jnp.where(lane == 1, sq_hi, jnp.where(lane == 2, sq - sq_hi, 0.0)))
    pay[:, :LANES] = total[:, :LANES].astype(bf16)
    pay[:, LANES:] = extra.astype(bf16)
    lanes_here = pl.ds(pl.multiple_of(me_m * LANES, LANES), LANES)
    aslots[...] = dot(sel[...], pay[:, lanes_here]).astype(bf16).reshape(aslots.shape)
    agot[me_m, me_d] = aslots[me_d]

    def a_copy(n):
        return to_dp(0, n, aslots.at[(me_d + n) % n_dp], agot.at[me_m, me_d])

    @pl.loop(1, n_dp)
    def _(n):
        a_copy(n).start()

    mg_sent.wait_recv()
    mgs[me_s] = (mgx[...] + mggot[...]).astype(bf16)
    mg_x = [to_seg(1, n, mgs.at[me_s], mgs.at[me_s]) for n in range(1, n_seg)]
    for copy in mg_x:
        copy.start()

    @pl.loop(0, tiles)
    def _(n):
        span = pl.ds(pl.multiple_of(n * tile, tile), tile)
        upx[:, span] = dot(ucat[...], p[:, span])

    up_sent = to_peer(2, upx.at[:, away], upgot)
    up_sent.start()
    x_in.wait()
    sxx[...] = jnp.zeros(sxx.shape, f32)

    @pl.loop(0, x.shape[1] // LANES)
    def _(n):
        span = pl.ds(pl.multiple_of(n * LANES, LANES), LANES)
        wide = x[:, span].astype(f32)
        sxx[...] += wide * wide
        sg[:, span] = (wide * sgain[pl.ds(n, 1), :]).astype(bf16)

    sx_sent = to_peer(4, sxx, sxgot)
    sx_sent.start()
    up_sent.wait_recv()
    blocks[me_d, :, :out_half] = (upx[:, kept] + upgot[...]).astype(bf16)
    for copy in mg_x:
        copy.wait_recv()
    for n in range(pair):
        low = out_half + n * LANES
        blocks[me_d, :, low : low + LANES] = mgs[me_m * pair + n]
    firsts = [gather_first(n) for n in range(1, side)]
    for copy in firsts:
        copy.start()
    seconds = [gather_second(0, n) for n in range(1, side)]
    for copy in seconds:
        copy.start()

    def student(n):
        span = pl.ds(pl.multiple_of(n * tile, tile), tile)
        w_copy(n).wait()
        sox[:, span] = dot(sg[...], w[:, span])

    pl.loop(0, 2)(student)

    @pl.loop(1, n_dp)
    def _(n):
        a_copy(n).wait_recv()

    a_x = [to_seg(2, n, aall.at[me_s], aall.at[me_s]) for n in range(1, n_seg)]
    extra_swap = to_peer(6, agot.at[1], agot.at[1])

    @pl.when(me_m == 0)
    def _():
        aall[me_s] = agot[0].reshape(slots, LANES)
        for copy in a_x:
            copy.start()

    @pl.when(me_m == 1)
    def _():
        extra_swap.start()

    pl.loop(2, 3)(student)
    for k in range(1, side):
        firsts[k - 1].wait_recv()
        for n in range(1, side):
            copy = gather_second(k, n)
            copy.start()
            seconds.append(copy)


    pl.loop(3, tiles)(student)
    sosend[...] = sox[:, away].astype(bf16)
    so_sent = to_peer(5, sosend, sogot)
    so_sent.start()
    a_swap = to_peer(7, aall, aall)

    @pl.when(me_m == 0)
    def _():
        for copy in a_x:
            copy.wait_recv()
        a_swap.start()

    @pl.loop(0, x.shape[1] // LANES)
    def _(n):
        span = pl.ds(pl.multiple_of(n * LANES, LANES), LANES)
        sgt[span, :] = sg[:, span].T

    for copy in seconds:
        copy.wait_recv()
    tables[me_m] = blocks[:, :, out_half:]
    table_swap = to_peer(8, tables.at[me_m], tables.at[me_m])
    table_swap.start()

    @pl.when(me_m == 0)
    def _():
        extra_swap.wait_recv()

    @pl.when(me_m == 1)
    def _():
        a_swap.wait_recv()

    xmap_in.wait()
    extra = agot[1].reshape(slots, LANES).astype(f32)
    id_slot = extra[:, 0:1]
    norm = extra[:, 1:2] + extra[:, 2:3]
    keep = kcol[...] == id_slot
    lane = iota((slots, LANES), 1)
    known = rows_u * n_dp
    both = jnp.zeros((slots, LANES), f32)
    table_swap.wait_recv()
    for s in range(n_seg):
        ab = aall[s].astype(f32)
        lat = (ab + both) * lax.rsqrt(jnp.maximum(norm, 0.0) * (1.0 / D) + 1e-06)
        lat = lat.astype(bf16)
        lat_low = jnp.where(lane < RANK, lat.astype(f32), 0.0)
        wide_c = jnp.where(keep, dot(lat_low.astype(bf16), xmap[s]), 0.0).astype(bf16)
        if s == 0:
            ctil[...] = wide_c
        else:
            ctil[...] += wide_c
        if s + 1 < n_seg:
            low, high = (s % pair) * LANES, ((s + 1) % pair) * LANES
            here = tables[s // pair, :, :, low : low + LANES].reshape(known, LANES)
            after = tables[(s + 1) // pair, :, :, high : high + LANES].reshape(known, LANES)
            self_part = dot(ctil[...], here)
            lat_high = pltpu.roll(lat_low, RANK, 1)
            norm = norm + jnp.sum(lat_high * (2.0 * ab + both + self_part), axis=1, keepdims=True)
            both = dot(ctil[...], after)

    @pl.loop(1, n_dp)
    def _(n):
        h_copy(n).wait_recv()

    sx_sent.wait_recv()
    so_sent.wait_recv()
    table = blocks[:, :, :out_half].reshape(known, out_half)
    slot = iota((slots, n_dp), 0)
    source = iota((slots, n_dp), 1)
    room = slot - source * cap
    valid = jnp.sum(
        jnp.where((room >= 0) & (room < cap) & (room < counts[...]), 1.0, 0.0), axis=1, keepdims=True
    )
    square = jnp.sum(sxx[...] + sxgot[...], axis=1, keepdims=True)
    recip = lax.rsqrt(square * (1.0 / S) + 1e-06)
    target = dot(ctil[...], table) + hgot[...].reshape(slots, out_half).astype(f32)
    student_out = (sox[:, kept] + sogot[...].astype(f32)) * recip
    diff = jnp.where(valid > 0.0, student_out - target, 0.0)
    loss = jnp.sum(diff * diff, axis=1, keepdims=True)
    gd[me_m] = (diff * (recip * (1.0 / TOK_DEV))).astype(bf16)
    gd_swap = to_peer(9, gd.at[me_m], gd.at[me_m])
    gd_swap.start()
    losspart[...] = jnp.broadcast_to(loss, (slots, LANES)).T[0:1, :]
    loss_swap = to_peer(10, losspart, lossgot)
    loss_swap.start()

    share = out.shape[0]
    edge = share // 2
    wide_out = gd.shape[2]

    def step(way):
        return 1 + way * (side - 2)

    def ring(f, way):
        ahead = step(way)
        return (1 - f) * (z * side + (y + ahead) % side) + f * (((z + ahead) % side) * side + y)

    def product(f, ahead, mid, b):
        first = ((1 - f) * y + f * z + ahead) % side
        second = ((1 - f) * z + f * y + (1 - mid) * (2 - 2 * b) + mid * (1 + 2 * b)) % side
        owner = (1 - f) * (second * side + first) + f * (first * side + second)
        return jnp.dot(
            sgt[pl.ds(pl.multiple_of(owner * share, share), share), :], gd[f], preferred_element_type=f32
        )

    def sent(f, slot, row, count):
        low = pl.multiple_of(((f * 3 + slot) * 4 + row) * share, share)
        return p.at[pl.ds(low, count * share), wide_out:]

    def landed(f, way, row, count):
        low = pl.multiple_of(((f * 2 + way) * 6 + row) * share, share)
        return p.at[pl.ds(low, count * share), :wide_out]

    def first_copy(f, way, msg):
        number = (f * 2 + way) * 4 + msg
        if msg == 0:
            src, dst = sent(f, 0, 2 * way, 2), landed(f, way, 0, 2)
        elif msg == 1:
            src, dst = sent(f, 1 + way, 2 - 2 * way, 2), landed(f, way, 2, 2)
        else:
            src, dst = sent(f, 1 + way, 2 * way + msg - 2, 1), landed(f, way, 2 + msg, 1)
        return remote(src, dst, s_r.at[number], r_r.at[number], dp=ring(f, way))

    def second_copy(f, way, msg):
        number = 16 + (f * 2 + way) * 3 + msg
        slot = 0 if msg == 0 else 1 + way
        low = (1 - way) * edge if msg == 1 else way * edge
        src = part2.at[f, slot, pl.ds(pl.multiple_of(low, edge), edge)]
        return remote(src, got2.at[f, way, msg], s_r.at[number], r_r.at[number], dp=ring(1 - f, way))

    def flow(n):
        return me_m + n * (1 - 2 * me_m)

    for n in range(2):
        if n == 1:
            gd_swap.wait_recv()

        @pl.loop(0, 2)
        def _(way):
            @pl.loop(0, 2)
            def _(b):
                sent(flow(n), 0, 2 * way + b, 1)[...] = product(flow(n), 2, way, b).astype(bf16)

            first_copy(flow(n), way, 0).start()

    @pl.loop(0, 2)
    def _(n):
        @pl.loop(0, 2)
        def _(way):
            @pl.loop(0, 2)
            def _(b):
                blk = product(flow(n), step(way), 1 - way, b)
                sent(flow(n), 1 + way, 2 - 2 * way + b, 1)[...] = blk.astype(bf16)

            first_copy(flow(n), way, 1).start()

    loss_swap.wait_recv()
    losses[me_s] = losspart[...] + lossgot[...]
    tells = [to_seg(3, n, losses.at[me_s], losses.at[me_s]) for n in range(1, n_seg)]
    for copy in tells:
        copy.start()

    @pl.loop(0, 2)
    def _(n):
        @pl.loop(0, 2)
        def _(mid):
            @pl.loop(0, 2)
            def _(b):
                held[flow(n), 2 * mid + b] = product(flow(n), 0, mid, b)

    for b in range(2):

        @pl.loop(0, 2)
        def _(n):
            @pl.loop(0, 2)
            def _(way):
                f = flow(n)
                if b == 0:
                    first_copy(f, way, 0).wait_recv()
                blk = product(f, step(way), way, b) + landed(f, way, b, 1)[...].astype(f32)
                sent(f, 1 + way, 2 * way + b, 1)[...] = blk.astype(bf16)
                first_copy(f, way, 2 + b).start()

    for copy in tells:
        copy.wait_recv()
    total = losses[0]
    for n in range(1, n_seg):
        total = total + losses[n]
    loss_out[...] = total * (1.0 / S)

    @pl.loop(0, 2)
    def _(n):
        f = flow(n)

        @pl.loop(0, 2)
        def _(way):
            first_copy(f, way, 1).wait_recv()
            for b in range(2):
                held[f, 2 - 2 * way + b] += landed(f, way, 2 + b, 1)[...].astype(f32)

    for b in range(2):

        @pl.loop(0, 2)
        def _(n):
            f = flow(n)

            @pl.loop(0, 2)
            def _(way):
                first_copy(f, way, 2 + b).wait_recv()
                held[f, 2 * way + b] += landed(f, way, 4 + b, 1)[...].astype(f32)

            if b == 0:
                part2[f, 0] = held[f, 0].astype(bf16)
                for way in range(2):
                    second_copy(f, way, 0).start()
                part2[f, 1, edge:] = held[f, 2, edge:].astype(bf16)
                second_copy(f, 0, 1).start()
            else:
                part2[f, 2, :edge] = held[f, 3, :edge].astype(bf16)
                second_copy(f, 1, 1).start()

    @pl.loop(0, 2)
    def _(n):
        f = flow(n)
        for way in range(2):
            second_copy(f, way, 0).wait_recv()
            rows = slice(way * edge, (way + 1) * edge)
            part2[f, 1 + way, rows] = (held[f, 2 + way, rows] + got2[f, way, 0].astype(f32)).astype(bf16)
            second_copy(f, way, 2).start()

    @pl.loop(0, 2)
    def _(n):
        f = flow(n)
        for msg in (1, 2):
            for way in range(2):
                second_copy(f, way, msg).wait_recv()
        span = pl.ds(pl.multiple_of(f * wide_out, LANES), wide_out)
        out[:edge, span] = held[f, 1, :edge] + got2[f, 0, 2].astype(f32) + got2[f, 1, 1].astype(f32)
        out[edge:, span] = held[f, 1, edge:] + got2[f, 0, 1].astype(f32) + got2[f, 1, 2].astype(f32)

    @pl.loop(0, 2)
    def _(f):
        @pl.loop(0, 2)
        def _(way):
            for msg in range(4):
                first_copy(f, way, msg).wait_send()

        for way in range(2):
            for msg in range(3):
                second_copy(f, way, msg).wait_send()

    for copy in u_sent + mg_x + firsts + seconds + [ab_sent, mg_sent, up_sent, hp_sent, sx_sent, so_sent, table_swap, gd_swap, loss_swap] + tells:
        copy.wait_send()

    @pl.when(me_m == 0)
    def _():
        for copy in a_x + [a_swap]:
            copy.wait_send()

    @pl.when(me_m == 1)
    def _():
        extra_swap.wait_send()

    @pl.loop(1, n_dp)
    def _(n):
        a_copy(n).wait_send()
        h_copy(n).wait_send()


def run_step(h, ids, dest, counts, gain, down, up, x, sgain, w, p):
    side = 4
    n_seg = lax.axis_size("segment")
    n_dp = lax.axis_size("dp")
    tok, half = h.shape
    slots, width = x.shape
    cols = p.shape[1]
    out_half = cols // 2
    cap = slots // n_dp
    q = RANK // n_dp
    per = TEACH * q
    rows_u = n_seg * per
    known = rows_u * n_dp
    share = width // n_dp
    c = np.arange(known)
    c_i, c_t, c_k, c_q = c // rows_u, c % rows_u // per, c % per // q, c % q
    spot = np.arange(LANES)[None, :, None]
    xmap = (np.arange(n_seg)[:, None, None] == c_t) & (spot == c_i * q + c_q)
    xmap = jnp.asarray(xmap.astype(np.float32), dtype=bf16)
    kcol = jnp.asarray(c_k[None, :].astype(np.float32))
    vmem = pl.BlockSpec(memory_space=pltpu.VMEM)
    hbm = pl.BlockSpec(memory_space=pl.ANY)
    flops = 2 * (tok * half * cols + 2 * slots * width * cols)
    scratch = [
        (h.shape, bf16), (down.shape, bf16), (up.shape, bf16), (x.shape, bf16), (w.shape, bf16), (p.shape, bf16),
        (xmap.shape, bf16),
        ((rows_u, half // n_seg), bf16), ((n_seg, rows_u, half // n_seg), bf16), ((rows_u, half), bf16),
        ((tok, 2 * LANES), f32), ((tok, 2 * LANES), f32), ((tok, 2 * LANES), f32), ((tok, 2 * LANES), f32),
        ((slots, tok), bf16), ((tok, 2 * LANES), bf16),
        ((n_dp, cap, LANES), bf16), ((2, n_dp, cap, LANES), bf16), ((n_seg, slots, LANES), bf16),
        ((rows_u, LANES), f32), ((rows_u, LANES), f32), ((n_seg, rows_u, LANES), bf16),
        ((rows_u, cols), f32), ((rows_u, out_half), f32),
        ((n_dp, rows_u, out_half + n_seg // 2 * LANES), bf16), ((2, n_dp, rows_u, n_seg // 2 * LANES), bf16),
        ((tok, cols), f32), ((tok, out_half), bf16), ((tok, out_half), bf16),
        ((n_dp, cap, out_half), bf16), ((n_dp, cap, out_half), bf16),
        (x.shape, bf16), ((slots, cols), f32), ((slots, out_half), bf16), ((slots, out_half), bf16),
        ((slots, LANES), f32), ((slots, LANES), f32), ((slots, known), bf16),
        ((width, slots), bf16), ((2, slots, out_half), bf16), ((2, 4, share, out_half), f32),
        ((2, 3, share, out_half), bf16), ((2, 2, 3, share // 2, out_half), bf16),
        ((1, slots), f32), ((1, slots), f32), ((n_seg, 1, slots), f32),
    ]
    sems = [5 + cols // LANES, 11, 11, 4 * (n_seg - 1), 4 * (n_seg - 1), 3 * (n_dp - 1), 3 * (n_dp - 1), 28, 28]
    return pl.pallas_call(
        functools.partial(step_kernel, n_seg, side, cap),
        out_shape=(
            jax.ShapeDtypeStruct((share, cols), f32),
            jax.ShapeDtypeStruct((1, slots), f32),
        ),
        in_specs=[hbm] * 7 + [vmem] * 6,
        out_specs=(vmem, vmem),
        scratch_shapes=[pltpu.VMEM(*s) for s in scratch] + [pltpu.SemaphoreType.DMA((n,)) for n in sems],
        compiler_params=pltpu.CompilerParams(
            collective_id=0, has_side_effects=True, vmem_limit_bytes=60 * 2**20
        ),
        cost_estimate=pl.CostEstimate(flops=flops, bytes_accessed=25 * 2**20, transcendentals=0),
    )(
        h, down, up, x, w, p, xmap,
        ids.reshape(1, tok), dest.reshape(1, tok), counts, gain, sgain.reshape(width // LANES, LANES), kcol,
    )


def local(
    teacher_hidden,
    teacher_id,
    destination,
    row_counts,
    section_gain,
    adapter_down,
    adapter_up,
    student_in,
    student_gain,
    student_weight,
    projector,
):
    weight_grad, row_loss = run_step(
        teacher_hidden,
        teacher_id,
        destination,
        row_counts,
        section_gain,
        adapter_down[0].T,
        adapter_up[0],
        student_in,
        student_gain,
        student_weight,
        projector,
    )
    share, cols = weight_grad.shape
    return (weight_grad.reshape(1, share, cols), row_loss.reshape(student_in.shape[0]))


def solution(mesh):
    placed = (
        P("dp", "mp"),
        P("dp"),
        P("dp"),
        P("dp", None),
        P("segment", "mp"),
        P("segment", "mp", None),
        P("segment", None, "mp"),
        P("dp", "mp"),
        P("mp"),
        P("mp", "segment"),
        P("mp", "segment"),
    )
    return jax.shard_map(
        local,
        mesh=mesh,
        in_specs=placed,
        out_specs=(P("mp", "dp", "segment"), P("dp")),
        check_vma=False,
    )
```

time: 105 us -> 86.8 us (0.83)
  Pallas kernels: 101 us -> 82.6 us
    pallas_call x2 -> x1, Pallas kernels: 101 us -> 82.6 us  [run_step(): pl.pallas_call(functools.partial(step_kernel, n_seg, side, cap), out_shap...]
where the time goes in v5:
time: 86.8 us; the launch traced here: 86.6 us
  Pallas kernels  82.6 us (95%)
  local copies, waits for them, and re-layouts  3.33 us (4%)
    pallas_call x1, Pallas kernels, run_step(): pl.pallas_call(functools.partial(step_kernel, n_seg, side, cap), out_shap...  82.6 us
    unnamed x2, local copies, waits for them, and re-layouts  3.33 us

profile of v5, /device:TPU:1, one launch (start us, length us, event | category | flops | bytes accessed | tf_op | source)
XLA Modules:
  0.0 86.6 jit_solution(626037063985110761)
XLA Ops:
  0.6 82.6 %shard_map.140 = (f32[160,1280]{1,0:T(8,128)}, f32[1,512]{1,0:T(1,128)}) custom-call(bf16[256,4096]{1,0:T(8,128)(2,1)} %h_hbm.1, bf16[192,4096]{1,0:T(8,128)(2,1)} %bitcast.11, bf16[192,4096]{1,0:T(8,128)(2,1)} %bitcast.12, bf16[512,2560]{1,0:T(8,128)(2,1)} %x_hbm.1, bf16[2560,1280]{1,0:T(8,128)(2,1)} %w_hbm.1, bf16[4096,1280]{1,0:T(8,128)(2,1)} %p_hbm.1, ...), custom_call_target="tpu_custom_call" | custom-call | flops 9395240960 | bytes 26214400 | tf_op jit(solution)/shard_map/pallas_call | solution.py:645
  83.3 2.1 %copy.17 = f32[1,160,1280]{2,1,0:T(8,128)} copy(f32[1,160,1280]{2,1,0:T(8,128)} %bitcast.9) | data formatting | bytes 1638400
  85.3 1.2 %copy.18 = f32[512]{0:T(512)} copy(f32[512]{0:T(512)} %bitcast.10) | data formatting | bytes 4096

commit v6 on v5

--- a/solution.py
+++ b/solution.py
@@ -65,8 +65,8 @@
     mgx, mggot, mgs, upx, upgot, blocks, tables,
     hpx, hpsend, hpgot, hslots, hgot,
     sg, sox, sosend, sogot, sxx, sxgot, ctil,
-    sgt, gd, held, part2, got2, losspart, lossgot, losses,
-    lsem, s_m, r_m, s_x, r_x, s_d, r_d, s_r, r_r,
+    sgt, nb, held, finsend, fingot, losspart, lossgot, losses,
+    lsem, s_m, r_m, s_x, r_x, s_d, r_d, s_n, r_n, s_r, r_r,
 ):
     me_s = lax.axis_index("segment")
     me_m = lax.axis_index("mp")
@@ -98,14 +98,22 @@
         return pltpu.make_async_copy(w_hbm.at[:, span], w.at[:, span], lsem.at[5 + tiles + n])
 
     up_in = load(0, up_hbm, up)
+    x_in = load(3, x_hbm, x)
     h_in = load(1, h_hbm, h)
     for n in range(tiles):
         p_copy(n).start()
     down_in = load(2, down_hbm, down)
-    x_in = load(3, x_hbm, x)
     for n in range(tiles):
         w_copy(n).start()
     xmap_in = load(4, xmap_hbm, xmap)
+
+    z = me_d // side
+    y = me_d % side
+
+    def place(first, second):
+        a = ((z * other + y * me_m) + second) % side
+        b = ((y * other + z * me_m) + first) % side
+        return (a * other + b * me_m) * side + b * other + a * me_m
 
     barrier = pltpu.get_barrier_semaphore()
     mesh_id = pl.DeviceIdType.MESH
@@ -117,6 +125,9 @@
     def _(n):
         pl.semaphore_signal(barrier, inc=1, device_id={"dp": (me_d + n) % n_dp}, device_id_type=mesh_id)
 
+    for n in range(1, side):
+        pl.semaphore_signal(barrier, inc=1, device_id={"dp": place(n, 0), "mp": other}, device_id_type=mesh_id)
+
     def to_peer(n, src, dst):
         return remote(src, dst, s_m.at[n], r_m.at[n], mp=other)
 
@@ -127,14 +138,6 @@
     def to_dp(kind, n, src, dst):
         number = kind * (n_dp - 1) + n - 1
         return remote(src, dst, s_d.at[number], r_d.at[number], dp=(me_d + n) % n_dp)
-
-    z = me_d // side
-    y = me_d % side
-
-    def place(first, second):
-        a = ((z * other + y * me_m) + second) % side
-        b = ((y * other + z * me_m) + first) % side
-        return (a * other + b * me_m) * side + b * other + a * me_m
 
     def gather_first(n):
         return remote(blocks.at[me_d], blocks.at[me_d], s_d.at[n + 29], r_d.at[n + 29], dp=place(n, 0))
@@ -167,25 +170,72 @@
     wide_b[...] = jnp.zeros(wide_b.shape, f32)
     abx[...] = jnp.zeros(abx.shape, f32)
 
-    pl.semaphore_wait(barrier, 1 + (n_seg - 1) + (n_dp - 1))
+    x_in.wait()
+    sxx[...] = jnp.zeros(sxx.shape, f32)
+
+    @pl.loop(0, x.shape[1] // LANES)
+    def _(n):
+        span = pl.ds(pl.multiple_of(n * LANES, LANES), LANES)
+        wide = x[:, span].astype(f32)
+        sxx[...] += wide * wide
+        scaled = (wide * sgain[pl.ds(n, 1), :]).astype(bf16)
+        sg[:, span] = scaled
+        sgt[span, :] = scaled.T
+
+    pl.semaphore_wait(barrier, 1 + (n_seg - 1) + (n_dp - 1) + (side - 1))
     u_sent = [to_seg(0, n, usend, ugot.at[me_s]) for n in range(1, n_seg)]
     for copy in u_sent:
         copy.start()
 
+    share = out.shape[0]
+
+    def rows_of(owner):
+        return sgt.at[pl.ds(pl.multiple_of(owner * share, share), share)]
+
+    def owner_of(f, other_ring):
+        return (1 - f) * (other_ring * side + y) + f * (z * side + other_ring)
+
+    def block_copy(f, n):
+        if f == 0:
+            where = z * side + (y + n) % side
+            owner = me_s * side + (y + n) % side
+        else:
+            where = ((z + n) % side) * side + y
+            owner = ((z + n) % side) * side + me_s
+        number = f * (side - 1) + n - 1
+        return remote(
+            rows_of(owner), nb.at[me_s, me_m, side - n], s_n.at[number], r_n.at[(n - 1) * 2 + me_m], dp=where, mp=f
+        )
+
+    def block_landed(m, n):
+        where = nb.at[me_s, m, side - n]
+        return remote(where, where, s_n.at[0], r_n.at[(n - 1) * 2 + m], mp=other)
+
+    def chip_copy(n):
+        return remote(rows_of(owner_of(other, n)), nb.at[n, me_m, 0], s_n.at[6 + n], r_n.at[6 + n], mp=other)
+
+    def plane_copy(way, m):
+        number = 10 + way * 2 + m
+        block = nb.at[me_s, m, 1:side]
+        return remote(block, block, s_n.at[number], r_n.at[number], segment=(me_s + 1 + way * (n_seg - 2)) % n_seg)
+
+    def plane_forward(way):
+        block = nb.at[(me_s + n_seg - 1 + 2 * way) % n_seg, way, 1:side]
+        return remote(block, block, s_n.at[14 + way], r_n.at[14 + way], segment=(me_s + 1 + way * (n_seg - 2)) % n_seg)
+
+    for n in range(1, side):
+        for f in (0, 1):
+            block_copy(f, n).start()
+    for n in range(side):
+        chip_copy(n).start()
+    sx_sent = to_peer(4, sxx, sxgot)
+    sx_sent.start()
+    for n in range(side):
+        nb[n, me_m, 0] = rows_of(owner_of(me_m, n))[...]
+
     away = pl.ds(pl.multiple_of(other * out_half, LANES), out_half)
     kept = pl.ds(pl.multiple_of(me_m * out_half, LANES), out_half)
     h_in.wait()
-
-    @pl.loop(0, tiles)
-    def _(n):
-        span = pl.ds(pl.multiple_of(n * tile, tile), tile)
-        p_copy(n).wait()
-        hpx[:, span] = dot(h[...], p[:, span])
-
-    hpsend[...] = hpx[:, away].astype(bf16)
-    hp_sent = to_peer(3, hpsend, hpgot)
-    hp_sent.start()
-
     down_in.wait()
     rank_all = down.shape[0]
 
@@ -206,6 +256,35 @@
     abx[:, :LANES] = jnp.where(lane < RANK, fold(wide_a[...], own), fold(wide_b[...], own))
     ab_sent = to_peer(0, abx, abgot)
     ab_sent.start()
+
+
+    @pl.loop(0, tiles)
+    def _(n):
+        span = pl.ds(pl.multiple_of(n * tile, tile), tile)
+        p_copy(n).wait()
+        hpx[:, span] = dot(h[...], p[:, span])
+
+    hpsend[...] = hpx[:, away].astype(bf16)
+    hp_sent = to_peer(3, hpsend, hpgot)
+    hp_sent.start()
+
+    ab_sent.wait_recv()
+    total = abx[...] + abgot[...]
+    sq = total[:, LANES:]
+    sq_hi = sq.astype(bf16).astype(f32)
+    extra = jnp.where(lane == 0, id_col, jnp.where(lane == 1, sq_hi, jnp.where(lane == 2, sq - sq_hi, 0.0)))
+    pay[:, :LANES] = total[:, :LANES].astype(bf16)
+    pay[:, LANES:] = extra.astype(bf16)
+    lanes_here = pl.ds(pl.multiple_of(me_m * LANES, LANES), LANES)
+    aslots[...] = dot(sel[...], pay[:, lanes_here]).astype(bf16).reshape(aslots.shape)
+    agot[me_m, me_d] = aslots[me_d]
+
+    def a_copy(n):
+        return to_dp(0, n, aslots.at[(me_d + n) % n_dp], agot.at[me_m, me_d])
+
+    @pl.loop(1, n_dp)
+    def _(n):
+        a_copy(n).start()
 
     hp_sent.wait_recv()
     hp = (hpx[:, kept] + hpgot[...].astype(f32)).astype(bf16)
@@ -242,49 +321,49 @@
     mg_sent = to_peer(1, mgx, mggot)
     mg_sent.start()
 
-    ab_sent.wait_recv()
-    total = abx[...] + abgot[...]
-    sq = total[:, LANES:]
-    sq_hi = sq.astype(bf16).astype(f32)
-    extra = jnp.where(lane == 0, id_col, jnp.where(lane == 1, sq_hi, jnp.where(lane == 2, sq - sq_hi, 0.0)))
-    pay[:, :LANES] = total[:, :LANES].astype(bf16)
-    pay[:, LANES:] = extra.astype(bf16)
-    lanes_here = pl.ds(pl.multiple_of(me_m * LANES, LANES), LANES)
-    aslots[...] = dot(sel[...], pay[:, lanes_here]).astype(bf16).reshape(aslots.shape)
-    agot[me_m, me_d] = aslots[me_d]
-
-    def a_copy(n):
-        return to_dp(0, n, aslots.at[(me_d + n) % n_dp], agot.at[me_m, me_d])
-
-    @pl.loop(1, n_dp)
-    def _(n):
-        a_copy(n).start()
-
+    @pl.loop(0, tiles)
+    def _(n):
+        span = pl.ds(pl.multiple_of(n * tile, tile), tile)
+        upx[:, span] = dot(ucat[...], p[:, span])
+
+    up_sent = to_peer(2, upx.at[:, away], upgot)
+    up_sent.start()
     mg_sent.wait_recv()
     mgs[me_s] = (mgx[...] + mggot[...]).astype(bf16)
     mg_x = [to_seg(1, n, mgs.at[me_s], mgs.at[me_s]) for n in range(1, n_seg)]
     for copy in mg_x:
         copy.start()
 
-    @pl.loop(0, tiles)
-    def _(n):
+    def student(n):
         span = pl.ds(pl.multiple_of(n * tile, tile), tile)
-        upx[:, span] = dot(ucat[...], p[:, span])
-
-    up_sent = to_peer(2, upx.at[:, away], upgot)
-    up_sent.start()
-    x_in.wait()
-    sxx[...] = jnp.zeros(sxx.shape, f32)
-
-    @pl.loop(0, x.shape[1] // LANES)
-    def _(n):
-        span = pl.ds(pl.multiple_of(n * LANES, LANES), LANES)
-        wide = x[:, span].astype(f32)
-        sxx[...] += wide * wide
-        sg[:, span] = (wide * sgain[pl.ds(n, 1), :]).astype(bf16)
-
-    sx_sent = to_peer(4, sxx, sxgot)
-    sx_sent.start()
+        w_copy(n).wait()
+        sox[:, span] = dot(sg[...], w[:, span])
+
+    @pl.loop(1, n_dp)
+    def _(n):
+        a_copy(n).wait_recv()
+
+    a_x = [to_seg(2, n, aall.at[me_s], aall.at[me_s]) for n in range(1, n_seg)]
+    extra_swap = to_peer(6, agot.at[1], agot.at[1])
+
+    @pl.when(me_m == 0)
+    def _():
+        aall[me_s] = agot[0].reshape(slots, LANES)
+        for copy in a_x:
+            copy.start()
+
+    @pl.when(me_m == 1)
+    def _():
+        extra_swap.start()
+
+    for n in range(1, side):
+        for m in (0, 1):
+            block_landed(m, n).wait_recv()
+    for way in (0, 1):
+        for m in (way, 1 - way):
+            plane_copy(way, m).start()
+    pl.loop(0, 2)(student)
+
     up_sent.wait_recv()
     blocks[me_d, :, :out_half] = (upx[:, kept] + upgot[...]).astype(bf16)
     for copy in mg_x:
@@ -299,30 +378,6 @@
     for copy in seconds:
         copy.start()
 
-    def student(n):
-        span = pl.ds(pl.multiple_of(n * tile, tile), tile)
-        w_copy(n).wait()
-        sox[:, span] = dot(sg[...], w[:, span])
-
-    pl.loop(0, 2)(student)
-
-    @pl.loop(1, n_dp)
-    def _(n):
-        a_copy(n).wait_recv()
-
-    a_x = [to_seg(2, n, aall.at[me_s], aall.at[me_s]) for n in range(1, n_seg)]
-    extra_swap = to_peer(6, agot.at[1], agot.at[1])
-
-    @pl.when(me_m == 0)
-    def _():
-        aall[me_s] = agot[0].reshape(slots, LANES)
-        for copy in a_x:
-            copy.start()
-
-    @pl.when(me_m == 1)
-    def _():
-        extra_swap.start()
-
     pl.loop(2, 3)(student)
     for k in range(1, side):
         firsts[k - 1].wait_recv()
@@ -343,11 +398,6 @@
         for copy in a_x:
             copy.wait_recv()
         a_swap.start()
-
-    @pl.loop(0, x.shape[1] // LANES)
-    def _(n):
-        span = pl.ds(pl.multiple_of(n * LANES, LANES), LANES)
-        sgt[span, :] = sg[:, span].T
 
     for copy in seconds:
         copy.wait_recv()
@@ -410,109 +460,69 @@
     student_out = (sox[:, kept] + sogot[...].astype(f32)) * recip
     diff = jnp.where(valid > 0.0, student_out - target, 0.0)
     loss = jnp.sum(diff * diff, axis=1, keepdims=True)
-    gd[me_m] = (diff * (recip * (1.0 / TOK_DEV))).astype(bf16)
-    gd_swap = to_peer(9, gd.at[me_m], gd.at[me_m])
-    gd_swap.start()
+    edge = slots // 2
+
+    def gathered(ahead, low=0, count=slots):
+        return p.at[pl.ds(ahead * slots + low, count), :out_half]
+
+    def diff_copy(way, part):
+        ahead = (side - 1, 1)[way]
+        number = way * 2 + part
+        return remote(
+            gathered(0, part * edge, edge), gathered(ahead, part * edge, edge),
+            s_r.at[number], r_r.at[number], dp=place(1 + way * (side - 2), 0),
+        )
+
+    def diff_forward(way):
+        ahead = (side - 1, 1)[way]
+        return remote(
+            gathered(ahead, way * edge, edge), gathered(2, way * edge, edge),
+            s_r.at[4 + way], r_r.at[4 + way], dp=place(1 + way * (side - 2), 0),
+        )
+
+    gathered(0)[...] = (diff * (recip * (1.0 / TOK_DEV))).astype(bf16)
+    for way in (0, 1):
+        diff_copy(way, way).start()
+    for way in (0, 1):
+        diff_copy(way, 1 - way).start()
     losspart[...] = jnp.broadcast_to(loss, (slots, LANES)).T[0:1, :]
-    loss_swap = to_peer(10, losspart, lossgot)
+    loss_swap = to_peer(9, losspart, lossgot)
     loss_swap.start()
-
-    share = out.shape[0]
-    edge = share // 2
-    wide_out = gd.shape[2]
-
-    def step(way):
-        return 1 + way * (side - 2)
-
-    def ring(f, way):
-        ahead = step(way)
-        return (1 - f) * (z * side + (y + ahead) % side) + f * (((z + ahead) % side) * side + y)
-
-    def product(f, ahead, mid, b):
-        first = ((1 - f) * y + f * z + ahead) % side
-        second = ((1 - f) * z + f * y + (1 - mid) * (2 - 2 * b) + mid * (1 + 2 * b)) % side
-        owner = (1 - f) * (second * side + first) + f * (first * side + second)
-        return jnp.dot(
-            sgt[pl.ds(pl.multiple_of(owner * share, share), share), :], gd[f], preferred_element_type=f32
-        )
-
-    def sent(f, slot, row, count):
-        low = pl.multiple_of(((f * 3 + slot) * 4 + row) * share, share)
-        return p.at[pl.ds(low, count * share), wide_out:]
-
-    def landed(f, way, row, count):
-        low = pl.multiple_of(((f * 2 + way) * 6 + row) * share, share)
-        return p.at[pl.ds(low, count * share), :wide_out]
-
-    def first_copy(f, way, msg):
-        number = (f * 2 + way) * 4 + msg
-        if msg == 0:
-            src, dst = sent(f, 0, 2 * way, 2), landed(f, way, 0, 2)
-        elif msg == 1:
-            src, dst = sent(f, 1 + way, 2 - 2 * way, 2), landed(f, way, 2, 2)
-        else:
-            src, dst = sent(f, 1 + way, 2 * way + msg - 2, 1), landed(f, way, 2 + msg, 1)
-        return remote(src, dst, s_r.at[number], r_r.at[number], dp=ring(f, way))
-
-    def second_copy(f, way, msg):
-        number = 16 + (f * 2 + way) * 3 + msg
-        slot = 0 if msg == 0 else 1 + way
-        low = (1 - way) * edge if msg == 1 else way * edge
-        src = part2.at[f, slot, pl.ds(pl.multiple_of(low, edge), edge)]
-        return remote(src, got2.at[f, way, msg], s_r.at[number], r_r.at[number], dp=ring(1 - f, way))
-
-    def flow(n):
-        return me_m + n * (1 - 2 * me_m)
-
-    for n in range(2):
-        if n == 1:
-            gd_swap.wait_recv()
-
+    for way in (0, 1):
+        plane_copy(way, way).wait_recv()
+        plane_forward(way).start()
+
+    def product(owner, m, ahead):
+        return dot(nb[owner, m, ahead], gathered(ahead)[...])
+
+    for n in range(side):
+        chip_copy(n).wait_recv()
+
+    @pl.loop(0, side)
+    def _(n):
         @pl.loop(0, 2)
-        def _(way):
-            @pl.loop(0, 2)
-            def _(b):
-                sent(flow(n), 0, 2 * way + b, 1)[...] = product(flow(n), 2, way, b).astype(bf16)
-
-            first_copy(flow(n), way, 0).start()
-
-    @pl.loop(0, 2)
-    def _(n):
-        @pl.loop(0, 2)
-        def _(way):
-            @pl.loop(0, 2)
-            def _(b):
-                blk = product(flow(n), step(way), 1 - way, b)
-                sent(flow(n), 1 + way, 2 - 2 * way + b, 1)[...] = blk.astype(bf16)
-
-            first_copy(flow(n), way, 1).start()
-
+        def _(m):
+            held[n, m] = product(n, m, 0)
+
+    for way in (0, 1):
+        diff_copy(way, way).wait_recv()
+        diff_forward(way).start()
     loss_swap.wait_recv()
     losses[me_s] = losspart[...] + lossgot[...]
     tells = [to_seg(3, n, losses.at[me_s], losses.at[me_s]) for n in range(1, n_seg)]
     for copy in tells:
         copy.start()
-
-    @pl.loop(0, 2)
+    for way in (0, 1):
+        plane_copy(way, 1 - way).wait_recv()
+        plane_forward(way).wait_recv()
+    for way in (0, 1):
+        diff_copy(way, 1 - way).wait_recv()
+
+    @pl.loop(0, side)
     def _(n):
         @pl.loop(0, 2)
-        def _(mid):
-            @pl.loop(0, 2)
-            def _(b):
-                held[flow(n), 2 * mid + b] = product(flow(n), 0, mid, b)
-
-    for b in range(2):
-
-        @pl.loop(0, 2)
-        def _(n):
-            @pl.loop(0, 2)
-            def _(way):
-                f = flow(n)
-                if b == 0:
-                    first_copy(f, way, 0).wait_recv()
-                blk = product(f, step(way), way, b) + landed(f, way, b, 1)[...].astype(f32)
-                sent(f, 1 + way, 2 * way + b, 1)[...] = blk.astype(bf16)
-                first_copy(f, way, 2 + b).start()
+        def _(m):
+            held[n, m] += product(n, m, 1) + product(n, m, 3)
 
     for copy in tells:
         copy.wait_recv()
@@ -521,68 +531,72 @@
         total = total + losses[n]
     loss_out[...] = total * (1.0 / S)
 
+    ring_at = z * other + y * me_m
+    base = side * slots
+
+    def sent(slot, m):
+        return p.at[pl.ds(base + (slot * 2 + m) * share, share), :out_half]
+
+    def landed(way, msg):
+        return p.at[pl.ds(pl.multiple_of(base + (way * 3 + msg) * share, 16), share), out_half:]
+
+    def sum_copy(way, msg):
+        slot = 0 if msg == 0 else 1 + way
+        m = 1 - way if msg == 1 else way
+        number = 6 + way * 3 + msg
+        return remote(
+            sent(slot, m), landed(way, msg), s_r.at[number], r_r.at[number], dp=place(0, 1 + way * (side - 2))
+        )
+
+    for way in (0, 1):
+        diff_forward(way).wait_recv()
+    far = (ring_at + 2) % side
+    nears = [(ring_at + 1) % side, (ring_at + side - 1) % side]
+    for way in (0, 1):
+        sent(0, way)[...] = (held[far, way] + product(far, way, 2)).astype(bf16)
+        sum_copy(way, 0).start()
+    for way in (0, 1):
+        sent(1 + way, 1 - way)[...] = (held[nears[way], 1 - way] + product(nears[way], 1 - way, 2)).astype(bf16)
+        sum_copy(way, 1).start()
+    for way in (0, 1):
+        held[nears[way], way] += product(nears[way], way, 2)
+
     @pl.loop(0, 2)
-    def _(n):
-        f = flow(n)
-
-        @pl.loop(0, 2)
-        def _(way):
-            first_copy(f, way, 1).wait_recv()
-            for b in range(2):
-                held[f, 2 - 2 * way + b] += landed(f, way, 2 + b, 1)[...].astype(f32)
-
-    for b in range(2):
-
-        @pl.loop(0, 2)
-        def _(n):
-            f = flow(n)
-
-            @pl.loop(0, 2)
-            def _(way):
-                first_copy(f, way, 2 + b).wait_recv()
-                held[f, 2 * way + b] += landed(f, way, 4 + b, 1)[...].astype(f32)
-
-            if b == 0:
-                part2[f, 0] = held[f, 0].astype(bf16)
-                for way in range(2):
-                    second_copy(f, way, 0).start()
-                part2[f, 1, edge:] = held[f, 2, edge:].astype(bf16)
-                second_copy(f, 0, 1).start()
-            else:
-                part2[f, 2, :edge] = held[f, 3, :edge].astype(bf16)
-                second_copy(f, 1, 1).start()
-
-    @pl.loop(0, 2)
-    def _(n):
-        f = flow(n)
-        for way in range(2):
-            second_copy(f, way, 0).wait_recv()
-            rows = slice(way * edge, (way + 1) * edge)
-            part2[f, 1 + way, rows] = (held[f, 2 + way, rows] + got2[f, way, 0].astype(f32)).astype(bf16)
-            second_copy(f, way, 2).start()
-
-    @pl.loop(0, 2)
-    def _(n):
-        f = flow(n)
-        for msg in (1, 2):
-            for way in range(2):
-                second_copy(f, way, msg).wait_recv()
-        span = pl.ds(pl.multiple_of(f * wide_out, LANES), wide_out)
-        out[:edge, span] = held[f, 1, :edge] + got2[f, 0, 2].astype(f32) + got2[f, 1, 1].astype(f32)
-        out[edge:, span] = held[f, 1, edge:] + got2[f, 0, 1].astype(f32) + got2[f, 1, 2].astype(f32)
-
-    @pl.loop(0, 2)
-    def _(f):
-        @pl.loop(0, 2)
-        def _(way):
-            for msg in range(4):
-                first_copy(f, way, msg).wait_send()
-
-        for way in range(2):
-            for msg in range(3):
-                second_copy(f, way, msg).wait_send()
-
-    for copy in u_sent + mg_x + firsts + seconds + [ab_sent, mg_sent, up_sent, hp_sent, sx_sent, so_sent, table_swap, gd_swap, loss_swap] + tells:
+    def _(m):
+        held[ring_at, m] += product(ring_at, m, 2)
+
+    for way in (0, 1):
+        sum_copy(way, 0).wait_recv()
+        sent(1 + way, way)[...] = (held[nears[way], way] + landed(way, 0)[...].astype(f32)).astype(bf16)
+        sum_copy(way, 2).start()
+    for msg in (1, 2):
+        for way in (0, 1):
+            sum_copy(way, msg).wait_recv()
+
+    def summed(m):
+        return held[ring_at, m] + landed(0, 2 - m)[...].astype(f32) + landed(1, 1 + m)[...].astype(f32)
+
+    finsend[...] = summed(other)
+    last_swap = to_peer(10, finsend, fingot)
+    last_swap.start()
+    out[:, kept] = summed(me_m)
+    last_swap.wait_recv()
+    out[:, away] = fingot[...]
+
+    for n in range(1, side):
+        for f in (0, 1):
+            block_copy(f, n).wait_send()
+    for n in range(side):
+        chip_copy(n).wait_send()
+    for way in (0, 1):
+        for m in (0, 1):
+            plane_copy(way, m).wait_send()
+            diff_copy(way, m).wait_send()
+        plane_forward(way).wait_send()
+        diff_forward(way).wait_send()
+        for msg in range(3):
+            sum_copy(way, msg).wait_send()
+    for copy in u_sent + mg_x + firsts + seconds + [ab_sent, mg_sent, up_sent, hp_sent, sx_sent, so_sent, table_swap, loss_swap, last_swap] + tells:
         copy.wait_send()
 
     @pl.when(me_m == 0)
@@ -637,11 +651,11 @@
         ((n_dp, cap, out_half), bf16), ((n_dp, cap, out_half), bf16),
         (x.shape, bf16), ((slots, cols), f32), ((slots, out_half), bf16), ((slots, out_half), bf16),
         ((slots, LANES), f32), ((slots, LANES), f32), ((slots, known), bf16),
-        ((width, slots), bf16), ((2, slots, out_half), bf16), ((2, 4, share, out_half), f32),
-        ((2, 3, share, out_half), bf16), ((2, 2, 3, share // 2, out_half), bf16),
+        ((width, slots), bf16), ((n_seg, 2, side, share, slots), bf16), ((side, 2, share, out_half), f32),
+        ((share, out_half), f32), ((share, out_half), f32),
         ((1, slots), f32), ((1, slots), f32), ((n_seg, 1, slots), f32),
     ]
-    sems = [5 + cols // LANES, 11, 11, 4 * (n_seg - 1), 4 * (n_seg - 1), 3 * (n_dp - 1), 3 * (n_dp - 1), 28, 28]
+    sems = [5 + cols // LANES, 11, 11, 4 * (n_seg - 1), 4 * (n_seg - 1), 3 * (n_dp - 1), 3 * (n_dp - 1), 16, 16, 12, 12]
     return pl.pallas_call(
         functools.partial(step_kernel, n_seg, side, cap),
         out_shape=(

time: 86.8 us -> 83.7 us (0.964)
  Pallas kernels: 82.6 us -> 79.5 us
    pallas_call x1, Pallas kernels: 82.6 us -> 79.5 us  [run_step(): pl.pallas_call(functools.partial(step_kernel, n_seg, side, cap), out_shap...]
where the time goes in v6:
time: 83.7 us; the launch traced here: 83.5 us
  Pallas kernels  79.5 us (95%)
  local copies, waits for them, and re-layouts  3.33 us (4%)
    pallas_call x1, Pallas kernels, run_step(): pl.pallas_call(functools.partial(step_kernel, n_seg, side, cap), out_shap...  79.5 us
    unnamed x2, local copies, waits for them, and re-layouts  3.33 us

profile of v6, /device:TPU:1, one launch (start us, length us, event | category | flops | bytes accessed | tf_op | source)
XLA Modules:
  0.0 83.5 jit_solution(8280894200917381391)
XLA Ops:
  0.6 79.5 %shard_map.140 = (f32[160,1280]{1,0:T(8,128)}, f32[1,512]{1,0:T(1,128)}) custom-call(bf16[256,4096]{1,0:T(8,128)(2,1)} %h_hbm.1, bf16[192,4096]{1,0:T(8,128)(2,1)} %bitcast.11, bf16[192,4096]{1,0:T(8,128)(2,1)} %bitcast.12, bf16[512,2560]{1,0:T(8,128)(2,1)} %x_hbm.1, bf16[2560,1280]{1,0:T(8,128)(2,1)} %w_hbm.1, bf16[4096,1280]{1,0:T(8,128)(2,1)} %p_hbm.1, ...), custom_call_target="tpu_custom_call" | custom-call | flops 9395240960 | bytes 26214400 | tf_op jit(solution)/shard_map/pallas_call | solution.py:659
  80.1 2.1 %copy.17 = f32[1,160,1280]{2,1,0:T(8,128)} copy(f32[1,160,1280]{2,1,0:T(8,128)} %bitcast.9) | data formatting | bytes 1638400
  82.2 1.2 %copy.18 = f32[512]{0:T(512)} copy(f32[512]{0:T(512)} %bitcast.10) | data formatting | bytes 4096

commit v7 on v6

--- a/solution.py
+++ b/solution.py
@@ -64,7 +64,7 @@
     usend, ugot, ucat, wide_a, wide_b, abx, abgot, sel, pay, aslots, agot, aall,
     mgx, mggot, mgs, upx, upgot, blocks, tables,
     hpx, hpsend, hpgot, hslots, hgot,
-    sg, sox, sosend, sogot, sxx, sxgot, ctil,
+    sg, sox, sosend, sogot, sxx, sxgot, ctil, base,
     sgt, nb, held, finsend, fingot, losspart, lossgot, losses,
     lsem, s_m, r_m, s_x, r_x, s_d, r_d, s_n, r_n, s_r, r_r,
 ):
@@ -140,11 +140,11 @@
         return remote(src, dst, s_d.at[number], r_d.at[number], dp=(me_d + n) % n_dp)
 
     def gather_first(n):
-        return remote(blocks.at[me_d], blocks.at[me_d], s_d.at[n + 29], r_d.at[n + 29], dp=place(n, 0))
+        return remote(blocks.at[me_d], blocks.at[me_d], s_d.at[n + 44], r_d.at[n + 44], dp=place(n, 0))
 
     def gather_second(k, n):
         source = place(side - k, 0)
-        number = 33 + k * (side - 1) + n - 1
+        number = 48 + k * (side - 1) + n - 1
         return remote(blocks.at[source], blocks.at[source], s_d.at[number], r_d.at[number], dp=place(0, n))
 
     packed = n_seg * per
@@ -160,12 +160,6 @@
         mine = mine + dot(ones_where(hit & (block == g)), up[:, g * part : (g + 1) * part])
     usend[...] = mine.astype(bf16)
     ugot[me_s] = usend[...]
-    dest_f = dest[...].astype(f32)
-    onehot = jnp.where(iota((n_dp, tok), 0).astype(f32) == dest_f, 1.0, 0.0)
-    before = ones_where(iota((tok, tok), 0) < iota((tok, tok), 1))
-    earlier = dot(onehot.astype(bf16), before)
-    position = dest_f * cap + jnp.sum(earlier * onehot, axis=0, keepdims=True)
-    sel[...] = ones_where(iota((slots, tok), 0).astype(f32) == position)
     wide_a[...] = jnp.zeros(wide_a.shape, f32)
     wide_b[...] = jnp.zeros(wide_b.shape, f32)
     abx[...] = jnp.zeros(abx.shape, f32)
@@ -268,6 +262,12 @@
     hp_sent = to_peer(3, hpsend, hpgot)
     hp_sent.start()
 
+    dest_f = dest[...].astype(f32)
+    onehot = jnp.where(iota((n_dp, tok), 0).astype(f32) == dest_f, 1.0, 0.0)
+    before = ones_where(iota((tok, tok), 0) < iota((tok, tok), 1))
+    earlier = dot(onehot.astype(bf16), before)
+    position = dest_f * cap + jnp.sum(earlier * onehot, axis=0, keepdims=True)
+    sel[...] = ones_where(iota((slots, tok), 0).astype(f32) == position)
     ab_sent.wait_recv()
     total = abx[...] + abgot[...]
     sq = total[:, LANES:]
@@ -321,56 +321,42 @@
     mg_sent = to_peer(1, mgx, mggot)
     mg_sent.start()
 
-    @pl.loop(0, tiles)
-    def _(n):
+    def up_tile(n):
         span = pl.ds(pl.multiple_of(n * tile, tile), tile)
         upx[:, span] = dot(ucat[...], p[:, span])
 
-    up_sent = to_peer(2, upx.at[:, away], upgot)
-    up_sent.start()
+    pl.loop(0, 2)(up_tile)
     mg_sent.wait_recv()
     mgs[me_s] = (mgx[...] + mggot[...]).astype(bf16)
     mg_x = [to_seg(1, n, mgs.at[me_s], mgs.at[me_s]) for n in range(1, n_seg)]
     for copy in mg_x:
         copy.start()
 
+    pl.loop(2, tiles)(up_tile)
+    up_sent = to_peer(2, upx.at[:, away], upgot)
+    up_sent.start()
+
     def student(n):
         span = pl.ds(pl.multiple_of(n * tile, tile), tile)
         w_copy(n).wait()
         sox[:, span] = dot(sg[...], w[:, span])
 
-    @pl.loop(1, n_dp)
-    def _(n):
-        a_copy(n).wait_recv()
-
-    a_x = [to_seg(2, n, aall.at[me_s], aall.at[me_s]) for n in range(1, n_seg)]
-    extra_swap = to_peer(6, agot.at[1], agot.at[1])
-
-    @pl.when(me_m == 0)
-    def _():
-        aall[me_s] = agot[0].reshape(slots, LANES)
-        for copy in a_x:
-            copy.start()
-
-    @pl.when(me_m == 1)
-    def _():
-        extra_swap.start()
-
-    for n in range(1, side):
-        for m in (0, 1):
-            block_landed(m, n).wait_recv()
-    for way in (0, 1):
-        for m in (way, 1 - way):
-            plane_copy(way, m).start()
-    pl.loop(0, 2)(student)
-
-    up_sent.wait_recv()
-    blocks[me_d, :, :out_half] = (upx[:, kept] + upgot[...]).astype(bf16)
+    pl.loop(0, 1)(student)
+
     for copy in mg_x:
         copy.wait_recv()
     for n in range(pair):
-        low = out_half + n * LANES
-        blocks[me_d, :, low : low + LANES] = mgs[me_m * pair + n]
+        tables[me_m, me_d, :, n * LANES : (n + 1) * LANES] = mgs[me_m * pair + n]
+
+    def m_copy(n):
+        return to_dp(2, n, tables.at[me_m, me_d], tables.at[me_m, me_d])
+
+    @pl.loop(1, n_dp)
+    def _(n):
+        m_copy(n).start()
+
+    up_sent.wait_recv()
+    blocks[me_d] = (upx[:, kept] + upgot[...]).astype(bf16)
     firsts = [gather_first(n) for n in range(1, side)]
     for copy in firsts:
         copy.start()
@@ -378,7 +364,31 @@
     for copy in seconds:
         copy.start()
 
-    pl.loop(2, 3)(student)
+    @pl.loop(1, n_dp)
+    def _(n):
+        a_copy(n).wait_recv()
+
+    a_x = [to_seg(2, n, aall.at[me_s], aall.at[me_s]) for n in range(1, n_seg)]
+    extra_swap = to_peer(6, agot.at[1], agot.at[1])
+
+    @pl.when(me_m == 0)
+    def _():
+        aall[me_s] = agot[0].reshape(slots, LANES)
+        for copy in a_x:
+            copy.start()
+
+    @pl.when(me_m == 1)
+    def _():
+        extra_swap.start()
+
+    for n in range(1, side):
+        for m in (0, 1):
+            block_landed(m, n).wait_recv()
+    for way in (0, 1):
+        for m in (way, 1 - way):
+            plane_copy(way, m).start()
+
+    pl.loop(1, 4)(student)
     for k in range(1, side):
         firsts[k - 1].wait_recv()
         for n in range(1, side):
@@ -386,8 +396,7 @@
             copy.start()
             seconds.append(copy)
 
-
-    pl.loop(3, tiles)(student)
+    pl.loop(4, tiles)(student)
     sosend[...] = sox[:, away].astype(bf16)
     so_sent = to_peer(5, sosend, sogot)
     so_sent.start()
@@ -399,9 +408,10 @@
             copy.wait_recv()
         a_swap.start()
 
-    for copy in seconds:
-        copy.wait_recv()
-    tables[me_m] = blocks[:, :, out_half:]
+    @pl.loop(1, n_dp)
+    def _(n):
+        m_copy(n).wait_recv()
+
     table_swap = to_peer(8, tables.at[me_m], tables.at[me_m])
     table_swap.start()
 
@@ -445,9 +455,8 @@
     def _(n):
         h_copy(n).wait_recv()
 
-    sx_sent.wait_recv()
+    sx_sent.wait()
     so_sent.wait_recv()
-    table = blocks[:, :, :out_half].reshape(known, out_half)
     slot = iota((slots, n_dp), 0)
     source = iota((slots, n_dp), 1)
     room = slot - source * cap
@@ -456,10 +465,12 @@
     )
     square = jnp.sum(sxx[...] + sxgot[...], axis=1, keepdims=True)
     recip = lax.rsqrt(square * (1.0 / S) + 1e-06)
-    target = dot(ctil[...], table) + hgot[...].reshape(slots, out_half).astype(f32)
     student_out = (sox[:, kept] + sogot[...].astype(f32)) * recip
-    diff = jnp.where(valid > 0.0, student_out - target, 0.0)
-    loss = jnp.sum(diff * diff, axis=1, keepdims=True)
+    base[...] = jnp.where(valid > 0.0, student_out - hgot[...].reshape(slots, out_half).astype(f32), 0.0)
+    sxx[...] = jnp.broadcast_to(recip * (1.0 / TOK_DEV), sxx.shape)
+    for copy in seconds:
+        copy.wait_recv()
+    table = blocks[...].reshape(known, out_half)
     edge = slots // 2
 
     def gathered(ahead, low=0, count=slots):
@@ -480,12 +491,19 @@
             s_r.at[4 + way], r_r.at[4 + way], dp=place(1 + way * (side - 2), 0),
         )
 
-    gathered(0)[...] = (diff * (recip * (1.0 / TOK_DEV))).astype(bf16)
-    for way in (0, 1):
-        diff_copy(way, way).start()
+    def difference(part):
+        rows = slice(part * edge, (part + 1) * edge)
+        diff = base[rows, :] - dot(ctil[rows, :], table)
+        gathered(0, part * edge, edge)[...] = (diff * sxx[rows, 0:1]).astype(bf16)
+        loss = jnp.sum(diff * diff, axis=1, keepdims=True)
+        losspart[:, rows] = jnp.broadcast_to(loss, (edge, LANES)).T[0:1, :]
+
+    difference(0)
+    diff_copy(0, 0).start()
+    difference(1)
+    diff_copy(1, 1).start()
     for way in (0, 1):
         diff_copy(way, 1 - way).start()
-    losspart[...] = jnp.broadcast_to(loss, (slots, LANES)).T[0:1, :]
     loss_swap = to_peer(9, losspart, lossgot)
     loss_swap.start()
     for way in (0, 1):
@@ -532,13 +550,13 @@
     loss_out[...] = total * (1.0 / S)
 
     ring_at = z * other + y * me_m
-    base = side * slots
+    below = side * slots
 
     def sent(slot, m):
-        return p.at[pl.ds(base + (slot * 2 + m) * share, share), :out_half]
+        return p.at[pl.ds(below + (slot * 2 + m) * share, share), :out_half]
 
     def landed(way, msg):
-        return p.at[pl.ds(pl.multiple_of(base + (way * 3 + msg) * share, 16), share), out_half:]
+        return p.at[pl.ds(pl.multiple_of(below + (way * 3 + msg) * share, 16), share), out_half:]
 
     def sum_copy(way, msg):
         slot = 0 if msg == 0 else 1 + way
@@ -596,7 +614,7 @@
         diff_forward(way).wait_send()
         for msg in range(3):
             sum_copy(way, msg).wait_send()
-    for copy in u_sent + mg_x + firsts + seconds + [ab_sent, mg_sent, up_sent, hp_sent, sx_sent, so_sent, table_swap, loss_swap, last_swap] + tells:
+    for copy in u_sent + mg_x + firsts + seconds + [ab_sent, mg_sent, up_sent, hp_sent, so_sent, table_swap, loss_swap, last_swap] + tells:
         copy.wait_send()
 
     @pl.when(me_m == 0)
@@ -611,6 +629,7 @@
     @pl.loop(1, n_dp)
     def _(n):
         a_copy(n).wait_send()
+        m_copy(n).wait_send()
         h_copy(n).wait_send()
 
 
@@ -646,16 +665,16 @@
         ((n_dp, cap, LANES), bf16), ((2, n_dp, cap, LANES), bf16), ((n_seg, slots, LANES), bf16),
         ((rows_u, LANES), f32), ((rows_u, LANES), f32), ((n_seg, rows_u, LANES), bf16),
         ((rows_u, cols), f32), ((rows_u, out_half), f32),
-        ((n_dp, rows_u, out_half + n_seg // 2 * LANES), bf16), ((2, n_dp, rows_u, n_seg // 2 * LANES), bf16),
+        ((n_dp, rows_u, out_half), bf16), ((2, n_dp, rows_u, n_seg // 2 * LANES), bf16),
         ((tok, cols), f32), ((tok, out_half), bf16), ((tok, out_half), bf16),
         ((n_dp, cap, out_half), bf16), ((n_dp, cap, out_half), bf16),
         (x.shape, bf16), ((slots, cols), f32), ((slots, out_half), bf16), ((slots, out_half), bf16),
-        ((slots, LANES), f32), ((slots, LANES), f32), ((slots, known), bf16),
+        ((slots, LANES), f32), ((slots, LANES), f32), ((slots, known), bf16), ((slots, out_half), f32),
         ((width, slots), bf16), ((n_seg, 2, side, share, slots), bf16), ((side, 2, share, out_half), f32),
         ((share, out_half), f32), ((share, out_half), f32),
         ((1, slots), f32), ((1, slots), f32), ((n_seg, 1, slots), f32),
     ]
-    sems = [5 + cols // LANES, 11, 11, 4 * (n_seg - 1), 4 * (n_seg - 1), 3 * (n_dp - 1), 3 * (n_dp - 1), 16, 16, 12, 12]
+    sems = [5 + cols // LANES, 11, 11, 4 * (n_seg - 1), 4 * (n_seg - 1), 4 * (n_dp - 1), 4 * (n_dp - 1), 16, 16, 12, 12]
     return pl.pallas_call(
         functools.partial(step_kernel, n_seg, side, cap),
         out_shape=(

time: 83.7 us -> 85.1 us (1.017)
  Pallas kernels: 79.5 us -> 80.9 us
    pallas_call x1, Pallas kernels: 79.5 us -> 80.9 us  [run_step(): pl.pallas_call(functools.partial(step_kernel, n_seg, side, cap), out_shap...]
where the time goes in v7:
time: 85.1 us; the launch traced here: 84.8 us
  Pallas kernels  80.9 us (95%)
  local copies, waits for them, and re-layouts  3.33 us (4%)
    pallas_call x1, Pallas kernels, run_step(): pl.pallas_call(functools.partial(step_kernel, n_seg, side, cap), out_shap...  80.9 us
    unnamed x2, local copies, waits for them, and re-layouts  3.33 us

profile of v7, /device:TPU:1, one launch (start us, length us, event | category | flops | bytes accessed | tf_op | source)
XLA Modules:
  0.0 84.8 jit_solution(17975130252775272056)
XLA Ops:
  0.6 80.9 %shard_map.140 = (f32[160,1280]{1,0:T(8,128)}, f32[1,512]{1,0:T(1,128)}) custom-call(bf16[256,4096]{1,0:T(8,128)(2,1)} %h_hbm.1, bf16[192,4096]{1,0:T(8,128)(2,1)} %bitcast.11, bf16[192,4096]{1,0:T(8,128)(2,1)} %bitcast.12, bf16[512,2560]{1,0:T(8,128)(2,1)} %x_hbm.1, bf16[2560,1280]{1,0:T(8,128)(2,1)} %w_hbm.1, bf16[4096,1280]{1,0:T(8,128)(2,1)} %p_hbm.1, ...), custom_call_target="tpu_custom_call" | custom-call | flops 9395240960 | bytes 26214400 | tf_op jit(solution)/shard_map/pallas_call | solution.py:678
  81.5 2.1 %copy.17 = f32[1,160,1280]{2,1,0:T(8,128)} copy(f32[1,160,1280]{2,1,0:T(8,128)} %bitcast.9) | data formatting | bytes 1638400
  83.6 1.2 %copy.18 = f32[512]{0:T(512)} copy(f32[512]{0:T(512)} %bitcast.10) | data formatting | bytes 4096

commit v8 on v7

--- a/solution.py
+++ b/solution.py
@@ -198,26 +198,27 @@
             owner = ((z + n) % side) * side + me_s
         number = f * (side - 1) + n - 1
         return remote(
-            rows_of(owner), nb.at[me_s, me_m, side - n], s_n.at[number], r_n.at[(n - 1) * 2 + me_m], dp=where, mp=f
+            rows_of(owner), nb.at[me_s, side - n, me_m], s_n.at[number], r_n.at[(n - 1) * 2 + me_m], dp=where, mp=f
         )
 
     def block_landed(m, n):
-        where = nb.at[me_s, m, side - n]
+        where = nb.at[me_s, side - n, m]
         return remote(where, where, s_n.at[0], r_n.at[(n - 1) * 2 + m], mp=other)
 
     def chip_copy(n):
-        return remote(rows_of(owner_of(other, n)), nb.at[n, me_m, 0], s_n.at[6 + n], r_n.at[6 + n], mp=other)
-
-    def plane_copy(way, m):
-        number = 10 + way * 2 + m
-        block = nb.at[me_s, m, 1:side]
+        return remote(rows_of(owner_of(other, n)), nb.at[n, 0, me_m], s_n.at[6 + n], r_n.at[6 + n], mp=other)
+
+    def plane_copy(way, m, k):
+        number = 10 + (way * 2 + m) * (side - 1) + k - 1
+        block = nb.at[me_s, k, m]
         return remote(block, block, s_n.at[number], r_n.at[number], segment=(me_s + 1 + way * (n_seg - 2)) % n_seg)
 
-    def plane_forward(way):
-        block = nb.at[(me_s + n_seg - 1 + 2 * way) % n_seg, way, 1:side]
-        return remote(block, block, s_n.at[14 + way], r_n.at[14 + way], segment=(me_s + 1 + way * (n_seg - 2)) % n_seg)
-
-    for n in range(1, side):
+    def plane_forward(way, k):
+        number = 10 + (4 + way) * (side - 1) + k - 1
+        block = nb.at[(me_s + n_seg - 1 + 2 * way) % n_seg, k, way]
+        return remote(block, block, s_n.at[number], r_n.at[number], segment=(me_s + 1 + way * (n_seg - 2)) % n_seg)
+
+    for n in (1, side - 1, 2):
         for f in (0, 1):
             block_copy(f, n).start()
     for n in range(side):
@@ -225,7 +226,7 @@
     sx_sent = to_peer(4, sxx, sxgot)
     sx_sent.start()
     for n in range(side):
-        nb[n, me_m, 0] = rows_of(owner_of(me_m, n))[...]
+        nb[n, 0, me_m] = rows_of(owner_of(me_m, n))[...]
 
     away = pl.ds(pl.multiple_of(other * out_half, LANES), out_half)
     kept = pl.ds(pl.multiple_of(me_m * out_half, LANES), out_half)
@@ -261,6 +262,12 @@
     hpsend[...] = hpx[:, away].astype(bf16)
     hp_sent = to_peer(3, hpsend, hpgot)
     hp_sent.start()
+    for n in (1, side - 1):
+        for m in (0, 1):
+            block_landed(m, n).wait_recv()
+    for n in (1, side - 1):
+        for way in (0, 1):
+            plane_copy(way, way, n).start()
 
     dest_f = dest[...].astype(f32)
     onehot = jnp.where(iota((n_dp, tok), 0).astype(f32) == dest_f, 1.0, 0.0)
@@ -381,12 +388,17 @@
     def _():
         extra_swap.start()
 
-    for n in range(1, side):
-        for m in (0, 1):
-            block_landed(m, n).wait_recv()
-    for way in (0, 1):
-        for m in (way, 1 - way):
-            plane_copy(way, m).start()
+    for m in (0, 1):
+        block_landed(m, 2).wait_recv()
+    for way in (0, 1):
+        plane_copy(way, way, 2).start()
+    for n in (1, side - 1):
+        for way in (0, 1):
+            plane_copy(way, way, n).wait_recv()
+            plane_forward(way, n).start()
+    for n in (1, side - 1, 2):
+        for way in (0, 1):
+            plane_copy(way, 1 - way, n).start()
 
     pl.loop(1, 4)(student)
     for k in range(1, side):
@@ -407,6 +419,10 @@
         for copy in a_x:
             copy.wait_recv()
         a_swap.start()
+
+    for way in (0, 1):
+        plane_copy(way, way, 2).wait_recv()
+        plane_forward(way, 2).start()
 
     @pl.loop(1, n_dp)
     def _(n):
@@ -506,21 +522,15 @@
         diff_copy(way, 1 - way).start()
     loss_swap = to_peer(9, losspart, lossgot)
     loss_swap.start()
-    for way in (0, 1):
-        plane_copy(way, way).wait_recv()
-        plane_forward(way).start()
-
-    def product(owner, m, ahead):
-        return dot(nb[owner, m, ahead], gathered(ahead)[...])
+    def product(owner, ahead):
+        return dot(nb[owner, ahead].reshape(2 * share, slots), gathered(ahead)[...])
 
     for n in range(side):
         chip_copy(n).wait_recv()
 
     @pl.loop(0, side)
     def _(n):
-        @pl.loop(0, 2)
-        def _(m):
-            held[n, m] = product(n, m, 0)
+        held[n] = product(n, 0)
 
     for way in (0, 1):
         diff_copy(way, way).wait_recv()
@@ -531,16 +541,15 @@
     for copy in tells:
         copy.start()
     for way in (0, 1):
-        plane_copy(way, 1 - way).wait_recv()
-        plane_forward(way).wait_recv()
+        for n in range(1, side):
+            plane_copy(way, 1 - way, n).wait_recv()
+            plane_forward(way, n).wait_recv()
     for way in (0, 1):
         diff_copy(way, 1 - way).wait_recv()
 
     @pl.loop(0, side)
     def _(n):
-        @pl.loop(0, 2)
-        def _(m):
-            held[n, m] += product(n, m, 1) + product(n, m, 3)
+        held[n] += product(n, 1) + product(n, 3)
 
     for copy in tells:
         copy.wait_recv()
@@ -570,29 +579,31 @@
         diff_forward(way).wait_recv()
     far = (ring_at + 2) % side
     nears = [(ring_at + 1) % side, (ring_at + side - 1) % side]
-    for way in (0, 1):
-        sent(0, way)[...] = (held[far, way] + product(far, way, 2)).astype(bf16)
+
+    def half_rows(m):
+        return pl.ds(m * share, share)
+
+    block = held[far] + product(far, 2)
+    for way in (0, 1):
+        sent(0, way)[...] = block[way * share : (way + 1) * share].astype(bf16)
         sum_copy(way, 0).start()
     for way in (0, 1):
-        sent(1 + way, 1 - way)[...] = (held[nears[way], 1 - way] + product(nears[way], 1 - way, 2)).astype(bf16)
+        block = held[nears[way]] + product(nears[way], 2)
+        sent(1 + way, 1 - way)[...] = block[(1 - way) * share : (2 - way) * share].astype(bf16)
         sum_copy(way, 1).start()
-    for way in (0, 1):
-        held[nears[way], way] += product(nears[way], way, 2)
-
-    @pl.loop(0, 2)
-    def _(m):
-        held[ring_at, m] += product(ring_at, m, 2)
-
+        held[nears[way], half_rows(way)] = block[way * share : (way + 1) * share]
+    held[ring_at] += product(ring_at, 2)
     for way in (0, 1):
         sum_copy(way, 0).wait_recv()
-        sent(1 + way, way)[...] = (held[nears[way], way] + landed(way, 0)[...].astype(f32)).astype(bf16)
+        sent(1 + way, way)[...] = (held[nears[way], half_rows(way)] + landed(way, 0)[...].astype(f32)).astype(bf16)
         sum_copy(way, 2).start()
     for msg in (1, 2):
         for way in (0, 1):
             sum_copy(way, msg).wait_recv()
 
     def summed(m):
-        return held[ring_at, m] + landed(0, 2 - m)[...].astype(f32) + landed(1, 1 + m)[...].astype(f32)
+        mine = held[ring_at, pl.ds(pl.multiple_of(m * share, share), share)]
+        return mine + landed(0, 2 - m)[...].astype(f32) + landed(1, 1 + m)[...].astype(f32)
 
     finsend[...] = summed(other)
     last_swap = to_peer(10, finsend, fingot)
@@ -607,10 +618,12 @@
     for n in range(side):
         chip_copy(n).wait_send()
     for way in (0, 1):
+        for n in range(1, side):
+            for m in (0, 1):
+                plane_copy(way, m, n).wait_send()
+            plane_forward(way, n).wait_send()
         for m in (0, 1):
-            plane_copy(way, m).wait_send()
             diff_copy(way, m).wait_send()
-        plane_forward(way).wait_send()
         diff_forward(way).wait_send()
         for msg in range(3):
             sum_copy(way, msg).wait_send()
@@ -670,11 +683,11 @@
         ((n_dp, cap, out_half), bf16), ((n_dp, cap, out_half), bf16),
         (x.shape, bf16), ((slots, cols), f32), ((slots, out_half), bf16), ((slots, out_half), bf16),
         ((slots, LANES), f32), ((slots, LANES), f32), ((slots, known), bf16), ((slots, out_half), f32),
-        ((width, slots), bf16), ((n_seg, 2, side, share, slots), bf16), ((side, 2, share, out_half), f32),
+        ((width, slots), bf16), ((n_seg, side, 2, share, slots), bf16), ((side, 2 * share, out_half), f32),
         ((share, out_half), f32), ((share, out_half), f32),
         ((1, slots), f32), ((1, slots), f32), ((n_seg, 1, slots), f32),
     ]
-    sems = [5 + cols // LANES, 11, 11, 4 * (n_seg - 1), 4 * (n_seg - 1), 4 * (n_dp - 1), 4 * (n_dp - 1), 16, 16, 12, 12]
+    sems = [5 + cols // LANES, 11, 11, 4 * (n_seg - 1), 4 * (n_seg - 1), 4 * (n_dp - 1), 4 * (n_dp - 1), 28, 28, 12, 12]
     return pl.pallas_call(
         functools.partial(step_kernel, n_seg, side, cap),
         out_shape=(
@@ -692,6 +705,25 @@
         h, down, up, x, w, p, xmap,
         ids.reshape(1, tok), dest.reshape(1, tok), counts, gain, sgain.reshape(width // LANES, LANES), kcol,
     )
+
+
+def finish_kernel(grad, loss, grad_out, loss_out, sems):
+    copies = [pltpu.make_async_copy(grad, grad_out, sems.at[0]), pltpu.make_async_copy(loss, loss_out, sems.at[1])]
+    for copy in copies:
+        copy.start()
+    for copy in copies:
+        copy.wait()
+
+
+def finish(grad, loss):
+    hbm = pl.BlockSpec(memory_space=pl.ANY)
+    return pl.pallas_call(
+        finish_kernel,
+        out_shape=(jax.ShapeDtypeStruct(grad.shape, f32), jax.ShapeDtypeStruct(loss.shape, f32)),
+        in_specs=[hbm, hbm],
+        out_specs=(hbm, hbm),
+        scratch_shapes=[pltpu.SemaphoreType.DMA((2,))],
+    )(grad, loss)
 
 
 def local(
@@ -720,6 +752,7 @@
         student_weight,
         projector,
     )
+    weight_grad, row_loss = finish(weight_grad, row_loss)
     share, cols = weight_grad.shape
     return (weight_grad.reshape(1, share, cols), row_loss.reshape(student_in.shape[0]))
 

time: 85.1 us -> 103 us (1.21)
  Pallas kernels: 80.9 us -> 102 us
  local copies, waits for them, and re-layouts: 3.33 us -> 0 us
    pallas_call x0 -> x1, Pallas kernels: none -> 26 us  [finish(): pl.pallas_call(finish_kernel, out_shape=(jax.ShapeDtypeStruct(grad.shape,...]
    pallas_call x1, Pallas kernels: 80.9 us -> 75.9 us  [run_step(): pl.pallas_call(functools.partial(step_kernel, n_seg, side, cap), out_shap...]
    unnamed x2 -> x0, local copies, waits for them, and re-layouts: 3.33 us -> none
where the time goes in v8:
time: 103 us
  Pallas kernels  102 us (99%)
    pallas_call x1, Pallas kernels, run_step(): pl.pallas_call(functools.partial(step_kernel, n_seg, side, cap), out_shap...  75.9 us
    pallas_call x1, Pallas kernels, finish(): pl.pallas_call(finish_kernel, out_shape=(jax.ShapeDtypeStruct(grad.shape,...  26 us

profile of v8, /device:TPU:1, one launch (start us, length us, event | category | flops | bytes accessed | tf_op | source)
XLA Modules:
  0.0 102.7 jit_solution(15286451233739843344)
XLA Ops:
  0.6 75.9 %shard_map.140 = (f32[160,1280]{1,0:T(8,128)}, f32[1,512]{1,0:T(1,128)}) custom-call(bf16[256,4096]{1,0:T(8,128)(2,1)} %h_hbm.1, bf16[192,4096]{1,0:T(8,128)(2,1)} %bitcast.9, bf16[192,4096]{1,0:T(8,128)(2,1)} %bitcast.10, bf16[512,2560]{1,0:T(8,128)(2,1)} %x_hbm.1, bf16[2560,1280]{1,0:T(8,128)(2,1)} %w_hbm.1, bf16[4096,1280]{1,0:T(8,128)(2,1)} %p_hbm.1, ...), custom_call_target="tpu_custom_call" | custom-call | flops 9395240960 | bytes 26214400 | tf_op jit(solution)/shard_map/pallas_call | solution.py:691
  76.5 26.0 %shard_map.141 = (f32[160,1280]{1,0:T(8,128)}, f32[1,512]{1,0:T(1,128)}) custom-call(f32[160,1280]{1,0:T(8,128)} %get-tuple-element.6.grad, f32[1,512]{1,0:T(1,128)} %get-tuple-element.7.loss), custom_call_target="tpu_custom_call" | custom-call | tf_op jit(solution)/shard_map/pallas_call | solution.py:720

commit v9 on v8

--- a/solution.py
+++ b/solution.py
@@ -707,22 +707,18 @@
     )
 
 
-def finish_kernel(grad, loss, grad_out, loss_out, sems):
-    copies = [pltpu.make_async_copy(grad, grad_out, sems.at[0]), pltpu.make_async_copy(loss, loss_out, sems.at[1])]
-    for copy in copies:
-        copy.start()
-    for copy in copies:
-        copy.wait()
+def finish_kernel(grad, loss, grad_out, loss_out):
+    grad_out[...] = grad[...]
+    loss_out[...] = loss[...]
 
 
 def finish(grad, loss):
-    hbm = pl.BlockSpec(memory_space=pl.ANY)
+    vmem = pl.BlockSpec(memory_space=pltpu.VMEM)
     return pl.pallas_call(
         finish_kernel,
         out_shape=(jax.ShapeDtypeStruct(grad.shape, f32), jax.ShapeDtypeStruct(loss.shape, f32)),
-        in_specs=[hbm, hbm],
-        out_specs=(hbm, hbm),
-        scratch_shapes=[pltpu.SemaphoreType.DMA((2,))],
+        in_specs=[vmem, vmem],
+        out_specs=(vmem, vmem),
     )(grad, loss)
 
 

time: 103 us -> 78.8 us (0.77)
  Pallas kernels: 102 us -> 77.9 us
    pallas_call x1, Pallas kernels: 26 us -> 2.09 us  [finish(): pl.pallas_call(finish_kernel, out_shape=(jax.ShapeDtypeStruct(grad.shape,...]
where the time goes in v9:
time: 78.8 us; the launch traced here: 78.6 us
  Pallas kernels  77.9 us (99%)
    pallas_call x1, Pallas kernels, run_step(): pl.pallas_call(functools.partial(step_kernel, n_seg, side, cap), out_shap...  75.9 us
    pallas_call x1, Pallas kernels, finish(): pl.pallas_call(finish_kernel, out_shape=(jax.ShapeDtypeStruct(grad.shape,...  2.09 us

profile of v9, /device:TPU:1, one launch (start us, length us, event | category | flops | bytes accessed | tf_op | source)
XLA Modules:
  0.0 78.6 jit_solution(8836061222937762376)
XLA Ops:
  0.6 75.9 %shard_map.140 = (f32[160,1280]{1,0:T(8,128)}, f32[1,512]{1,0:T(1,128)}) custom-call(bf16[256,4096]{1,0:T(8,128)(2,1)} %h_hbm.1, bf16[192,4096]{1,0:T(8,128)(2,1)} %bitcast.9, bf16[192,4096]{1,0:T(8,128)(2,1)} %bitcast.10, bf16[512,2560]{1,0:T(8,128)(2,1)} %x_hbm.1, bf16[2560,1280]{1,0:T(8,128)(2,1)} %w_hbm.1, bf16[4096,1280]{1,0:T(8,128)(2,1)} %p_hbm.1, ...), custom_call_target="tpu_custom_call" | custom-call | flops 9395240960 | bytes 26214400 | tf_op jit(solution)/shard_map/pallas_call | solution.py:691
  76.5 2.1 %shard_map.141 = (f32[160,1280]{1,0:T(8,128)}, f32[1,512]{1,0:T(1,128)}) custom-call(f32[160,1280]{1,0:T(8,128)} %get-tuple-element.6.grad, f32[1,512]{1,0:T(1,128)} %get-tuple-element.7.loss), custom_call_target="tpu_custom_call" | custom-call | tf_op jit(solution)/shard_map/pallas_call | solution.py:717

commit v10 on v9

--- a/solution.py
+++ b/solution.py
@@ -350,18 +350,6 @@
 
     pl.loop(0, 1)(student)
 
-    for copy in mg_x:
-        copy.wait_recv()
-    for n in range(pair):
-        tables[me_m, me_d, :, n * LANES : (n + 1) * LANES] = mgs[me_m * pair + n]
-
-    def m_copy(n):
-        return to_dp(2, n, tables.at[me_m, me_d], tables.at[me_m, me_d])
-
-    @pl.loop(1, n_dp)
-    def _(n):
-        m_copy(n).start()
-
     up_sent.wait_recv()
     blocks[me_d] = (upx[:, kept] + upgot[...]).astype(bf16)
     firsts = [gather_first(n) for n in range(1, side)]
@@ -371,6 +359,18 @@
     for copy in seconds:
         copy.start()
 
+    for copy in mg_x:
+        copy.wait_recv()
+    for n in range(pair):
+        tables[me_m, me_d, :, n * LANES : (n + 1) * LANES] = mgs[me_m * pair + n]
+
+    def m_copy(n):
+        return to_dp(2, n, tables.at[me_m, me_d], tables.at[me_m, me_d])
+
+    @pl.loop(1, n_dp)
+    def _(n):
+        m_copy(n).start()
+
     @pl.loop(1, n_dp)
     def _(n):
         a_copy(n).wait_recv()
@@ -392,22 +392,22 @@
         block_landed(m, 2).wait_recv()
     for way in (0, 1):
         plane_copy(way, way, 2).start()
-    for n in (1, side - 1):
-        for way in (0, 1):
-            plane_copy(way, way, n).wait_recv()
-            plane_forward(way, n).start()
     for n in (1, side - 1, 2):
         for way in (0, 1):
             plane_copy(way, 1 - way, n).start()
 
-    pl.loop(1, 4)(student)
-    for k in range(1, side):
+    pl.loop(1, 3)(student)
+
+    def gather_on(k):
         firsts[k - 1].wait_recv()
-        for n in range(1, side):
-            copy = gather_second(k, n)
+        copies = [gather_second(k, n) for n in range(1, side)]
+        for copy in copies:
             copy.start()
-            seconds.append(copy)
-
+        return copies
+
+    seconds += gather_on(1) + gather_on(side - 1)
+    pl.loop(3, 4)(student)
+    seconds += gather_on(2)
     pl.loop(4, tiles)(student)
     sosend[...] = sox[:, away].astype(bf16)
     so_sent = to_peer(5, sosend, sogot)
@@ -420,9 +420,10 @@
             copy.wait_recv()
         a_swap.start()
 
-    for way in (0, 1):
-        plane_copy(way, way, 2).wait_recv()
-        plane_forward(way, 2).start()
+    for n in (1, side - 1, 2):
+        for way in (0, 1):
+            plane_copy(way, way, n).wait_recv()
+            plane_forward(way, n).start()
 
     @pl.loop(1, n_dp)
     def _(n):

time: 78.8 us -> 78 us (0.990)
  Pallas kernels: 77.9 us -> 77 us
    pallas_call x1, Pallas kernels: 75.9 us -> 74.9 us  [run_step(): pl.pallas_call(functools.partial(step_kernel, n_seg, side, cap), out_shap...]
where the time goes in v10:
time: 78 us; the launch traced here: 77.6 us
  Pallas kernels  77 us (99%)
    pallas_call x1, Pallas kernels, run_step(): pl.pallas_call(functools.partial(step_kernel, n_seg, side, cap), out_shap...  74.9 us
    pallas_call x1, Pallas kernels, finish(): pl.pallas_call(finish_kernel, out_shape=(jax.ShapeDtypeStruct(grad.shape,...  2.09 us

profile of v10, /device:TPU:1, one launch (start us, length us, event | category | flops | bytes accessed | tf_op | source)
XLA Modules:
  0.0 77.6 jit_solution(5108069026490802507)
XLA Ops:
  0.6 74.9 %shard_map.140 = (f32[160,1280]{1,0:T(8,128)}, f32[1,512]{1,0:T(1,128)}) custom-call(bf16[256,4096]{1,0:T(8,128)(2,1)} %h_hbm.1, bf16[192,4096]{1,0:T(8,128)(2,1)} %bitcast.9, bf16[192,4096]{1,0:T(8,128)(2,1)} %bitcast.10, bf16[512,2560]{1,0:T(8,128)(2,1)} %x_hbm.1, bf16[2560,1280]{1,0:T(8,128)(2,1)} %w_hbm.1, bf16[4096,1280]{1,0:T(8,128)(2,1)} %p_hbm.1, ...), custom_call_target="tpu_custom_call" | custom-call | flops 9395240960 | bytes 26214400 | tf_op jit(solution)/shard_map/pallas_call | solution.py:692
  75.5 2.1 %shard_map.141 = (f32[160,1280]{1,0:T(8,128)}, f32[1,512]{1,0:T(1,128)}) custom-call(f32[160,1280]{1,0:T(8,128)} %get-tuple-element.6.grad, f32[1,512]{1,0:T(1,128)} %get-tuple-element.7.loss), custom_call_target="tpu_custom_call" | custom-call | tf_op jit(solution)/shard_map/pallas_call | solution.py:718

commit v11 on v10

--- a/solution.py
+++ b/solution.py
@@ -167,8 +167,7 @@
     x_in.wait()
     sxx[...] = jnp.zeros(sxx.shape, f32)
 
-    @pl.loop(0, x.shape[1] // LANES)
-    def _(n):
+    def scale(n):
         span = pl.ds(pl.multiple_of(n * LANES, LANES), LANES)
         wide = x[:, span].astype(f32)
         sxx[...] += wide * wide
@@ -176,10 +175,13 @@
         sg[:, span] = scaled
         sgt[span, :] = scaled.T
 
+    groups = x.shape[1] // LANES
+    pl.loop(0, groups // 2)(scale)
     pl.semaphore_wait(barrier, 1 + (n_seg - 1) + (n_dp - 1) + (side - 1))
     u_sent = [to_seg(0, n, usend, ugot.at[me_s]) for n in range(1, n_seg)]
     for copy in u_sent:
         copy.start()
+    pl.loop(groups // 2, groups)(scale)
 
     share = out.shape[0]
 
@@ -565,16 +567,25 @@
     def sent(slot, m):
         return p.at[pl.ds(below + (slot * 2 + m) * share, share), :out_half]
 
-    def landed(way, msg):
-        return p.at[pl.ds(pl.multiple_of(below + (way * 3 + msg) * share, 16), share), out_half:]
-
-    def sum_copy(way, msg):
-        slot = 0 if msg == 0 else 1 + way
-        m = 1 - way if msg == 1 else way
-        number = 6 + way * 3 + msg
+    def landed(number):
+        return p.at[pl.ds(pl.multiple_of(below + number * share, 16), share), out_half:]
+
+    def far_copy(way):
         return remote(
-            sent(slot, m), landed(way, msg), s_r.at[number], r_r.at[number], dp=place(0, 1 + way * (side - 2))
+            sent(0, way), landed(way), s_r.at[6 + way], r_r.at[6 + way], dp=place(0, 1 + way * (side - 2))
         )
+
+    def near_copy(way, last):
+        m = way if last else 1 - way
+        number = 2 * me_m + last
+        return remote(
+            sent(1 + way, m), landed(2 + number), s_r.at[8 + 2 * way + last], r_r.at[8 + number],
+            dp=place(0, 1 + way * (side - 2)), mp=m,
+        )
+
+    def near_landed(f, last):
+        where = landed(2 + 2 * f + last)
+        return remote(where, where, s_r.at[0], r_r.at[8 + 2 * f + last], mp=other)
 
     for way in (0, 1):
         diff_forward(way).wait_recv()
@@ -587,31 +598,27 @@
     block = held[far] + product(far, 2)
     for way in (0, 1):
         sent(0, way)[...] = block[way * share : (way + 1) * share].astype(bf16)
-        sum_copy(way, 0).start()
+        far_copy(way).start()
     for way in (0, 1):
         block = held[nears[way]] + product(nears[way], 2)
         sent(1 + way, 1 - way)[...] = block[(1 - way) * share : (2 - way) * share].astype(bf16)
-        sum_copy(way, 1).start()
+        near_copy(way, 0).start()
         held[nears[way], half_rows(way)] = block[way * share : (way + 1) * share]
     held[ring_at] += product(ring_at, 2)
-    for way in (0, 1):
-        sum_copy(way, 0).wait_recv()
-        sent(1 + way, way)[...] = (held[nears[way], half_rows(way)] + landed(way, 0)[...].astype(f32)).astype(bf16)
-        sum_copy(way, 2).start()
-    for msg in (1, 2):
-        for way in (0, 1):
-            sum_copy(way, msg).wait_recv()
-
-    def summed(m):
-        mine = held[ring_at, pl.ds(pl.multiple_of(m * share, share), share)]
-        return mine + landed(0, 2 - m)[...].astype(f32) + landed(1, 1 + m)[...].astype(f32)
-
-    finsend[...] = summed(other)
-    last_swap = to_peer(10, finsend, fingot)
-    last_swap.start()
-    out[:, kept] = summed(me_m)
-    last_swap.wait_recv()
-    out[:, away] = fingot[...]
+    finsend[...] = held[ring_at, pl.ds(pl.multiple_of(other * share, share), share)]
+    own_swap = to_peer(10, finsend, fingot)
+    own_swap.start()
+    for way in (0, 1):
+        far_copy(way).wait_recv()
+        sent(1 + way, way)[...] = (held[nears[way], half_rows(way)] + landed(way)[...].astype(f32)).astype(bf16)
+        near_copy(way, 1).start()
+    own_swap.wait_recv()
+    mine = held[ring_at, pl.ds(pl.multiple_of(me_m * share, share), share)]
+    for last in (0, 1):
+        near_landed(me_m, last).wait_recv()
+        near_landed(other, last).wait_recv()
+    out[:, kept] = mine + landed(2 + 2 * me_m)[...].astype(f32) + landed(3 + 2 * me_m)[...].astype(f32)
+    out[:, away] = fingot[...] + landed(2 + 2 * other)[...].astype(f32) + landed(3 + 2 * other)[...].astype(f32)
 
     for n in range(1, side):
         for f in (0, 1):
@@ -626,9 +633,10 @@
         for m in (0, 1):
             diff_copy(way, m).wait_send()
         diff_forward(way).wait_send()
-        for msg in range(3):
-            sum_copy(way, msg).wait_send()
-    for copy in u_sent + mg_x + firsts + seconds + [ab_sent, mg_sent, up_sent, hp_sent, so_sent, table_swap, loss_swap, last_swap] + tells:
+        far_copy(way).wait_send()
+        for last in (0, 1):
+            near_copy(way, last).wait_send()
+    for copy in u_sent + mg_x + firsts + seconds + [ab_sent, mg_sent, up_sent, hp_sent, so_sent, table_swap, loss_swap, own_swap] + tells:
         copy.wait_send()
 
     @pl.when(me_m == 0)

time: 78 us -> 76.3 us (0.978)
  Pallas kernels: 77 us -> 75.5 us
    pallas_call x1, Pallas kernels: 74.9 us -> 73.4 us  [run_step(): pl.pallas_call(functools.partial(step_kernel, n_seg, side, cap), out_shap...]
where the time goes in v11:
time: 76.3 us; the launch traced here: 76.1 us
  Pallas kernels  75.5 us (99%)
    pallas_call x1, Pallas kernels, run_step(): pl.pallas_call(functools.partial(step_kernel, n_seg, side, cap), out_shap...  73.4 us
    pallas_call x1, Pallas kernels, finish(): pl.pallas_call(finish_kernel, out_shape=(jax.ShapeDtypeStruct(grad.shape,...  2.09 us

profile of v11, /device:TPU:1, one launch (start us, length us, event | category | flops | bytes accessed | tf_op | source)
XLA Modules:
  0.0 76.1 jit_solution(17116820660383795645)
XLA Ops:
  0.6 73.4 %shard_map.140 = (f32[160,1280]{1,0:T(8,128)}, f32[1,512]{1,0:T(1,128)}) custom-call(bf16[256,4096]{1,0:T(8,128)(2,1)} %h_hbm.1, bf16[192,4096]{1,0:T(8,128)(2,1)} %bitcast.9, bf16[192,4096]{1,0:T(8,128)(2,1)} %bitcast.10, bf16[512,2560]{1,0:T(8,128)(2,1)} %x_hbm.1, bf16[2560,1280]{1,0:T(8,128)(2,1)} %w_hbm.1, bf16[4096,1280]{1,0:T(8,128)(2,1)} %p_hbm.1, ...), custom_call_target="tpu_custom_call" | custom-call | flops 9395240960 | bytes 26214400 | tf_op jit(solution)/shard_map/pallas_call | solution.py:700
  74.0 2.1 %shard_map.141 = (f32[160,1280]{1,0:T(8,128)}, f32[1,512]{1,0:T(1,128)}) custom-call(f32[160,1280]{1,0:T(8,128)} %get-tuple-element.6.grad, f32[1,512]{1,0:T(1,128)} %get-tuple-element.7.loss), custom_call_target="tpu_custom_call" | custom-call | tf_op jit(solution)/shard_map/pallas_call | solution.py:726

commit v12 on v11

--- a/solution.py
+++ b/solution.py
@@ -100,9 +100,9 @@
     up_in = load(0, up_hbm, up)
     x_in = load(3, x_hbm, x)
     h_in = load(1, h_hbm, h)
+    down_in = load(2, down_hbm, down)
     for n in range(tiles):
         p_copy(n).start()
-    down_in = load(2, down_hbm, down)
     for n in range(tiles):
         w_copy(n).start()
     xmap_in = load(4, xmap_hbm, xmap)
@@ -227,8 +227,6 @@
         chip_copy(n).start()
     sx_sent = to_peer(4, sxx, sxgot)
     sx_sent.start()
-    for n in range(side):
-        nb[n, 0, me_m] = rows_of(owner_of(me_m, n))[...]
 
     away = pl.ds(pl.multiple_of(other * out_half, LANES), out_half)
     kept = pl.ds(pl.multiple_of(me_m * out_half, LANES), out_half)
@@ -264,12 +262,6 @@
     hpsend[...] = hpx[:, away].astype(bf16)
     hp_sent = to_peer(3, hpsend, hpgot)
     hp_sent.start()
-    for n in (1, side - 1):
-        for m in (0, 1):
-            block_landed(m, n).wait_recv()
-    for n in (1, side - 1):
-        for way in (0, 1):
-            plane_copy(way, way, n).start()
 
     dest_f = dest[...].astype(f32)
     onehot = jnp.where(iota((n_dp, tok), 0).astype(f32) == dest_f, 1.0, 0.0)
@@ -306,6 +298,13 @@
     @pl.loop(1, n_dp)
     def _(n):
         h_copy(n).start()
+
+    for n in (1, side - 1):
+        for m in (0, 1):
+            block_landed(m, n).wait_recv()
+    for n in (1, side - 1):
+        for way in (0, 1):
+            plane_copy(way, way, n).start()
 
     for copy in u_sent:
         copy.wait_recv()
@@ -426,6 +425,9 @@
         for way in (0, 1):
             plane_copy(way, way, n).wait_recv()
             plane_forward(way, n).start()
+
+    for n in range(side):
+        nb[n, 0, me_m] = rows_of(owner_of(me_m, n))[...]
 
     @pl.loop(1, n_dp)
     def _(n):

time: 76.3 us -> 78.4 us (1.028)
  Pallas kernels: 75.5 us -> 77.6 us
    pallas_call x1, Pallas kernels: 73.4 us -> 75.5 us  [run_step(): pl.pallas_call(functools.partial(step_kernel, n_seg, side, cap), out_shap...]
where the time goes in v12:
time: 78.4 us; the launch traced here: 78.2 us
  Pallas kernels  77.6 us (99%)
    pallas_call x1, Pallas kernels, run_step(): pl.pallas_call(functools.partial(step_kernel, n_seg, side, cap), out_shap...  75.5 us
    pallas_call x1, Pallas kernels, finish(): pl.pallas_call(finish_kernel, out_shape=(jax.ShapeDtypeStruct(grad.shape,...  2.09 us

profile of v12, /device:TPU:1, one launch (start us, length us, event | category | flops | bytes accessed | tf_op | source)
XLA Modules:
  0.0 78.2 jit_solution(4809632797089058075)
XLA Ops:
  0.6 75.5 %shard_map.140 = (f32[160,1280]{1,0:T(8,128)}, f32[1,512]{1,0:T(1,128)}) custom-call(bf16[256,4096]{1,0:T(8,128)(2,1)} %h_hbm.1, bf16[192,4096]{1,0:T(8,128)(2,1)} %bitcast.9, bf16[192,4096]{1,0:T(8,128)(2,1)} %bitcast.10, bf16[512,2560]{1,0:T(8,128)(2,1)} %x_hbm.1, bf16[2560,1280]{1,0:T(8,128)(2,1)} %w_hbm.1, bf16[4096,1280]{1,0:T(8,128)(2,1)} %p_hbm.1, ...), custom_call_target="tpu_custom_call" | custom-call | flops 9395240960 | bytes 26214400 | tf_op jit(solution)/shard_map/pallas_call | solution.py:702
  76.1 2.1 %shard_map.141 = (f32[160,1280]{1,0:T(8,128)}, f32[1,512]{1,0:T(1,128)}) custom-call(f32[160,1280]{1,0:T(8,128)} %get-tuple-element.6.grad, f32[1,512]{1,0:T(1,128)} %get-tuple-element.7.loss), custom_call_target="tpu_custom_call" | custom-call | tf_op jit(solution)/shard_map/pallas_call | solution.py:728

commit v13 on v11

--- a/solution.py
+++ b/solution.py
@@ -100,9 +100,9 @@
     up_in = load(0, up_hbm, up)
     x_in = load(3, x_hbm, x)
     h_in = load(1, h_hbm, h)
+    down_in = load(2, down_hbm, down)
     for n in range(tiles):
         p_copy(n).start()
-    down_in = load(2, down_hbm, down)
     for n in range(tiles):
         w_copy(n).start()
     xmap_in = load(4, xmap_hbm, xmap)
@@ -227,8 +227,6 @@
         chip_copy(n).start()
     sx_sent = to_peer(4, sxx, sxgot)
     sx_sent.start()
-    for n in range(side):
-        nb[n, 0, me_m] = rows_of(owner_of(me_m, n))[...]
 
     away = pl.ds(pl.multiple_of(other * out_half, LANES), out_half)
     kept = pl.ds(pl.multiple_of(me_m * out_half, LANES), out_half)
@@ -426,6 +424,9 @@
         for way in (0, 1):
             plane_copy(way, way, n).wait_recv()
             plane_forward(way, n).start()
+
+    for n in range(side):
+        nb[n, 0, me_m] = rows_of(owner_of(me_m, n))[...]
 
     @pl.loop(1, n_dp)
     def _(n):

time: 76.3 us -> 76.3 us (level)
  no operation moved by 1% of the time
where the time goes in v13:
time: 76.3 us; the launch traced here: 76.1 us
  Pallas kernels  75.5 us (99%)
    pallas_call x1, Pallas kernels, run_step(): pl.pallas_call(functools.partial(step_kernel, n_seg, side, cap), out_shap...  73.4 us
    pallas_call x1, Pallas kernels, finish(): pl.pallas_call(finish_kernel, out_shape=(jax.ShapeDtypeStruct(grad.shape,...  2.09 us

profile of v13, /device:TPU:1, one launch (start us, length us, event | category | flops | bytes accessed | tf_op | source)
XLA Modules:
  0.0 76.1 jit_solution(18354404658976256157)
XLA Ops:
  0.6 73.4 %shard_map.140 = (f32[160,1280]{1,0:T(8,128)}, f32[1,512]{1,0:T(1,128)}) custom-call(bf16[256,4096]{1,0:T(8,128)(2,1)} %h_hbm.1, bf16[192,4096]{1,0:T(8,128)(2,1)} %bitcast.9, bf16[192,4096]{1,0:T(8,128)(2,1)} %bitcast.10, bf16[512,2560]{1,0:T(8,128)(2,1)} %x_hbm.1, bf16[2560,1280]{1,0:T(8,128)(2,1)} %w_hbm.1, bf16[4096,1280]{1,0:T(8,128)(2,1)} %p_hbm.1, ...), custom_call_target="tpu_custom_call" | custom-call | flops 9395240960 | bytes 26214400 | tf_op jit(solution)/shard_map/pallas_call | solution.py:701
  74.0 2.1 %shard_map.141 = (f32[160,1280]{1,0:T(8,128)}, f32[1,512]{1,0:T(1,128)}) custom-call(f32[160,1280]{1,0:T(8,128)} %get-tuple-element.6.grad, f32[1,512]{1,0:T(1,128)} %get-tuple-element.7.loss), custom_call_target="tpu_custom_call" | custom-call | tf_op jit(solution)/shard_map/pallas_call | solution.py:727
